TPU v7x, 32 devices: a whole 2x2x4 slice. The times are simulated.
32 devices in a mesh: fsdp: 16 (over z, x, core), seq: 2 (over y).
Axes of the slice: x: 2, y: 2, z: 4, core: 2. Of those that a mesh axis runs over, the one named last changes fastest.
Arguments:
- tokens: bfloat16 [32, 1024, 1152], P('fsdp', 'seq'), may hold values from -6 to 6
- condition: float32 [32, 1152], P('fsdp'), may hold values from -6 to 6
- adapter: int32 [32], P('fsdp'), may hold values from 0 to 7, as said below
- cotangent: bfloat16 [32, 1024, 1152], P('fsdp', 'seq'), may hold values from -6 to 6
- modulation_weight: bfloat16 [1152, 6912], P('fsdp', 'seq'), may hold values from -0.1875 to 0.1875
- modulation_bias: float32 [6912], replicated, may hold values from -3 to 3
- query_key_value_weight: bfloat16 [1152, 3456], P('fsdp', 'seq'), may hold values from -0.1875 to 0.1875
- attention_out_weight: bfloat16 [1152, 1152], P('fsdp', 'seq'), may hold values from -0.75 to 0.75
- attention_out_bias: float32 [1152], replicated, may hold values from -1.75 to 1.75
- widen_weight: bfloat16 [1152, 4608], P('fsdp', 'seq'), may hold values from -0.1875 to 0.1875
- widen_bias: float32 [4608], replicated, may hold values from -3 to 3
- narrow_weight: bfloat16 [4608, 1152], P('fsdp', 'seq'), may hold values from -0.09375 to 0.09375
- narrow_bias: float32 [1152], replicated, may hold values from -1.75 to 1.75
- lowrank_down: float32 [8, 16, 9216], P('seq', None, 'fsdp'), may hold values from -0.1875 to 0.1875
- lowrank_up: float32 [8, 16, 17280], P('seq', None, 'fsdp'), may hold values from -0.5 to 0.5
- first_moment_down: float32 [8, 16, 9216], P('seq', None, 'fsdp'), may hold values from -0.00036621094 to 0.00036621094
- first_moment_up: float32 [8, 16, 17280], P('seq', None, 'fsdp'), may hold values from -0.00036621094 to 0.00036621094
- second_moment_down: float32 [8, 16, 9216], P('seq', None, 'fsdp'), may hold values from 1.4742791e-09 to 1.4742791e-08
- second_moment_up: float32 [8, 16, 17280], P('seq', None, 'fsdp'), may hold values from 8.845675e-11 to 8.845675e-10
Outputs:
- block_out: bfloat16 [32, 1024, 1152], P('fsdp', 'seq')
- token_grad: float32 [32, 1024, 1152], P('fsdp', 'seq')
- cond_grad: float32 [32, 1152], P('fsdp')
- grad_norm: float32 [], replicated
- stepped_down: float32 [8, 16, 9216], P('seq', None, 'fsdp')
- stepped_up: float32 [8, 16, 17280], P('seq', None, 'fsdp')
- next_first_down: float32 [8, 16, 9216], P('seq', None, 'fsdp')
- next_first_up: float32 [8, 16, 17280], P('seq', None, 'fsdp')
- next_second_down: float32 [8, 16, 9216], P('seq', None, 'fsdp')
- next_second_up: float32 [8, 16, 17280], P('seq', None, 'fsdp')
Inputs may be any that keep to these rules, and one draw needn't show every extreme that they name: Sequence s uses adapter[s]; the values never fall from one sequence to the next, and each of the 8 adapters is used by at least one sequence.
All inputs are finite; a program needn't handle non-finite values.
Results may differ from a plain program's by a relative error of at most 0.025.
The roundings to bfloat16 on the way count: a program that leaves them out, or rounds other values in their place, can miss the bound.
Values may be sent and summed in bfloat16 or wider, within the bound.
No kernel may reach another device: no remote copies, remote signals or barrier semaphores. Data moves between devices by JAX's collectives and lax.ppermute only.
A program may use at most 256 MiB of HBM per device.

v0:
```python
import jax
import jax.numpy as jnp
from jax import lax
from jax.sharding import PartitionSpec as P

MODEL_WIDTH = 1152
HD = 72
FF = 4608
ADAPTER_RANK = 16
ADAPTER_COUNT = 8
MB = 2
SEQ_MB = 1
STEP = 10


beta_first = 0.9
beta_second = 0.999
learn_rate = 0.05
decay_rate = 0.1
adam_eps = 1e-08
clip_limit = 1.0
norm_eps = 1e-06
pair_heads = 2
highest = lax.Precision.HIGHEST


def linear(inputs, weight):
    return jnp.einsum("sti,io->sto", inputs, weight, preferred_element_type=jnp.float32)


def linear_back(gradient, weight):
    return jnp.einsum("sto,io->sti", gradient, weight, preferred_element_type=jnp.float32)


def normalize(stream):
    center = stream - jnp.mean(stream, -1, keepdims=True)
    inverse = lax.rsqrt(jnp.mean(center * center, -1, keepdims=True) + norm_eps)
    return (center * inverse, inverse)


def normalize_back(gradient, normed, inverse):
    return inverse * (
        gradient
        - jnp.mean(gradient, -1, keepdims=True)
        - normed * jnp.mean(gradient * normed, -1, keepdims=True)
    )


def adapt_forward(inputs, down_part, up_part):
    middle = jnp.einsum(
        "sti,sri->str", inputs, down_part, preferred_element_type=jnp.float32
    ).astype(jnp.bfloat16)
    return (middle, jnp.einsum("str,sro->sto", middle, up_part, preferred_element_type=jnp.float32))


def adapt_backward(inputs, middle, gradient, down_part, up_part):
    up_grad = jnp.einsum("str,sto->sro", middle, gradient, preferred_element_type=jnp.float32)
    middle_grad = jnp.einsum(
        "sto,sro->str", gradient, up_part, preferred_element_type=jnp.float32
    ).astype(jnp.bfloat16)
    down_grad = jnp.einsum("str,sti->sri", middle_grad, inputs, preferred_element_type=jnp.float32)
    input_grad = jnp.einsum(
        "str,sri->sti", middle_grad, down_part, preferred_element_type=jnp.float32
    )
    return (input_grad, down_grad, up_grad)


def grouped(matrix):
    seq_count, row_count, col_count = matrix.shape
    return jnp.moveaxis(
        matrix.reshape(seq_count, row_count, col_count // (pair_heads * HD), pair_heads, HD), 2, 0
    )


def ungrouped(stacked):
    moved = jnp.moveaxis(stacked, 0, 2)
    return moved.reshape(moved.shape[0], moved.shape[1], -1)


def attend_group(group_inputs):
    queries, all_keys, all_values = group_inputs
    factor = queries.shape[-1] ** (-0.5)
    scores = (
        jnp.einsum("sqhd,skhd->shqk", queries, all_keys, preferred_element_type=jnp.float32)
        * factor
    )
    row_max = jnp.max(scores, -1, keepdims=True)
    exponent = jnp.exp(scores - row_max)
    row_total = jnp.sum(exponent, -1, keepdims=True)
    weights = (exponent / row_total).astype(jnp.bfloat16)
    mixed_heads = jnp.einsum(
        "shqk,skhd->sqhd", weights, all_values, preferred_element_type=jnp.float32
    )
    return (mixed_heads, row_max + jnp.log(row_total))


def attend_back(group_inputs):
    queries, all_keys, all_values, d_mixed, log_total = group_inputs
    factor = queries.shape[-1] ** (-0.5)
    scores = (
        jnp.einsum("sqhd,skhd->shqk", queries, all_keys, preferred_element_type=jnp.float32)
        * factor
    )
    probable = jnp.exp(scores - log_total)
    d_values = jnp.einsum(
        "shqk,sqhd->skhd",
        probable.astype(jnp.bfloat16),
        d_mixed,
        preferred_element_type=jnp.float32,
    )
    d_weights = jnp.einsum(
        "sqhd,skhd->shqk", d_mixed, all_values, preferred_element_type=jnp.float32
    )
    inner_sum = jnp.sum(d_weights * probable, -1, keepdims=True)
    d_scores = (probable * (d_weights - inner_sum) * factor).astype(jnp.bfloat16)
    d_queries = jnp.einsum(
        "shqk,skhd->sqhd", d_scores, all_keys, preferred_element_type=jnp.float32
    )
    d_keys = jnp.einsum("shqk,sqhd->skhd", d_scores, queries, preferred_element_type=jnp.float32)
    return (d_queries, d_keys, d_values)


def gelu_tanh(inner_act):
    return jax.nn.gelu(inner_act, approximate=True)


def shards(
    tokens,
    condition,
    adapter,
    cotangent,
    modulation_weight,
    modulation_bias,
    query_key_value_weight,
    attention_out_weight,
    attention_out_bias,
    widen_weight,
    widen_bias,
    narrow_weight,
    narrow_bias,
    lowrank_down,
    lowrank_up,
    first_moment_down,
    first_moment_up,
    second_moment_down,
    second_moment_up,
):
    seq_count_axis = lax.axis_size("seq")
    seq_share = 1.0 / seq_count_axis
    down_portion = lowrank_down.astype(jnp.bfloat16)
    up_portion = lowrank_up.astype(jnp.bfloat16)
    down_edges = (
        0,
        MODEL_WIDTH,
        2 * MODEL_WIDTH,
        3 * MODEL_WIDTH,
        4 * MODEL_WIDTH,
        4 * MODEL_WIDTH + FF,
    )
    up_edges = (
        0,
        6 * MODEL_WIDTH,
        9 * MODEL_WIDTH,
        10 * MODEL_WIDTH,
        10 * MODEL_WIDTH + FF,
        11 * MODEL_WIDTH + FF,
    )

    def fetch():
        across = (
            lax.all_gather(modulation_weight, "seq", axis=1, tiled=True),
            lax.all_gather(query_key_value_weight, "seq", axis=1, tiled=True),
            lax.all_gather(attention_out_weight, "seq", axis=1, tiled=True),
            lax.all_gather(widen_weight, "seq", axis=1, tiled=True),
            lax.all_gather(narrow_weight, "seq", axis=1, tiled=True),
            lax.all_gather(down_portion, "seq", axis=0, tiled=True),
            lax.all_gather(up_portion, "seq", axis=0, tiled=True),
        )
        return (
            lax.all_gather(across[0], "fsdp", axis=0, tiled=True),
            lax.all_gather(across[1], "fsdp", axis=0, tiled=True),
            lax.all_gather(across[2], "fsdp", axis=0, tiled=True),
            lax.all_gather(across[3], "fsdp", axis=0, tiled=True),
            lax.all_gather(across[4], "fsdp", axis=0, tiled=True),
            lax.all_gather(across[5], "fsdp", axis=2, tiled=True),
            lax.all_gather(across[6], "fsdp", axis=2, tiled=True),
        )

    def select(gathered_now, picked_adapter):
        down_sel = gathered_now[5][picked_adapter]
        up_sel = gathered_now[6][picked_adapter]
        down_blocks = [
            down_sel[:, :, down_edges[target] : down_edges[target + 1]] for target in range(5)
        ]
        up_blocks = [up_sel[:, :, up_edges[target] : up_edges[target + 1]] for target in range(5)]
        return (
            gathered_now[0],
            gathered_now[1],
            gathered_now[2],
            gathered_now[3],
            gathered_now[4],
            down_blocks,
            up_blocks,
        )

    down_gradient = jnp.zeros((ADAPTER_COUNT, ADAPTER_RANK, down_edges[5]), jnp.float32)
    up_gradient = jnp.zeros((ADAPTER_COUNT, ADAPTER_RANK, up_edges[5]), jnp.float32)
    output_list, token_list, cond_list = ([], [], [])
    for micro_batch in range(MB):
        first_seq = micro_batch * SEQ_MB
        token_rows = tokens[first_seq : first_seq + SEQ_MB].astype(jnp.float32)
        cond_rows = condition[first_seq : first_seq + SEQ_MB]
        picked_adapter = adapter[first_seq : first_seq + SEQ_MB]
        cot_rows = cotangent[first_seq : first_seq + SEQ_MB].astype(jnp.float32)
        batch_seqs = token_rows.shape[0]
        local_rows = token_rows.shape[1]
        gathered = fetch()
        full_ada, full_qkv, full_proj, full_expand, full_shrink, down_blocks, up_blocks = select(
            gathered, picked_adapter
        )
        cond_act = jax.nn.silu(cond_rows).astype(jnp.bfloat16)[:, None, :]
        middle_ada, extra_ada = adapt_forward(cond_act, down_blocks[0], up_blocks[0])
        modulation = linear(cond_act, full_ada) + modulation_bias + extra_ada
        shift_first, scale_first, gate_first, shift_second, scale_second, gate_second = jnp.split(
            modulation, 6, axis=-1
        )
        normed_first, inverse_first = normalize(token_rows)
        hidden = (normed_first * (1.0 + scale_first) + shift_first).astype(jnp.bfloat16)
        middle_qkv, extra_qkv = adapt_forward(hidden, down_blocks[1], up_blocks[1])
        packed = (linear(hidden, full_qkv) + extra_qkv).astype(jnp.bfloat16)
        head_blocks = packed.reshape(
            batch_seqs, local_rows, 3, seq_count_axis, MODEL_WIDTH // seq_count_axis
        )
        by_heads = lax.all_to_all(head_blocks, "seq", split_axis=3, concat_axis=1, tiled=True)
        query_groups = grouped(by_heads[:, :, 0, 0])
        key_groups = grouped(by_heads[:, :, 1, 0])
        value_groups = grouped(by_heads[:, :, 2, 0])
        mixed_groups, log_total = lax.map(attend_group, (query_groups, key_groups, value_groups))
        mixed = lax.all_to_all(
            ungrouped(mixed_groups).astype(jnp.bfloat16),
            "seq",
            split_axis=1,
            concat_axis=2,
            tiled=True,
        )
        middle_proj, extra_proj = adapt_forward(mixed, down_blocks[2], up_blocks[2])
        branch = linear(mixed, full_proj) + attention_out_bias + extra_proj
        residual = token_rows + gate_first * branch
        normed_second, inverse_second = normalize(residual)
        second = (normed_second * (1.0 + scale_second) + shift_second).astype(jnp.bfloat16)
        middle_expand, extra_expand = adapt_forward(second, down_blocks[3], up_blocks[3])
        inner_act = linear(second, full_expand) + widen_bias + extra_expand
        active = gelu_tanh(inner_act).astype(jnp.bfloat16)
        middle_shrink, extra_shrink = adapt_forward(active, down_blocks[4], up_blocks[4])
        final_out = linear(active, full_shrink) + narrow_bias + extra_shrink
        output_list.append((residual + gate_second * final_out).astype(jnp.bfloat16))
        gathered = fetch()
        full_ada, full_qkv, full_proj, full_expand, full_shrink, down_blocks, up_blocks = select(
            gathered, picked_adapter
        )
        d_final = (gate_second * cot_rows).astype(jnp.bfloat16)
        d_gate_second = jnp.sum(cot_rows * final_out, axis=1, keepdims=True)
        d_active, down_shrink, up_shrink = adapt_backward(
            active, middle_shrink, d_final, down_blocks[4], up_blocks[4]
        )
        d_active = d_active + linear_back(d_final, full_shrink)
        d_inner = jax.vjp(gelu_tanh, inner_act)[1](d_active)[0].astype(jnp.bfloat16)
        d_second, down_expand, up_expand = adapt_backward(
            second, middle_expand, d_inner, down_blocks[3], up_blocks[3]
        )
        d_second = d_second + linear_back(d_inner, full_expand)
        d_shift_second = jnp.sum(d_second, axis=1, keepdims=True)
        d_scale_second = jnp.sum(d_second * normed_second, axis=1, keepdims=True)
        d_residual = cot_rows + normalize_back(
            d_second * (1.0 + scale_second), normed_second, inverse_second
        )
        d_branch = (gate_first * d_residual).astype(jnp.bfloat16)
        d_gate_first = jnp.sum(d_residual * branch, axis=1, keepdims=True)
        d_mixed, down_proj, up_proj = adapt_backward(
            mixed, middle_proj, d_branch, down_blocks[2], up_blocks[2]
        )
        d_mixed = (d_mixed + linear_back(d_branch, full_proj)).astype(jnp.bfloat16)
        d_by_heads = lax.all_to_all(d_mixed, "seq", split_axis=2, concat_axis=1, tiled=True)
        dquery_groups, dkey_groups, dvalue_groups = lax.map(
            attend_back, (query_groups, key_groups, value_groups, grouped(d_by_heads), log_total)
        )
        stacked = jnp.stack(
            [
                ungrouped(dquery_groups).astype(jnp.bfloat16),
                ungrouped(dkey_groups).astype(jnp.bfloat16),
                ungrouped(dvalue_groups).astype(jnp.bfloat16),
            ],
            2,
        )[:, :, :, None, :]
        returned = lax.all_to_all(stacked, "seq", split_axis=1, concat_axis=3, tiled=True)
        d_packed = returned.reshape(batch_seqs, local_rows, 3 * MODEL_WIDTH)
        d_hidden, down_qkv, up_qkv = adapt_backward(
            hidden, middle_qkv, d_packed, down_blocks[1], up_blocks[1]
        )
        d_hidden = d_hidden + linear_back(d_packed, full_qkv)
        d_shift_first = jnp.sum(d_hidden, axis=1, keepdims=True)
        d_scale_first = jnp.sum(d_hidden * normed_first, axis=1, keepdims=True)
        token_list.append(
            d_residual + normalize_back(d_hidden * (1.0 + scale_first), normed_first, inverse_first)
        )
        partial_mod = jnp.concatenate(
            [
                d_shift_first,
                d_scale_first,
                d_gate_first,
                d_shift_second,
                d_scale_second,
                d_gate_second,
            ],
            -1,
        )
        d_modulation = lax.psum(partial_mod, "seq").astype(jnp.bfloat16)
        d_cond_act, down_ada, up_ada = adapt_backward(
            cond_act, middle_ada, d_modulation, down_blocks[0], up_blocks[0]
        )
        d_cond_act = d_cond_act + linear_back(d_modulation, full_ada)
        cond_list.append(jax.vjp(jax.nn.silu, cond_rows)[1](d_cond_act[:, 0, :])[0])
        seq_down = jnp.concatenate(
            [down_ada * seq_share, down_qkv, down_proj, down_expand, down_shrink], -1
        )
        seq_up = jnp.concatenate([up_ada * seq_share, up_qkv, up_proj, up_expand, up_shrink], -1)
        selector = jax.nn.one_hot(picked_adapter, ADAPTER_COUNT, dtype=jnp.float32)
        down_gradient = down_gradient + jnp.einsum(
            "sa,src->arc", selector, seq_down, precision=highest
        )
        up_gradient = up_gradient + jnp.einsum("sa,src->arc", selector, seq_up, precision=highest)
    part_down, part_up = (
        lax.psum_scatter(down_gradient, "fsdp", scatter_dimension=2, tiled=True),
        lax.psum_scatter(up_gradient, "fsdp", scatter_dimension=2, tiled=True),
    )
    sequence_down, sequence_up = (
        lax.psum_scatter(
            part_down.astype(jnp.bfloat16), "seq", scatter_dimension=0, tiled=True
        ).astype(jnp.float32),
        lax.psum_scatter(
            part_up.astype(jnp.bfloat16), "seq", scatter_dimension=0, tiled=True
        ).astype(jnp.float32),
    )
    squared = lax.psum(
        jnp.sum(sequence_down * sequence_down) + jnp.sum(sequence_up * sequence_up), ("fsdp", "seq")
    )
    grad_norm = jnp.sqrt(squared)
    clip_factor = jnp.minimum(1.0, clip_limit / (grad_norm + norm_eps))

    def optimizer_update(params, gradient, moment, square):
        gradient = gradient * clip_factor
        moment_new = beta_first * moment + (1.0 - beta_first) * gradient
        square_new = beta_second * square + (1.0 - beta_second) * gradient * gradient
        direction = (
            moment_new
            / (1.0 - beta_first**STEP)
            / (jnp.sqrt(square_new / (1.0 - beta_second**STEP)) + adam_eps)
        )
        return (params - learn_rate * (direction + decay_rate * params), moment_new, square_new)

    stepped_down, next_first_down, next_second_down = optimizer_update(
        lowrank_down, sequence_down, first_moment_down, second_moment_down
    )
    stepped_up, next_first_up, next_second_up = optimizer_update(
        lowrank_up, sequence_up, first_moment_up, second_moment_up
    )
    block_out = jnp.concatenate(output_list, 0)
    token_grad = jnp.concatenate(token_list, 0)
    cond_grad = jnp.concatenate(cond_list, 0)
    return (
        block_out,
        token_grad,
        cond_grad,
        grad_norm,
        stepped_down,
        stepped_up,
        next_first_down,
        next_first_up,
        next_second_down,
        next_second_up,
    )


def solution(mesh):
    in_specs = (
        P("fsdp", "seq", None),
        P("fsdp", None),
        P("fsdp"),
        P("fsdp", "seq", None),
        P("fsdp", "seq"),
        P(),
        P("fsdp", "seq"),
        P("fsdp", "seq"),
        P(),
        P("fsdp", "seq"),
        P(),
        P("fsdp", "seq"),
        P(),
        P("seq", None, "fsdp"),
        P("seq", None, "fsdp"),
        P("seq", None, "fsdp"),
        P("seq", None, "fsdp"),
        P("seq", None, "fsdp"),
        P("seq", None, "fsdp"),
    )
    out_specs = (
        P("fsdp", "seq", None),
        P("fsdp", "seq", None),
        P("fsdp", None),
        P(),
        P("seq", None, "fsdp"),
        P("seq", None, "fsdp"),
        P("seq", None, "fsdp"),
        P("seq", None, "fsdp"),
        P("seq", None, "fsdp"),
        P("seq", None, "fsdp"),
    )
    return jax.shard_map(shards, mesh=mesh, in_specs=in_specs, out_specs=out_specs, check_vma=False)
```

profile of v0, /device:TPU:0, one launch (start us, length us, event | category | flops | bytes accessed | tf_op | source)
XLA Modules:
  0.0 2055.8 jit_solution(5371207684123763938)
XLA Ops:
  79.4 117.2 %all-gather.15.cloned.1.call-done = bf16[8,16,17280]{1,0,2:T(8,128)(2,1)} async-done(((bf16[8,16,1080]{1,0,2:T(8,128)(2,1)}), bf16[8,16,17280]{1,0,2:T(8,128)(2,1)}) %all-gather.15.cloned.1.call-update) | async-done | bytes 4423696 | tf_op jit(solution)/shard_map/all_gather | solution.py:186
  196.6 17.6 constant_dynamic-slice_fusion.14
  221.7 75.5 %all-gather.13.cloned.1.call-done = bf16[8,16,9216]{1,0,2:T(8,128)(2,1)} async-done(((bf16[8,16,576]{1,0,2:T(8,128)(2,1)}), bf16[8,16,9216]{1,0,2:T(8,128)(2,1)}) %all-gather.13.cloned.1.call-update) | async-done | bytes 2359312 | tf_op jit(solution)/shard_map/all_gather | solution.py:185
  297.2 17.9 constant_dynamic-slice_fusion.5
  342.5 78.5 %all-gather.11.cloned.1.call-done = bf16[1152,6912]{1,0:T(8,128)(2,1)} async-done(((bf16[72,6912]{1,0:T(8,128)(2,1)}), bf16[1152,6912]{1,0:T(8,128)(2,1)}) %all-gather.11.cloned.1.call-update) | async-done | bytes 15925264 | tf_op jit(solution)/shard_map/all_gather | solution.py:180
  436.6 56.7 %all-gather.17.cloned.1.call-done = bf16[1152,3456]{1,0:T(8,128)(2,1)} async-done(((bf16[72,3456]{1,0:T(8,128)(2,1)}), bf16[1152,3456]{1,0:T(8,128)(2,1)}) %all-gather.17.cloned.1.call-update) | async-done | bytes 7962640 | tf_op jit(solution)/shard_map/all_gather | solution.py:181
  519.6 23.4 %constant_dynamic-slice_fusion.1 = (bf16[1,16,4608]{1,0,2:T(2,128)(2,1)}, bf16[1,16,4608]{1,0,2:T(2,128)(2,1)}, bf16[1,16,4608]{1,0,2:T(2,128)(2,1)}, bf16[1,16,4608]{1,0,2:T(2,128)(2,1)}) fusion(bf16[8,16,17280]{1,0,2:T(8,128)(2,1)} %all-gather.15.cloned.1.call-done, s32[]{:T(128)} %bitcast.85, s32[]{:T(128)S(6)} %add.540, s32[]{:T(128)} %bitcast.42, ...), kind=kLoop, calls=%fused_computation.423 | loop fusion | bytes 1179664 | tf_op jit(solution)/shard_map/slice | solution.py:195
  558.6 22.1 %while.56 = (s32[]{:T(128)}, bf16[4,1,1024,2,72]{2,4,3,1,0:T(8,128)(2,1)}, f32[4,1,2,1024,1]{3,2,4,1,0:T(2,128)}, bf16[4,1,1024,2,72]{2,4,3,1,0:T(8,128)(2,1)S(1...) while((s32[]{:T(128)}, ...), condition=%wide.region_5.6_spmd, body=%wide.region_2.5_spmd.sunk | while | flops 622852096 | bytes 36145296 | solution.py:238
  640.7 75.6 %all-gather.21.cloned.1.call-done = bf16[1152,4608]{1,0:T(8,128)(2,1)} async-done(((bf16[72,4608]{1,0:T(8,128)(2,1)}), bf16[1152,4608]{1,0:T(8,128)(2,1)}) %all-gather.21.cloned.1.call-update) | async-done | bytes 10616848 | tf_op jit(solution)/shard_map/all_gather | solution.py:183
  821.0 183.6 %while.58 = (s32[]{:T(128)}, bf16[4,1,1024,2,72]{2,4,3,1,0:T(8,128)(2,1)}, bf16[4,1,1024,2,72]{2,4,3,1,0:T(8,128)(2,1)}, bf16[4,1,1024,2,72]{2,4,3,1,0:T(8,128)(...) while((s32[]{:T(128)}, ...), condition=%wide.region_20.21_spmd, body=%wide.region_18.20_spmd.sunk | while | flops 1553995776 | bytes 96171120 | solution.py:284
  831.9 15.6 fusion.511
  877.8 15.6 fusion.511
  923.7 15.6 fusion.511
  939.3 13.7 fusion.512
  969.6 15.6 fusion.511
  1033.3 45.3 %all-to-all-done.5 = bf16[1,1024,3,1,576]{4,2,3,0,1:T(4,128)(2,1)} async-done(((bf16[1,1024,3,1,576]{4,2,3,0,1:T(4,128)(2,1)}), bf16[1,1024,3,1,576]{4,2,3,0,1:T(4,128)(2,1)}, u32[]{:S(2)}, u32[]{:S(2)}) %all-to-all-start.5) | async-done | bytes 3538976 | tf_op jit(solution)/shard_map/all_to_all | solution.py:295
  1078.6 14.9 copy.205
  1149.5 23.3 %all-to-all-done.2 = bf16[1,512,3,2,576]{1,4,2,0,3:T(8,128)(2,1)} async-done(((bf16[1,512,3,2,576]{1,4,2,0,3:T(8,128)(2,1)}), bf16[1,512,3,2,576]{1,4,2,0,3:T(8,128)(2,1)}, u32[]{:S(2)}, u32[]{:S(2)}) %all-to-all-start.2) | async-done | bytes 3538976 | tf_op jit(solution)/shard_map/all_to_all | solution.py:234
  1178.8 30.2 %while.57 = (s32[]{:T(128)}, bf16[4,1,1024,2,72]{2,4,3,1,0:T(8,128)(2,1)}, f32[4,1,2,1024,1]{3,2,4,1,0:T(2,128)}, bf16[4,1,1024,2,72]{2,4,3,1,0:T(8,128)(2,1)}, ...) while((s32[]{:T(128)}, ...), condition=%wide.region_13.14_spmd, body=%wide.region_10.13_spmd.sunk | while | flops 622852096 | bytes 36145296 | solution.py:238
  1374.7 183.6 %while.59 = (s32[]{:T(128)}, bf16[4,1,1024,2,72]{2,4,3,1,0:T(8,128)(2,1)}, bf16[4,1,1024,2,72]{2,4,3,1,0:T(8,128)(2,1)}, bf16[4,1,1024,2,72]{2,4,3,1,0:T(8,128)(...) while((s32[]{:T(128)}, ...), condition=%wide.region_27.28_spmd, body=%wide.region_25.27_spmd.sunk | while | flops 1553995776 | bytes 96171120 | solution.py:284
  1385.6 15.6 fusion.526
  1431.5 15.6 fusion.526
  1477.4 15.6 fusion.526
  1493.0 13.7 fusion.527
  1523.3 15.6 fusion.526
  1580.2 48.4 %all-to-all-done.7 = bf16[1,1024,3,1,576]{4,2,3,0,1:T(4,128)(2,1)} async-done(((bf16[1,1024,3,1,576]{4,2,3,0,1:T(4,128)(2,1)}), bf16[1,1024,3,1,576]{4,2,3,0,1:T(4,128)(2,1)}, u32[]{:S(2)}, u32[]{:S(2)}) %all-to-all-start.7) | async-done | bytes 3538976 | tf_op jit(solution)/shard_map/all_to_all | solution.py:295
  1628.6 14.9 copy.206
  1660.2 15.2 all-reduce.1
  1694.0 18.9 copy.207
  1712.8 23.9 %reshape.1309 = f32[9216,128]{1,0:T(8,128)} reshape(f32[9216,8,16]{2,1,0:T(8,128)} %bitcast.805) | data formatting | bytes 9437184
  1764.3 200.6 %all-reduce.3 = bf16[8,16,17280]{2,1,0:T(8,128)(2,1)} all-reduce(f32[8,16,17280]{2,1,0:T(8,128)} %multiply_add_fusion), channel_id=4, replica_groups=mesh['fsdp'=16,'seq'=2] {'fsdp'}, use_global_device_ids=true, to_apply=%region_47.48.clone | all-reduce | flops 2211840 | bytes 13271040
  2003.5 39.3 %psum.23 = f32[]{:T(128)} all-reduce(f32[]{:T(128)S(6)} %add.489), channel_id=1, replica_groups=mesh['fsdp'=16,'seq'=2] {'fsdp','seq'}, use_global_device_ids=true, to_apply=%region_50.51 | all-reduce | flops 1 | bytes 8 | tf_op jit(solution)/shard_map/psum | solution.py:344
  (803 shorter events, 971.5 us)
Async XLA Ops:
  7.2 189.4 %all-gather.15.cloned.1.call-start = ((), (), s32[]{:S(2)}) async-start(), calls=%async_computation.13 | async-start | bytes 37601280 | tf_op jit(solution)/shard_map/all_gather | solution.py:186
  18.2 278.9 %all-gather.13.cloned.1.call-start = ((), (), s32[]{:S(2)}) async-start(), calls=%async_computation.12 | async-start | bytes 20054016 | tf_op jit(solution)/shard_map/all_gather | solution.py:185
  25.3 395.6 %all-gather.11.cloned.1.call-start = ((), (), s32[]{:S(2)}) async-start(), calls=%async_computation.11 | async-start | bytes 16920576 | tf_op jit(solution)/shard_map/all_gather | solution.py:180
  37.6 455.7 %all-gather.17.cloned.1.call-start = ((), (), s32[]{:S(2)}) async-start(), calls=%async_computation.14 | async-start | bytes 8460288 | tf_op jit(solution)/shard_map/all_gather | solution.py:181
  46.4 559.5 %all-gather.23.cloned.1.call-start = ((), (), s32[]{:S(2)}) async-start(), calls=%async_computation.17 | async-start | bytes 11280384 | tf_op jit(solution)/shard_map/all_gather | solution.py:184
  55.3 20.8 %copy-start.3 = (bf16[2,512,1152]{2,1,0:T(8,128)(2,1)S(1)}, bf16[2,512,1152]{2,1,0:T(8,128)(2,1)}, u32[]{:S(2)}) copy-start(bf16[2,512,1152]{2,1,0:T(8,128)(2,1)} %param.27) | copy-start | bytes 7077892
  56.7 574.6 %all-gather.19.cloned.1.call-start = ((), (), s32[]{:S(2)}) async-start(), calls=%async_computation.15 | async-start | bytes 2820096 | tf_op jit(solution)/shard_map/all_gather | solution.py:182
  63.6 652.7 %all-gather.21.cloned.1.call-start = ((), (), s32[]{:S(2)}) async-start(), calls=%async_computation.16 | async-start | bytes 11280384 | tf_op jit(solution)/shard_map/all_gather | solution.py:183
  76.3 137.9 %copy-start.164 = (f32[512]{0:T(512)}, f32[512]{0:T(512)S(1)}, u32[]{:S(2)}) copy-start(f32[512]{0:T(512)S(1)} %broadcast_multiply_fusion.11) | copy-start | bytes 6148
  435.6 57.8 %copy-start.28 = (bf16[512,1152]{1,0:T(8,128)(2,1)}, bf16[512,1152]{1,0:T(8,128)(2,1)S(1)}, u32[]{:S(2)}) copy-start(bf16[512,1152]{1,0:T(8,128)(2,1)S(1)} %fusion.244) | copy-start | bytes 3538948
  510.0 46.1 %all-to-all-start = ((bf16[1,512,3,2,576]{1,4,2,0,3:T(8,128)(2,1)}), bf16[1,512,3,2,576]{1,4,2,0,3:T(8,128)(2,1)S(1)}, u32[]{:S(2)}, u32[]{:S(2)}) async-start(bf16[1,512,3,2,576]{1,4,2,0,3:T(8,128)(2,1)} %copy.154), calls=%async_computation | async-start | bytes 7077888 | tf_op jit(solution)/shard_map/all_to_all | solution.py:234
  602.1 19.5 all-to-all-start.1
  637.2 121.6 %copy-start.1 = (f32[1,512,1152]{2,1,0:T(8,128)}, f32[1,512,1152]{2,1,0:T(8,128)S(1)}, u32[]{:S(2)}) copy-start(f32[1,512,1152]{2,1,0:T(8,128)S(1)} %get-tuple-element.394) | copy-start | bytes 7077892
  785.6 27.4 %all-to-all-start.4 = ((bf16[2,2,147456]{2,1,0:T(2,128)(2,1)}), bf16[2,2,147456]{2,1,0:T(2,128)(2,1)}, u32[]{:S(2)}, u32[]{:S(2)}) async-start(bf16[2,2,147456]{2,1,0:T(2,128)(2,1)} %reshape.1340), calls=%async_computation.4 | async-start | bytes 2359296 | tf_op jit(solution)/shard_map/all_to_all | solution.py:283
  813.0 294.9 %copy-start.92 = (f32[1152]{0:T(1024)}, f32[1152]{0:T(1024)S(1)}, u32[]{:S(2)}) copy-start(f32[1152]{0:T(1024)S(1)} %get-tuple-element.313) | copy-start | bytes 13828
  1013.2 65.5 %all-to-all-start.5 = ((bf16[1,1024,3,1,576]{4,2,3,0,1:T(4,128)(2,1)}), bf16[1,1024,3,1,576]{4,2,3,0,1:T(4,128)(2,1)}, u32[]{:S(2)}, u32[]{:S(2)}) async-start(bf16[1,1024,3,1,576]{4,2,3,0,1:T(4,128)(2,1)} %copy.183), calls=%async_computation.5 | async-start | bytes 10485760 | tf_op jit(solution)/shard_map/all_to_all | solution.py:295
  1127.0 45.7 %all-to-all-start.2 = ((bf16[1,512,3,2,576]{1,4,2,0,3:T(8,128)(2,1)}), bf16[1,512,3,2,576]{1,4,2,0,3:T(8,128)(2,1)}, u32[]{:S(2)}, u32[]{:S(2)}) async-start(bf16[1,512,3,2,576]{1,4,2,0,3:T(8,128)(2,1)} %copy.168), calls=%async_computation.2 | async-start | bytes 7077888 | tf_op jit(solution)/shard_map/all_to_all | solution.py:234
  1229.8 18.7 all-to-all-start.3
  1284.5 24.6 %copy-start.16 = (bf16[512,4608]{1,0:T(8,128)(2,1)}, bf16[512,4608]{1,0:T(8,128)(2,1)S(1)}, u32[]{:S(2)}) copy-start(bf16[512,4608]{1,0:T(8,128)(2,1)S(1)} %get-tuple-element.442) | copy-start | bytes 14155780
  1285.9 32.7 %copy-start.135 = (bf16[512,16]{0,1:T(8,128)(2,1)}, bf16[512,16]{0,1:T(8,128)(2,1)S(1)}, u32[]{:S(2)}) copy-start(bf16[512,16]{0,1:T(8,128)(2,1)S(1)} %convolution_convert_fusion.10) | copy-start | bytes 49156
  1348.9 17.6 all-to-all-start.6
  1566.8 61.8 %all-to-all-start.7 = ((bf16[1,1024,3,1,576]{4,2,3,0,1:T(4,128)(2,1)}), bf16[1,1024,3,1,576]{4,2,3,0,1:T(4,128)(2,1)}, u32[]{:S(2)}, u32[]{:S(2)}) async-start(bf16[1,1024,3,1,576]{4,2,3,0,1:T(4,128)(2,1)} %copy.192), calls=%async_computation.7 | async-start | bytes 10485760 | tf_op jit(solution)/shard_map/all_to_all | solution.py:295
  1572.9 408.6 %reduce-scatter.11.cloned.1.call-start = ((), (), s32[]{:S(2)}) async-start(), calls=%async_computation.20 | async-start | bytes 5013504
  1654.4 29.7 %copy-start.20 = (bf16[1,512,2,576]{1,3,2,0:T(8,128)(2,1)S(1)}, bf16[1,512,2,576]{1,3,2,0:T(8,128)(2,1)}, u32[]{:S(2)}) copy-start(bf16[1,512,2,576]{1,3,2,0:T(8,128)(2,1)} %copy-done.19) | copy-start | bytes 3538948
  1736.8 252.4 %reduce-scatter.9.cloned.1.call-start = ((), (), s32[]{:S(2)}) async-start(), calls=%async_computation.19 | async-start | bytes 442368 | tf_op jit(solution)/shard_map/reduce_scatter | solution.py:340
  1764.3 202.5 %copy-start.170 = (f32[512]{0:T(512)S(1)}, f32[512]{0:T(512)}, u32[]{:S(2)}) copy-start(f32[512]{0:T(512)} %broadcast_multiply_fusion.9) | copy-start | bytes 6148
  1764.3 202.5 %copy-start.173 = (f32[512]{0:T(512)S(1)}, f32[512]{0:T(512)}, u32[]{:S(2)}) copy-start(f32[512]{0:T(512)} %copy-done.171) | copy-start | bytes 6148
  1971.4 28.6 %reduce-scatter.7.cloned.1.call-start = ((), (), s32[]{:S(2)}) async-start(), calls=%async_computation.18 | async-start | bytes 245760 | tf_op jit(solution)/shard_map/reduce_scatter | solution.py:337
  1984.9 58.6 %copy-start.65 = (f32[4,16,576]{2,1,0:T(8,128)S(1)}, f32[4,16,576]{2,1,0:T(8,128)}, u32[]{:S(2)}) copy-start(f32[4,16,576]{2,1,0:T(8,128)} %param.40) | copy-start | bytes 442372
  1985.0 60.5 %copy-start.57 = (f32[4,16,1080]{2,1,0:T(8,128)S(1)}, f32[4,16,1080]{2,1,0:T(8,128)}, u32[]{:S(2)}) copy-start(f32[4,16,1080]{2,1,0:T(8,128)} %param.41) | copy-start | bytes 829444
  1985.0 60.5 %copy-start.88 = (f32[4,16,1080]{2,1,0:T(8,128)S(1)}, f32[4,16,1080]{2,1,0:T(8,128)}, u32[]{:S(2)}) copy-start(f32[4,16,1080]{2,1,0:T(8,128)} %param.43) | copy-start | bytes 829444
  1985.0 60.4 %copy-start.89 = (f32[4,16,1080]{2,1,0:T(8,128)S(1)}, f32[4,16,1080]{2,1,0:T(8,128)}, u32[]{:S(2)}) copy-start(f32[4,16,1080]{2,1,0:T(8,128)} %param.45) | copy-start | bytes 829444
  (209 other events, 1211.9 us)
Sparse Core Ops, SparseCore 0:
  18.4 178.1 all-gather.14
  198.2 98.9 all-gather.12
  299.4 121.5 all-gather.10
  422.9 70.3 all-gather.16
  495.5 87.0 all-gather.22
  585.1 41.5 all-gather.18
  629.0 87.2 all-gather.20
  1736.9 105.0 reduce-scatter.10
  1971.5 15.1 reduce-scatter.8
  1989.4 10.6 reduce-scatter.6
where the time goes:
time: 2070 us; the launch traced here: 2060 us
  matrix products  647 us (31%)
  waiting for transfers between devices  553 us (27%)
  local copies, waits for them, and re-layouts  374 us (18%)
  blocking collectives  309 us (15%)
  other arithmetic  108 us (5%)
  starting transfers between devices  39.9 us (2%)
  between operations  24.8 us (1%)
    unnamed x1, blocking collectives  201 us
    unnamed x465, local copies, waits for them, and re-layouts  168 us
    dot_general x8, matrix products, attend_back(): jnp.einsum('shqk,skhd->sqhd', d_scores, all_keys, preferred_element_type=...  125 us
    all_gather x1, waiting for transfers between devices, fetch(): lax.all_gather(across[6], 'fsdp', axis=2, tiled=True)  117 us
    dot_general x8, matrix products, attend_back(): jnp.einsum('shqk,sqhd->skhd', d_scores, queries, preferred_element_type=j...  109 us
    all_to_all x2, waiting for transfers between devices, shards(): lax.all_to_all(stacked, 'seq', split_axis=1, concat_axis=3, tiled=True)  93.7 us
    dot_general x10, matrix products, linear_back(): jnp.einsum('sto,io->sti', gradient, weight, preferred_element_type=jnp.fl...  84.7 us
    all_gather x1, waiting for transfers between devices, fetch(): lax.all_gather(across[0], 'fsdp', axis=0, tiled=True)  78.5 us
  transfers between devices with their start and end apart: 18, of which 12 were waited for; matrix products, arithmetic and copies ran while one was open for 17% of the time, Pallas kernels for 0%

commit v1 on v0

--- a/solution.py
+++ b/solution.py
@@ -1,6 +1,10 @@
+import functools
+
 import jax
 import jax.numpy as jnp
 from jax import lax
+from jax.experimental import pallas as pl
+from jax.experimental.pallas import tpu as pltpu
 from jax.sharding import PartitionSpec as P
 
 MODEL_WIDTH = 1152
@@ -381,6 +385,473 @@
     )
 
 
+HEADS = 16
+LOG2E = 1.4426950408889634
+SCORE_SCALE = HD ** (-0.5)
+
+
+def tn(left, right):
+    return lax.dot_general(left, right, (((0,), (0,)), ((), ())), preferred_element_type=jnp.float32)
+
+
+def nn(left, right):
+    return lax.dot_general(left, right, (((1,), (0,)), ((), ())), preferred_element_type=jnp.float32)
+
+
+def nt(left, right):
+    return lax.dot_general(left, right, (((1,), (1,)), ((), ())), preferred_element_type=jnp.float32)
+
+
+def heads_kernel(qkv_ref, mixed_ref, log_ref, *, step):
+    length = qkv_ref.shape[-1]
+    keys = qkv_ref[1, 0].astype(jnp.float32).T.astype(jnp.bfloat16)
+    values_t = qkv_ref[2, 0]
+    for start in range(0, length, step):
+        queries_t = qkv_ref[0, 0, :, start : start + step]
+        scores = nn(keys, queries_t) * (SCORE_SCALE * LOG2E)
+        top = jnp.max(scores, axis=0, keepdims=True)
+        exponent = jnp.exp2(scores - top)
+        total = jnp.sum(exponent, axis=0, keepdims=True)
+        weights = (exponent * (1.0 / total)).astype(jnp.bfloat16)
+        mixed_ref[0, :, start : start + step] = nn(values_t, weights).astype(jnp.bfloat16)
+        log_ref[0, :, start : start + step] = top + jnp.log2(total)
+
+
+def heads_forward(qkv, step=256):
+    _, heads, width, length = qkv.shape
+    return pl.pallas_call(
+        functools.partial(heads_kernel, step=step),
+        grid=(heads,),
+        in_specs=[pl.BlockSpec((3, 1, width, length), lambda h: (0, h, 0, 0))],
+        out_specs=[
+            pl.BlockSpec((1, width, length), lambda h: (h, 0, 0)),
+            pl.BlockSpec((1, 1, length), lambda h: (h, 0, 0)),
+        ],
+        out_shape=[
+            jax.ShapeDtypeStruct((heads, width, length), jnp.bfloat16),
+            jax.ShapeDtypeStruct((heads, 1, length), jnp.float32),
+        ],
+        cost_estimate=pl.CostEstimate(
+            flops=4 * heads * length * length * 256,
+            bytes_accessed=10 * heads * width * length,
+            transcendentals=heads * length * length,
+        ),
+        compiler_params=pltpu.CompilerParams(vmem_limit_bytes=48 * 1024 * 1024),
+        name="heads_forward",
+    )(qkv)
+
+
+def heads_back_kernel(qkv_ref, grad_ref, log_ref, out_ref, key_acc, value_acc, *, step):
+    length = qkv_ref.shape[-1]
+    keys_t = qkv_ref[1, 0]
+    keys = keys_t.astype(jnp.float32).T.astype(jnp.bfloat16)
+    values = qkv_ref[2, 0].astype(jnp.float32).T.astype(jnp.bfloat16)
+    for start in range(0, length, step):
+        queries_t = qkv_ref[0, 0, :, start : start + step]
+        grad_t = grad_ref[0, :, start : start + step]
+        queries = queries_t.astype(jnp.float32).T.astype(jnp.bfloat16)
+        grad = grad_t.astype(jnp.float32).T.astype(jnp.bfloat16)
+        scores = nn(keys, queries_t) * (SCORE_SCALE * LOG2E)
+        probable = jnp.exp2(scores - log_ref[0, :, start : start + step])
+        d_weights = nn(values, grad_t)
+        inner_sum = jnp.sum(d_weights * probable, axis=0, keepdims=True)
+        d_scores = (probable * (d_weights - inner_sum)).astype(jnp.bfloat16)
+        d_values = nn(probable.astype(jnp.bfloat16), grad)
+        d_keys = nn(d_scores, queries)
+        if start == 0:
+            value_acc[...] = d_values
+            key_acc[...] = d_keys
+        else:
+            value_acc[...] += d_values
+            key_acc[...] += d_keys
+        out_ref[0, 0, :, start : start + step] = (nn(keys_t, d_scores) * SCORE_SCALE).astype(
+            jnp.bfloat16
+        )
+    out_ref[1, 0] = (key_acc[...] * SCORE_SCALE).T.astype(jnp.bfloat16)
+    out_ref[2, 0] = value_acc[...].T.astype(jnp.bfloat16)
+
+
+def heads_back(qkv, grad, log_total, step=256):
+    _, heads, width, length = qkv.shape
+    return pl.pallas_call(
+        functools.partial(heads_back_kernel, step=step),
+        grid=(heads,),
+        in_specs=[
+            pl.BlockSpec((3, 1, width, length), lambda h: (0, h, 0, 0)),
+            pl.BlockSpec((1, width, length), lambda h: (h, 0, 0)),
+            pl.BlockSpec((1, 1, length), lambda h: (h, 0, 0)),
+        ],
+        out_specs=pl.BlockSpec((3, 1, width, length), lambda h: (0, h, 0, 0)),
+        out_shape=jax.ShapeDtypeStruct((3, heads, width, length), jnp.bfloat16),
+        scratch_shapes=[
+            pltpu.VMEM((length, width), jnp.float32),
+            pltpu.VMEM((length, width), jnp.float32),
+        ],
+        cost_estimate=pl.CostEstimate(
+            flops=10 * heads * length * length * 256,
+            bytes_accessed=16 * heads * width * length,
+            transcendentals=heads * length * length,
+        ),
+        compiler_params=pltpu.CompilerParams(vmem_limit_bytes=48 * 1024 * 1024),
+        name="heads_back",
+    )(qkv, grad, log_total)
+
+
+GELU_RATE = 0.7978845608
+GELU_CUBE = 0.044715
+
+
+def feed_kernel(
+    second_ref,
+    dfinal_ref,
+    middle_ref,
+    dmiddle_ref,
+    widen_ref,
+    narrow_ref,
+    up_ref,
+    down_ref,
+    bias_ref,
+    final_ref,
+    dsecond_ref,
+    up_grad_ref,
+    down_grad_ref,
+    widen_aug,
+    narrow_aug,
+    *,
+    rows,
+):
+    chunk = pl.program_id(0)
+    width = widen_ref.shape[0]
+    widen_aug[:width] = widen_ref[...]
+    widen_aug[width:] = up_ref[...]
+    narrow_aug[:, :width] = narrow_ref[...]
+    narrow_aug[:, width:] = down_ref[...]
+
+    @pl.when(chunk == 0)
+    def _():
+        final_ref[...] = jnp.zeros_like(final_ref)
+        dsecond_ref[...] = jnp.zeros_like(dsecond_ref)
+
+    up_grad_ref[...] = jnp.zeros_like(up_grad_ref)
+    down_grad_ref[...] = jnp.zeros_like(down_grad_ref)
+
+    def body(index, carry):
+        at = pl.ds(pl.multiple_of(index * rows, rows), rows)
+        inner = nn(second_ref[at, :], widen_aug[...]) + bias_ref[...]
+        square = inner * inner
+        tanh = jnp.tanh(GELU_RATE * inner * (1.0 + GELU_CUBE * square))
+        half = 0.5 * (1.0 + tanh)
+        active = (inner * half).astype(jnp.bfloat16)
+        slope = half + inner * (half * (1.0 - tanh)) * (
+            GELU_RATE * (1.0 + (3.0 * GELU_CUBE) * square)
+        )
+        final_ref[at, :] += nn(active, narrow_aug[...])
+        d_inner = (nt(dfinal_ref[at, :], narrow_aug[...]) * slope).astype(jnp.bfloat16)
+        dsecond_ref[at, :] += nt(d_inner, widen_aug[...])
+        up_grad_ref[...] += nn(middle_ref[:, at], d_inner)
+        down_grad_ref[...] += nn(dmiddle_ref[:, at], active)
+        return carry
+
+    lax.fori_loop(0, second_ref.shape[0] // rows, body, 0)
+
+
+def feed(second, dfinal, middle, dmiddle, widen, narrow, up, down, bias, chunk=768, rows=256):
+    length, padded = second.shape
+    width, hidden = widen.shape
+    rank = middle.shape[0]
+    whole = lambda j: (0, 0)
+    columns = lambda j: (0, j)
+    return pl.pallas_call(
+        functools.partial(feed_kernel, rows=rows),
+        grid=(hidden // chunk,),
+        in_specs=[
+            pl.BlockSpec((length, padded), whole),
+            pl.BlockSpec((length, padded), whole),
+            pl.BlockSpec((rank, length), whole),
+            pl.BlockSpec((rank, length), whole),
+            pl.BlockSpec((width, chunk), columns),
+            pl.BlockSpec((chunk, width), lambda j: (j, 0)),
+            pl.BlockSpec((padded - width, chunk), columns),
+            pl.BlockSpec((chunk, padded - width), lambda j: (j, 0)),
+            pl.BlockSpec((1, chunk), columns),
+        ],
+        out_specs=[
+            pl.BlockSpec((length, padded), whole),
+            pl.BlockSpec((length, padded), whole),
+            pl.BlockSpec((rank, chunk), columns),
+            pl.BlockSpec((rank, chunk), columns),
+        ],
+        out_shape=[
+            jax.ShapeDtypeStruct((length, padded), jnp.float32),
+            jax.ShapeDtypeStruct((length, padded), jnp.float32),
+            jax.ShapeDtypeStruct((rank, hidden), jnp.float32),
+            jax.ShapeDtypeStruct((rank, hidden), jnp.float32),
+        ],
+        scratch_shapes=[
+            pltpu.VMEM((padded, chunk), jnp.bfloat16),
+            pltpu.VMEM((chunk, padded), jnp.bfloat16),
+        ],
+        cost_estimate=pl.CostEstimate(
+            flops=8 * length * padded * hidden,
+            bytes_accessed=4 * width * hidden + 12 * length * padded,
+            transcendentals=length * hidden,
+        ),
+        compiler_params=pltpu.CompilerParams(vmem_limit_bytes=60 * 1024 * 1024),
+        name="feed",
+    )(second, dfinal, middle, dmiddle, widen, narrow, up, down, bias)
+
+
+RANK = ADAPTER_RANK
+DOWN_EDGES = (0, 1152, 2304, 3456, 4608, 9216)
+UP_EDGES = (0, 6912, 10368, 11520, 16128, 17280)
+PADDED = MODEL_WIDTH + 128
+
+
+def fits(mesh):
+    return mesh.shape["seq"] == MB and mesh.shape["fsdp"] == 16
+
+
+def dot(equation, left, right):
+    return jnp.einsum(equation, left, right, preferred_element_type=jnp.float32)
+
+
+def swap(block):
+    return lax.ppermute(block, "seq", [(0, 1), (1, 0)])
+
+
+def join(own, other, mine, axis):
+    first = mine == 0
+    return jnp.concatenate(
+        [jnp.where(first, own, other), jnp.where(first, other, own)], axis
+    )
+
+
+def fast_shards(
+    tokens,
+    condition,
+    adapter,
+    cotangent,
+    modulation_weight,
+    modulation_bias,
+    query_key_value_weight,
+    attention_out_weight,
+    attention_out_bias,
+    widen_weight,
+    widen_bias,
+    narrow_weight,
+    narrow_bias,
+    lowrank_down,
+    lowrank_up,
+    first_moment_down,
+    first_moment_up,
+    second_moment_down,
+    second_moment_up,
+):
+    bf16 = jnp.bfloat16
+    n_fsdp = lax.axis_size("fsdp")
+    mine = lax.axis_index("seq")
+    row = lax.axis_index("fsdp")
+
+    def gather(weight):
+        return lax.all_gather(
+            join(weight, swap(weight), mine, 1), "fsdp", axis=0, tiled=True
+        )
+
+    full_qkv = gather(query_key_value_weight)
+    full_proj = gather(attention_out_weight)
+    full_widen = gather(widen_weight)
+    full_narrow = gather(narrow_weight)
+
+    token_rows = lax.all_to_all(tokens, "seq", split_axis=0, concat_axis=1, tiled=True)[0]
+    cot_rows = lax.all_to_all(cotangent, "seq", split_axis=0, concat_axis=1, tiled=True)[0]
+    token_rows = token_rows.astype(jnp.float32)
+    cot_rows = cot_rows.astype(jnp.float32)
+
+    every_adapter = lax.all_gather(adapter, "fsdp", axis=0, tiled=True)
+    own_ids = lax.dynamic_index_in_dim(every_adapter.reshape(n_fsdp, MB), mine, 1, False)
+    portions = jnp.concatenate([lowrank_down.astype(bf16), lowrank_up.astype(bf16)], -1)
+    table = join(portions, swap(portions), mine, 0)
+    picks = jax.nn.one_hot(own_ids, ADAPTER_COUNT, dtype=bf16)
+    chosen = dot("fa,arc->frc", picks, table).astype(bf16)
+    chosen = lax.all_to_all(chosen, "fsdp", split_axis=0, concat_axis=0, tiled=True)
+    down_chunk = lowrank_down.shape[-1]
+    up_chunk = lowrank_up.shape[-1]
+    down_all = jnp.moveaxis(chosen[:, :, :down_chunk], 0, 1).reshape(RANK, -1)
+    up_all = jnp.moveaxis(chosen[:, :, down_chunk:], 0, 1).reshape(RANK, -1)
+    downs = [down_all[:, DOWN_EDGES[i] : DOWN_EDGES[i + 1]] for i in range(5)]
+    ups = [up_all[:, UP_EDGES[i] : UP_EDGES[i + 1]] for i in range(5)]
+
+    cond_act_pair = jax.nn.silu(condition).astype(bf16)
+    every_cond = lax.all_gather(cond_act_pair, "fsdp", axis=0, tiled=True)
+    depth = modulation_weight.shape[0]
+    cond_slice = lax.dynamic_slice_in_dim(every_cond, row * depth, depth, 1)
+    part = dot("si,io->so", cond_slice, modulation_weight)
+    part = part.reshape(n_fsdp, MB, -1)
+    part = lax.all_to_all(part, "fsdp", split_axis=0, concat_axis=0, tiled=True)
+    pair_half = jnp.sum(part, axis=0)
+    mod_base = lax.all_to_all(pair_half, "seq", split_axis=0, concat_axis=1, tiled=True)
+    cond_act = lax.dynamic_slice_in_dim(cond_act_pair, mine, 1, 0)
+    middle_ada = dot("ti,ri->tr", cond_act, downs[0]).astype(bf16)
+    modulation = mod_base + modulation_bias + dot("tr,ro->to", middle_ada, ups[0])
+    shift_first, scale_first, gate_first, shift_second, scale_second, gate_second = jnp.split(
+        modulation, 6, axis=-1
+    )
+
+    length = token_rows.shape[0]
+    normed_first, inverse_first = normalize(token_rows)
+    hidden = (normed_first * (1.0 + scale_first) + shift_first).astype(bf16)
+    middle_qkv = dot("ti,ri->tr", hidden, downs[1]).astype(bf16)
+    packed = dot(
+        "ti,io->ot",
+        jnp.concatenate([hidden, middle_qkv], 1),
+        jnp.concatenate([full_qkv, ups[1]], 0),
+    ).astype(bf16)
+    qkv = packed.reshape(3, HEADS, HD, length)
+    mixed_heads, log_total = heads_forward(qkv, step=1024)
+    mixed = mixed_heads.reshape(MODEL_WIDTH, length)
+
+    middle_proj = dot("it,ri->tr", mixed, downs[2]).astype(bf16)
+    branch = (
+        dot("it,io->to", mixed, full_proj)
+        + attention_out_bias
+        + dot("tr,ro->to", middle_proj, ups[2])
+    )
+    residual = token_rows + gate_first * branch
+    normed_second, inverse_second = normalize(residual)
+    second = (normed_second * (1.0 + scale_second) + shift_second).astype(bf16)
+    middle_expand = dot("ti,ri->tr", second, downs[3]).astype(bf16)
+    d_final = (gate_second * cot_rows).astype(bf16)
+    dmiddle_shrink = dot("to,ro->tr", d_final, ups[4]).astype(bf16)
+
+    fill = jnp.zeros((length, 128 - RANK), bf16)
+    final_ext, dsecond_ext, up_expand, down_shrink = feed(
+        jnp.concatenate([second, middle_expand, fill], 1),
+        jnp.concatenate([d_final, dmiddle_shrink, fill], 1),
+        middle_expand.T,
+        dmiddle_shrink.T,
+        full_widen,
+        full_narrow,
+        jnp.pad(ups[3], ((0, 128 - RANK), (0, 0))),
+        jnp.pad(downs[4].T, ((0, 0), (0, 128 - RANK))),
+        widen_bias[None],
+        chunk=512,
+        rows=1024,
+    )
+    middle_shrink = final_ext[:, MODEL_WIDTH : MODEL_WIDTH + RANK].astype(bf16)
+    final_out = (
+        final_ext[:, :MODEL_WIDTH] + narrow_bias + dot("tr,ro->to", middle_shrink, ups[4])
+    )
+    block_rows = (residual + gate_second * final_out).astype(bf16)
+    block_out = lax.all_to_all(block_rows[None], "seq", split_axis=1, concat_axis=0, tiled=True)
+    d_gate_second = jnp.sum(cot_rows * final_out, axis=0, keepdims=True)
+    up_shrink = dot("tr,to->ro", middle_shrink, d_final)
+    dmiddle_expand = dsecond_ext[:, MODEL_WIDTH : MODEL_WIDTH + RANK].astype(bf16)
+    down_expand = dot("tr,ti->ri", dmiddle_expand, second)
+    d_second = dsecond_ext[:, :MODEL_WIDTH] + dot("tr,ri->ti", dmiddle_expand, downs[3])
+    d_shift_second = jnp.sum(d_second, axis=0, keepdims=True)
+    d_scale_second = jnp.sum(d_second * normed_second, axis=0, keepdims=True)
+    d_residual = cot_rows + normalize_back(
+        d_second * (1.0 + scale_second), normed_second, inverse_second
+    )
+    d_branch = (gate_first * d_residual).astype(bf16)
+    d_gate_first = jnp.sum(d_residual * branch, axis=0, keepdims=True)
+    up_proj = dot("tr,to->ro", middle_proj, d_branch)
+    dmiddle_proj = dot("to,ro->tr", d_branch, ups[2]).astype(bf16)
+    down_proj = dot("tr,it->ri", dmiddle_proj, mixed)
+    d_mixed = (
+        dot("to,io->it", d_branch, full_proj) + dot("tr,ri->it", dmiddle_proj, downs[2])
+    ).astype(bf16)
+
+    d_qkv = heads_back(qkv, d_mixed.reshape(HEADS, HD, length), log_total, step=512)
+    d_packed = d_qkv.reshape(3 * MODEL_WIDTH, length)
+    up_qkv = dot("tr,ot->ro", middle_qkv, d_packed)
+    dmiddle_qkv = dot("ot,ro->tr", d_packed, ups[1]).astype(bf16)
+    down_qkv = dot("tr,ti->ri", dmiddle_qkv, hidden)
+    d_hidden = dot("ot,io->ti", d_packed, full_qkv) + dot("tr,ri->ti", dmiddle_qkv, downs[1])
+    d_shift_first = jnp.sum(d_hidden, axis=0, keepdims=True)
+    d_scale_first = jnp.sum(d_hidden * normed_first, axis=0, keepdims=True)
+    token_back = d_residual + normalize_back(
+        d_hidden * (1.0 + scale_first), normed_first, inverse_first
+    )
+    token_grad = lax.all_to_all(
+        token_back.astype(bf16)[None], "seq", split_axis=1, concat_axis=0, tiled=True
+    ).astype(jnp.float32)
+
+    d_modulation = jnp.concatenate(
+        [
+            d_shift_first,
+            d_scale_first,
+            d_gate_first,
+            d_shift_second,
+            d_scale_second,
+            d_gate_second,
+        ],
+        -1,
+    ).astype(bf16)
+    up_ada = dot("tr,to->ro", middle_ada, d_modulation)
+    dmiddle_ada = dot("to,ro->tr", d_modulation, ups[0]).astype(bf16)
+    down_ada = dot("tr,ti->ri", dmiddle_ada, cond_act)
+    own_cond = dot("tr,ri->ti", dmiddle_ada, downs[0])
+    mod_half = lax.all_to_all(d_modulation, "seq", split_axis=1, concat_axis=0, tiled=True)
+    every_mod = lax.all_gather(mod_half, "fsdp", axis=0, tiled=True)
+    cond_part = dot("so,io->si", every_mod, modulation_weight).reshape(n_fsdp, MB, -1)
+    cond_part = lax.all_to_all(cond_part, "fsdp", split_axis=0, concat_axis=0, tiled=True)
+    d_cond = jnp.moveaxis(cond_part, 0, 1).reshape(MB, MODEL_WIDTH)
+    d_cond = d_cond + jnp.where(jnp.arange(MB)[:, None] == mine, own_cond, 0.0)
+    d_cond = d_cond + swap(d_cond)
+    cond_grad = jax.vjp(jax.nn.silu, condition)[1](d_cond)[0]
+
+    seq_down = jnp.concatenate([down_ada, down_qkv, down_proj, down_expand, down_shrink], -1)
+    seq_up = jnp.concatenate([up_ada, up_qkv, up_proj, up_expand, up_shrink], -1)
+    sent = jnp.concatenate(
+        [seq_down.reshape(RANK, n_fsdp, down_chunk), seq_up.reshape(RANK, n_fsdp, up_chunk)], -1
+    )
+    sent = jnp.moveaxis(sent, 1, 0).astype(bf16)
+    came = lax.all_to_all(sent, "fsdp", split_axis=0, concat_axis=0, tiled=True)
+    summed = dot("fa,frc->arc", picks, came)
+    held = lowrank_down.shape[0]
+    kept = lax.dynamic_slice_in_dim(summed, mine * held, held, 0)
+    given = lax.dynamic_slice_in_dim(summed, (1 - mine) * held, held, 0)
+    gradient = kept + swap(given.astype(bf16)).astype(jnp.float32)
+    sequence_down = gradient[:, :, :down_chunk]
+    sequence_up = gradient[:, :, down_chunk:]
+
+    squared = jnp.broadcast_to(jnp.sum(gradient * gradient), (n_fsdp * MB, 128))
+    squared = lax.all_to_all(squared, ("fsdp", "seq"), split_axis=0, concat_axis=0, tiled=True)
+    grad_norm = jnp.sqrt(jnp.sum(squared[:, 0]))
+    clip_factor = jnp.minimum(1.0, clip_limit / (grad_norm + norm_eps))
+
+    def optimizer_update(params, gradient, moment, square):
+        gradient = gradient * clip_factor
+        moment_new = beta_first * moment + (1.0 - beta_first) * gradient
+        square_new = beta_second * square + (1.0 - beta_second) * gradient * gradient
+        direction = (
+            moment_new
+            / (1.0 - beta_first**STEP)
+            / (jnp.sqrt(square_new / (1.0 - beta_second**STEP)) + adam_eps)
+        )
+        return (params - learn_rate * (direction + decay_rate * params), moment_new, square_new)
+
+    stepped_down, next_first_down, next_second_down = optimizer_update(
+        lowrank_down, sequence_down, first_moment_down, second_moment_down
+    )
+    stepped_up, next_first_up, next_second_up = optimizer_update(
+        lowrank_up, sequence_up, first_moment_up, second_moment_up
+    )
+    return (
+        block_out,
+        token_grad,
+        cond_grad,
+        grad_norm,
+        stepped_down,
+        stepped_up,
+        next_first_down,
+        next_first_up,
+        next_second_down,
+        next_second_up,
+    )
+
+
 def solution(mesh):
     in_specs = (
         P("fsdp", "seq", None),
@@ -415,4 +886,5 @@
         P("seq", None, "fsdp"),
         P("seq", None, "fsdp"),
     )
-    return jax.shard_map(shards, mesh=mesh, in_specs=in_specs, out_specs=out_specs, check_vma=False)
+    body = fast_shards if fits(mesh) else shards
+    return jax.shard_map(body, mesh=mesh, in_specs=in_specs, out_specs=out_specs, check_vma=False)

time: 2070 us -> 737 us (0.36)
  matrix products: 647 us -> 101 us
  waiting for transfers between devices: 553 us -> 160 us
  local copies, waits for them, and re-layouts: 374 us -> 94 us
  blocking collectives: 309 us -> 86.7 us
  Pallas kernels: 0 us -> 149 us
  other arithmetic: 108 us -> 63.4 us
    dot_general x132 -> x29, matrix products: 647 us -> 101 us  [dot(): return jnp.einsum(equation, left, right, preferred_element_type=jnp.float32)]
    all_gather x7 -> x4, waiting for transfers between devices: 404 us -> 51.1 us  [gather(): lax.all_gather(join(weight, swap(weight), mine, 1), 'fsdp', axis=0, tiled...]
    unnamed x1, blocking collectives: 201 us -> 16.4 us
    pallas_call x0 -> x3, Pallas kernels: none -> 149 us  [the longest x1 64.9 us: feed(): pl.pallas_call(functools.partial(feed_kernel, rows=rows), grid=(hidden //...]
    unnamed x465 -> x144, local copies, waits for them, and re-layouts: 168 us -> 43.4 us
    all_to_all x8 -> x9, waiting for transfers between devices: 140 us -> 50.3 us  [the longest x1 19.5 us: fast_shards(): lax.all_to_all(chosen, 'fsdp', split_axis=0, concat_axis=0, tiled=True)]
    slice x7 -> x3, local copies, waits for them, and re-layouts: 71.3 us -> 1.66 us  [fast_shards(): ups = [up_all[:, UP_EDGES[i]:UP_EDGES[i + 1]] for i in range(5)]]
    ppermute x0 -> x7, waiting for transfers between devices: none -> 58 us  [swap(): return lax.ppermute(block, 'seq', [(0, 1), (1, 0)])]
  transfers between devices with their start and end apart: 18 -> 20, of which waited for: 12 -> 10; matrix products, arithmetic and copies ran while one was open for 17% -> 25% of each run, Pallas kernels for 0% -> 4%
where the time goes in v1:
time: 737 us; the launch traced here: 730 us
  waiting for transfers between devices  160 us (22%)
  Pallas kernels  149 us (20%)
  matrix products  101 us (14%)
  local copies, waits for them, and re-layouts  94 us (13%)
  blocking collectives  86.7 us (12%)
  other arithmetic  63.4 us (9%)
  starting transfers between devices  57.8 us (8%)
  between operations  17.7 us (2%)
    dot_general x29, matrix products, dot(): return jnp.einsum(equation, left, right, preferred_element_type=jnp.float32)  101 us
    pallas_call x1, Pallas kernels, feed(): pl.pallas_call(functools.partial(feed_kernel, rows=rows), grid=(hidden //...  64.9 us
    ppermute x7, waiting for transfers between devices, swap(): return lax.ppermute(block, 'seq', [(0, 1), (1, 0)])  58 us
    pallas_call x1, Pallas kernels, heads_back(): pl.pallas_call(functools.partial(heads_back_kernel, step=step), grid=(hea...  54.9 us
    all_gather x4, waiting for transfers between devices, gather(): lax.all_gather(join(weight, swap(weight), mine, 1), 'fsdp', axis=0, tiled...  51.1 us
    unnamed x144, local copies, waits for them, and re-layouts  43.4 us
    unnamed x10, other arithmetic  36.9 us
    pallas_call x1, Pallas kernels, heads_forward(): pl.pallas_call(functools.partial(heads_kernel, step=step), grid=(heads,),...  29.6 us
  transfers between devices with their start and end apart: 20, of which 10 were waited for; matrix products, arithmetic and copies ran while one was open for 25% of the time, Pallas kernels for 4%

profile of v1, /device:TPU:0, one launch (start us, length us, event | category | flops | bytes accessed | tf_op | source)
XLA Modules:
  0.0 729.7 jit_solution(18113066259143520497)
XLA Ops:
  10.3 6.4 collective-permute-done.1
  27.1 6.3 collective-permute-done.3
  36.9 6.3 collective-permute-done.4
  44.3 22.3 %all-gather.1 = bf16[16,2,1152]{2,1,0:T(2,128)(2,1)S(1)} all-gather(bf16[1,2,1152]{2,1,0:T(2,128)(2,1)S(1)} %fusion.121), channel_id=1, replica_groups=mesh['fsdp'=16,'seq'=2] {'fsdp'}, dimensions={0}, use_global_device_ids=true | all-gather | bytes 78336 | tf_op jit(solution)/shard_map/all_gather | solution.py:685
  67.2 21.9 %all_to_all.97 = f32[16,2,3456]{2,1,0:T(2,128)S(1)} all-to-all(f32[16,2,3456]{2,1,0:T(2,128)S(1)} %reshape.260), channel_id=1, replica_groups=mesh['fsdp'=16,'seq'=2] {'fsdp'}, dimensions={0} | all-to-all | bytes 884736 | tf_op jit(solution)/shard_map/all_to_all | solution.py:690
  89.3 6.5 all_to_all.98
  107.0 16.4 %all-reduce.3 = s32[16,2]{1,0:T(8,128)} all-reduce(s32[16,2]{1,0:T(8,128)} %reshape.262), channel_id=1, replica_groups=mesh['fsdp'=16,'seq'=2] {'fsdp'}, use_global_device_ids=true, to_apply=%add.2 | all-reduce | flops 32 | bytes 256
  124.3 6.6 collective-permute-done
  132.6 9.5 %all-to-all-start.3 = ((bf16[16,16,1656]{2,1,0:T(8,128)(2,1)}), bf16[16,16,1656]{2,1,0:T(8,128)(2,1)}, u32[]{:S(2)}, u32[]{:S(2)}) async-start(bf16[16,16,1656]{2,1,0:T(8,128)(2,1)} %copy.182), calls=%async_computation.3 | async-start | bytes 1703936 | tf_op jit(solution)/shard_map/all_to_all | solution.py:676
  144.8 19.5 %all-to-all-done.3 = bf16[16,16,1656]{2,1,0:T(8,128)(2,1)} async-done(((bf16[16,16,1656]{2,1,0:T(8,128)(2,1)}), bf16[16,16,1656]{2,1,0:T(8,128)(2,1)}, u32[]{:S(2)}, u32[]{:S(2)}) %all-to-all-start.3) | async-done | bytes 847904 | tf_op jit(solution)/shard_map/all_to_all | solution.py:676
  164.3 5.1 all-to-all-start.4
  181.9 13.7 %all-to-all-done.4 = bf16[2,512,1152]{2,1,0:T(8,128)(2,1)} async-done(((bf16[2,512,1152]{2,1,0:T(8,128)(2,1)}), bf16[2,512,1152]{2,1,0:T(8,128)(2,1)}, u32[]{:S(2)}, u32[]{:S(2)}) %all-to-all-start.4) | async-done | bytes 2359328 | tf_op jit(solution)/shard_map/all_to_all | solution.py:666
  204.8 5.1 concatenate.72.dfinal_ref
  214.2 15.5 %fusion.4 = bf16[3456,1024]{1,0:T(8,128)(2,1)} fusion(bf16[16,3456]{1,0:T(8,128)(2,1)S(1)} %slice-done, bf16[1152,3456]{1,0:T(8,128)(2,1)} %all-gather.7.cloned.1.call-done, bf16[1024,16]{1,0:T(8,128)(2,1)S(1)} %convolution_convert_fusion.7, bf16[1024,1152]{1,0:T(8,128)(2,1)} %copy-done.14), kind=kOutput, calls=%fused_computation.4 | convolution fusion | flops 8291442688 | bytes 17543168 | tf_op jit(solution)/shard_map/ti,io->ot/dot_general | solution.py:615
  229.7 29.6 %heads_forward.1 = (bf16[16,72,1024]{2,1,0:T(8,128)(2,1)S(1)}, f32[16,1,1024]{2,1,0:T(1,128)S(1)}) custom-call(bf16[3,16,72,1024]{3,2,1,0:T(8,128)(2,1)} %bitcast.168), custom_call_target="tpu_custom_call" | custom-call | flops 17179869184 | bytes 11796480 | tf_op jit(solution)/shard_map/heads_forward/pallas_call | solution.py:422
  261.0 5.6 fusion.92
  278.0 51.1 %all-gather.13.cloned.1.call-done.narrow_ref = bf16[4608,1152]{1,0:T(8,128)(2,1)} async-done(((bf16[288,1152]{1,0:T(8,128)(2,1)}), bf16[4608,1152]{1,0:T(8,128)(2,1)}) %all-gather.13.cloned.1.call-update) | async-done | bytes 10616848 | tf_op jit(solution)/shard_map/all_gather | solution.py:656
  329.1 64.9 %feed.1 = (f32[1024,1280]{1,0:T(8,128)}, f32[1024,1280]{1,0:T(8,128)}, f32[16,4608]{1,0:T(8,128)}, f32[16,4608]{1,0:T(8,128)}) custom-call(bf16[1024,1280]{1,0:T(8,128)(2,1)} %concatenate.71.second_ref, bf16[1024,1280]{1,0:T(8,128)(2,1)} %concatenate.72.dfinal_ref, bf16[16,1024]{1,0:T(8,128)(2,1)} %bitcast.157, bf16[16,1024]{1,0:T(8,128)(2,1)} %bitcast.156, ...), custom_call_target="tpu_custom_call" | custom-call | flops 48318382080 | bytes 36962304 | tf_op jit(solution)/shard_map/feed/pallas_call | solution.py:564
  394.1 6.9 multiply_reduce_fusion
  401.0 8.3 %fusion.8 = (bf16[1152]{0:T(1024)(128)(2,1)}, bf16[1,1024,1152]{2,1,0:T(8,128)(2,1)}, bf16[1152]{0:T(1024)(128)(2,1)}, f32[1024,1152]{1,0:T(8,128)S(1)}) fusion(bf16[2,512,1152]{2,1,0:T(8,128)(2,1)} %all-to-all-done.4, f32[1024,1152]{1,0:T(8,128)S(1)} %copy-done.7, f32[1152]{0:T(1024)S(1)} %get-tuple-element.90, f32[1024,1152]{1,0:T(8,128)} %get-tuple-element.124, ...), kind=kOutput, calls=%fused_computation.12 | convolution fusion | flops 58996480 | bytes 28918272 | tf_op jit(solution)/shard_map/tr,ro->to/dot_general | solution.py:615
  418.0 54.9 %heads_back.1 = bf16[3,16,72,1024]{3,2,1,0:T(8,128)(2,1)} custom-call(bf16[3,16,72,1024]{3,2,1,0:T(8,128)(2,1)} %bitcast.169, bf16[16,72,1024]{2,1,0:T(8,128)(2,1)S(1)} %bitcast.136, f32[16,1,1024]{2,1,0:T(1,128)S(1)} %get-tuple-element.19.log_ref), custom_call_target="tpu_custom_call" | custom-call | flops 42949672960 | bytes 18874368 | tf_op jit(solution)/shard_map/heads_back/pallas_call | solution.py:476
  481.7 16.9 %fusion.23 = (bf16[1152]{0:T(1024)(128)(2,1)}, f32[1024]{0:T(1024)}, f32[1024]{0:T(1024)}, bf16[1152]{0:T(1024)(128)(2,1)S(1)}, f32[1024,1152]{1,0:T(8,128)}) fusion(bf16[2,512,1152]{2,1,0:T(8,128)(2,1)S(1)} %copy-done.5, f32[1024]{0:T(1024)S(1)} %bitcast.163, f32[1024]{0:T(1024)S(1)} %bitcast.166, f32[1152]{0:T(1024)S(1)} %copy-done.36, ...), kind=kOutput, calls=%fused_computation.31 | convolution fusion | flops 8166699008 | bytes 26862592 | tf_op jit(solution)/shard_map/ot,io->ti/dot_general | solution.py:615
  522.5 5.9 fusion.24
  532.0 19.7 %all-gather = bf16[1,32,3456]{2,0,1:T(2,128)(2,1)S(1)} all-gather(bf16[1,2,3456]{2,0,1:T(2,128)(2,1)S(1)} %bitcast.158), channel_id=2, replica_groups=mesh['fsdp'=16,'seq'=2] {'fsdp'}, dimensions={1}, use_global_device_ids=true | all-gather | bytes 235008 | tf_op jit(solution)/shard_map/all_gather | solution.py:796
  558.7 7.5 %copy.222 = bf16[1,1024,1152]{2,0,1:T(2,128)(2,1)} copy(bf16[1,1024,1152]{2,1,0:T(8,128)(2,1)} %get-tuple-element.109) | data formatting | bytes 4718592 | tf_op jit(solution)/shard_map/broadcast_in_dim | solution.py:745
  566.2 16.5 %reduce.30 = bf16[1024,1152]{1,0:T(8,128)(2,1)} reduce(bf16[1024,1,1152]{2,1,0:T(2,128)(2,1)} %bitcast.141, bf16[]{:T(256)} %broadcast.151), dimensions={1}, to_apply=%bitcast.132.reduce_sub_computation | reduce | bytes 4718594
  602.3 17.1 %all-to-all-done.5 = bf16[2,2,294912]{2,1,0:T(2,128)(2,1)} async-done(((bf16[2,2,294912]{2,1,0:T(2,128)(2,1)}), bf16[2,2,294912]{2,1,0:T(2,128)(2,1)}, u32[]{:S(2)}, u32[]{:S(2)}) %all-to-all-start.5) | async-done | bytes 2359328 | tf_op jit(solution)/shard_map/all_to_all | solution.py:745
  619.4 5.9 all-to-all-start.9
  625.3 5.7 fusion.22
  631.0 7.5 %copy.221 = bf16[1,1024,1152]{2,0,1:T(2,128)(2,1)} copy(bf16[1,1024,1152]{2,1,0:T(8,128)(2,1)} %bitcast.153) | data formatting | bytes 4718592 | tf_op jit(solution)/shard_map/broadcast_in_dim | solution.py:777
  638.5 15.1 %reduce.31 = bf16[1024,1152]{1,0:T(8,128)(2,1)S(1)} reduce(bf16[1024,1,1152]{2,1,0:T(2,128)(2,1)} %bitcast.140, bf16[]{:T(256)} %broadcast.151), dimensions={1}, to_apply=%bitcast.131.reduce_sub_computation | reduce | bytes 4718594
  664.3 29.4 %collective-permute-done.6 = bf16[4,16,1656]{2,1,0:T(8,128)(2,1)S(1)} collective-permute-done((bf16[4,16,1656]{2,1,0:T(8,128)(2,1)S(1)}, bf16[4,16,1656]{2,1,0:T(8,128)(2,1)S(1)}, u32[]{:S(2)}, u32[]{:S(2)}) %collective-permute-start.6) | collective-permute-done | bytes 212000 | tf_op jit(solution)/shard_map/ppermute | solution.py:619
  (279 shorter events, 182.7 us)
Async XLA Ops:
  7.2 59.5 %copy-start = (bf16[72,3456]{1,0:T(8,128)(2,1)S(1)}, bf16[72,3456]{1,0:T(8,128)(2,1)}, u32[]{:S(2)}) copy-start(bf16[72,3456]{1,0:T(8,128)(2,1)} %param.23) | copy-start | bytes 1492996
  7.2 207.0 %all-gather.7.cloned.1.call-start = ((), (), s32[]{:S(2)}) async-start(), calls=%async_computation.11 | async-start | bytes 8460288 | tf_op jit(solution)/shard_map/all_gather | solution.py:656
  7.2 9.5 %collective-permute-start.1 = (bf16[72,1728]{1,0:T(8,128)(2,1)}, bf16[72,1728]{1,0:T(8,128)(2,1)S(1)}, u32[]{:S(2)}, u32[]{:S(2)}) collective-permute-start(bf16[72,1728]{1,0:T(8,128)(2,1)} %param.25), channel_id=1, source_target_pairs={{0,1},{1,0},{2,3},{3,2},{4,5},{5,4},{6,7},{7,6},{8,9},{9,8},{10,11... | collective-permute-start | bytes 746504 | tf_op jit(solution)/shard_map/ppermute | solution.py:619
  18.7 242.3 %all-gather.9.cloned.1.call-start = ((), (), s32[]{:S(2)}) async-start(), calls=%async_computation.12 | async-start | bytes 2820096 | tf_op jit(solution)/shard_map/all_gather | solution.py:656
  18.7 4.8 collective-permute-start.2
  25.2 252.8 %all-gather.11.cloned.1.call-start = ((), (), s32[]{:S(2)}) async-start(), calls=%async_computation.13 | async-start | bytes 11280384 | tf_op jit(solution)/shard_map/all_gather | solution.py:656
  25.3 8.1 %collective-permute-start.3 = (bf16[72,2304]{1,0:T(8,128)(2,1)}, bf16[72,2304]{1,0:T(8,128)(2,1)S(1)}, u32[]{:S(2)}, u32[]{:S(2)}) collective-permute-start(bf16[72,2304]{1,0:T(8,128)(2,1)} %param.28), channel_id=1, source_target_pairs={{0,1},{1,0},{2,3},{3,2},{4,5},{5,4},{6,7},{7,6},{8,9},{9,8},{10,11... | collective-permute-start | bytes 995336 | tf_op jit(solution)/shard_map/ppermute | solution.py:619
  35.3 293.8 %all-gather.13.cloned.1.call-start = ((), (), s32[]{:S(2)}) async-start(), calls=%async_computation.14 | async-start | bytes 11280384 | tf_op jit(solution)/shard_map/all_gather | solution.py:656
  35.4 7.8 %collective-permute-start.4 = (bf16[288,576]{1,0:T(8,128)(2,1)S(1)}, bf16[288,576]{1,0:T(8,128)(2,1)S(1)}, u32[]{:S(2)}, u32[]{:S(2)}) collective-permute-start(bf16[288,576]{1,0:T(8,128)(2,1)S(1)} %copy-done.24), channel_id=1, source_target_pairs={{0,1},{1,0},{2,3},{3,2},{4,5},{5,4},{6,7},{7,6},{8,9},{9,8},{10,11... | collective-permute-start | bytes 995336 | tf_op jit(solution)/shard_map/ppermute | solution.py:619
  44.3 55.3 %copy-start.19 = (f32[4,16,1080]{2,1,0:T(8,128)S(1)}, f32[4,16,1080]{2,1,0:T(8,128)}, u32[]{:S(2)}) copy-start(f32[4,16,1080]{2,1,0:T(8,128)} %param.33) | copy-start | bytes 829444
  44.3 55.4 %copy-start.21 = (f32[4,16,576]{2,1,0:T(8,128)S(1)}, f32[4,16,576]{2,1,0:T(8,128)}, u32[]{:S(2)}) copy-start(f32[4,16,576]{2,1,0:T(8,128)} %param.32) | copy-start | bytes 442372
  95.8 36.8 %all-to-all-start = ((bf16[2,512,1152]{2,1,0:T(8,128)(2,1)}), bf16[2,512,1152]{2,1,0:T(8,128)(2,1)S(1)}, u32[]{:S(2)}, u32[]{:S(2)}) async-start(bf16[2,512,1152]{2,1,0:T(8,128)(2,1)} %param.19), calls=%async_computation | async-start | bytes 4718592 | tf_op jit(solution)/shard_map/all_to_all | solution.py:665
  100.0 30.9 %collective-permute-start = (bf16[4,16,1656]{2,0,1:T(4,128)(2,1)S(1)}, bf16[4,16,1656]{2,0,1:T(4,128)(2,1)S(1)}, u32[]{:S(2)}, u32[]{:S(2)}) collective-permute-start(bf16[4,16,1656]{2,0,1:T(4,128)(2,1)S(1)} %pad_maximum_fusion.3), channel_id=1, source_target_pairs={{0,1},{1,0},{2,3},{3,2},{4,5},{5,4},{6,7},{7,6},{8,9},{9,8},{10,11... | collective-permute-start | bytes 635912 | tf_op jit(solution)/shard_map/ppermute | solution.py:619
  132.6 77.4 %copy-start.3 = (bf16[2,512,1152]{2,1,0:T(8,128)(2,1)}, bf16[2,512,1152]{2,1,0:T(8,128)(2,1)S(1)}, u32[]{:S(2)}) copy-start(bf16[2,512,1152]{2,1,0:T(8,128)(2,1)S(1)} %all-to-all-done) | copy-start | bytes 7077892
  132.6 31.6 %all-to-all-start.3 = ((bf16[16,16,1656]{2,1,0:T(8,128)(2,1)}), bf16[16,16,1656]{2,1,0:T(8,128)(2,1)}, u32[]{:S(2)}, u32[]{:S(2)}) async-start(bf16[16,16,1656]{2,1,0:T(8,128)(2,1)} %copy.182), calls=%async_computation.3 | async-start | bytes 1703936 | tf_op jit(solution)/shard_map/all_to_all | solution.py:676
  144.8 65.2 %copy-start.39 = (f32[1,4,2,128]{3,1,2,0:T(4,128)}, f32[1,4,2,128]{3,1,2,0:T(4,128)S(1)}, u32[]{:S(2)}) copy-start(f32[1,4,2,128]{3,1,2,0:T(4,128)S(1)} %copy.204) | copy-start | bytes 12292
  144.8 65.2 %copy-start.41 = (f32[1,4,2,128]{3,1,2,0:T(4,128)}, f32[1,4,2,128]{3,1,2,0:T(4,128)S(1)}, u32[]{:S(2)}) copy-start(f32[1,4,2,128]{3,1,2,0:T(4,128)S(1)} %copy.203) | copy-start | bytes 12292
  164.3 31.4 %all-to-all-start.4 = ((bf16[2,512,1152]{2,1,0:T(8,128)(2,1)}), bf16[2,512,1152]{2,1,0:T(8,128)(2,1)}, u32[]{:S(2)}, u32[]{:S(2)}) async-start(bf16[2,512,1152]{2,1,0:T(8,128)(2,1)} %param.22), calls=%async_computation.4 | async-start | bytes 4718592 | tf_op jit(solution)/shard_map/all_to_all | solution.py:666
  272.4 121.6 %copy-start.10 = (bf16[1024,1152]{1,0:T(8,128)(2,1)}, bf16[1024,1152]{1,0:T(8,128)(2,1)S(1)}, u32[]{:S(2)}) copy-start(bf16[1024,1152]{1,0:T(8,128)(2,1)S(1)} %add_convert_fusion.2) | copy-start | bytes 7077892
  274.3 54.8 %copy-start.32 = (bf16[1024,16]{0,1:T(8,128)(2,1)}, bf16[1024,16]{0,1:T(8,128)(2,1)S(1)}, u32[]{:S(2)}) copy-start(bf16[1024,16]{0,1:T(8,128)(2,1)S(1)} %convolution_convert_fusion.11) | copy-start | bytes 98308
  515.4 15.7 %all-to-all-start.7 = ((bf16[2,2,1728]{2,1,0:T(2,128)(2,1)}), bf16[2,2,1728]{2,1,0:T(2,128)(2,1)}, u32[]{:S(2)}, u32[]{:S(2)}) async-start(bf16[2,2,1728]{2,1,0:T(2,128)(2,1)} %reshape.309), calls=%async_computation.7 | async-start | bytes 28672 | tf_op jit(solution)/shard_map/all_to_all | solution.py:795
  552.5 33.2 %all-to-all-start.8 = ((f32[16,2,72]{2,1,0:T(2,128)}), f32[16,2,72]{2,1,0:T(2,128)S(1)}, u32[]{:S(2)}, u32[]{:S(2)}) async-start(f32[16,2,72]{2,1,0:T(2,128)} %bitcast.21), calls=%async_computation.8 | async-start | bytes 32768 | tf_op jit(solution)/shard_map/all_to_all | solution.py:798
  585.7 33.6 %all-to-all-start.5 = ((bf16[2,2,294912]{2,1,0:T(2,128)(2,1)}), bf16[2,2,294912]{2,1,0:T(2,128)(2,1)}, u32[]{:S(2)}, u32[]{:S(2)}) async-start(bf16[2,2,294912]{2,1,0:T(2,128)(2,1)} %reshape.307), calls=%async_computation.5 | async-start | bytes 4718592 | tf_op jit(solution)/shard_map/all_to_all | solution.py:745
  593.0 32.2 %copy-start.54 = (f32[1024]{0:T(1024)S(1)}, f32[1024]{0:T(1024)}, u32[]{:S(2)}) copy-start(f32[1024]{0:T(1024)} %get-tuple-element.85) | copy-start | bytes 12292
  593.1 32.2 %copy-start.55 = (f32[1024]{0:T(1024)S(1)}, f32[1024]{0:T(1024)}, u32[]{:S(2)}) copy-start(f32[1024]{0:T(1024)} %get-tuple-element.86) | copy-start | bytes 12292
  593.1 32.2 %copy-start.43 = (f32[1,4,2,128]{3,1,2,0:T(4,128)S(1)}, f32[1,4,2,128]{3,1,2,0:T(4,128)}, u32[]{:S(2)}) copy-start(f32[1,4,2,128]{3,1,2,0:T(4,128)} %copy-done.41) | copy-start | bytes 12292
  619.4 37.2 %all-to-all-start.9 = ((bf16[16,16,1656]{2,1,0:T(8,128)(2,1)}), bf16[16,16,1656]{2,1,0:T(8,128)(2,1)}, u32[]{:S(2)}, u32[]{:S(2)}) async-start(bf16[16,16,1656]{2,1,0:T(8,128)(2,1)} %copy.191), calls=%async_computation.9 | async-start | bytes 1703936 | tf_op jit(solution)/shard_map/all_to_all | solution.py:810
  656.5 43.9 %copy-start.34 = (f32[2,1152]{1,0:T(2,128)S(1)}, f32[2,1152]{1,0:T(2,128)}, u32[]{:S(2)}) copy-start(f32[2,1152]{1,0:T(2,128)} %param.20) | copy-start | bytes 27652
  656.6 37.7 %all-to-all-start.6 = ((bf16[2,2,294912]{2,1,0:T(2,128)(2,1)}), bf16[2,2,294912]{2,1,0:T(2,128)(2,1)S(1)}, u32[]{:S(2)}, u32[]{:S(2)}) async-start(bf16[2,2,294912]{2,1,0:T(2,128)(2,1)} %reshape.305), calls=%async_computation.6 | async-start | bytes 4718592 | tf_op jit(solution)/shard_map/all_to_all | solution.py:776
  660.5 39.8 %collective-permute-start.5 = (f32[2,1152]{1,0:T(2,128)S(1)}, f32[2,1152]{1,0:T(2,128)S(1)}, u32[]{:S(2)}, u32[]{:S(2)}) collective-permute-start(f32[2,1152]{1,0:T(2,128)S(1)} %select_add_fusion), channel_id=1, source_target_pairs={{0,1},{1,0},{2,3},{3,2},{4,5},{5,4},{6,7},{7,6},{8,9},{9,8},{10,11... | collective-permute-start | bytes 27656 | tf_op jit(solution)/shard_map/ppermute | solution.py:619
  664.1 29.5 %collective-permute-start.6 = (bf16[4,16,1656]{2,1,0:T(8,128)(2,1)S(1)}, bf16[4,16,1656]{2,1,0:T(8,128)(2,1)S(1)}, u32[]{:S(2)}, u32[]{:S(2)}) collective-permute-start(bf16[4,16,1656]{2,1,0:T(8,128)(2,1)S(1)} %copy.215), channel_id=1, source_target_pairs={{0,1},{1,0},{2,3},{3,2},{4,5},{5,4},{6,7},{7,6},{8,9},{9,8},{10,11... | collective-permute-start | bytes 635912 | tf_op jit(solution)/shard_map/ppermute | solution.py:619
  695.6 22.6 %all-to-all-start.10 = ((f32[32,1,128]{2,1,0:T(1,128)}), f32[32,1,128]{2,1,0:T(1,128)S(1)}, u32[]{:S(2)}, u32[]{:S(2)}) async-start(f32[32,1,128]{2,1,0:T(1,128)} %broadcast_in_dim.62), calls=%async_computation.10 | async-start | bytes 32768 | tf_op jit(solution)/shard_map/all_to_all | solution.py:820
  (47 other events, 454.4 us)
Sparse Core Ops, SparseCore 0:
  18.8 80.7 all-gather.6
  102.3 42.6 all-gather.8
  147.3 92.7 all-gather.10
  242.2 86.8 all-gather.12

commit v2 on v0

--- a/solution.py
+++ b/solution.py
@@ -1,6 +1,10 @@
+import functools
+
 import jax
 import jax.numpy as jnp
 from jax import lax
+from jax.experimental import pallas as pl
+from jax.experimental.pallas import tpu as pltpu
 from jax.sharding import PartitionSpec as P
 
 MODEL_WIDTH = 1152
@@ -381,6 +385,1219 @@
     )
 
 
+HEADS = 16
+LOG2E = 1.4426950408889634
+SCORE_SCALE = HD ** (-0.5)
+
+
+def tn(left, right):
+    return lax.dot_general(left, right, (((0,), (0,)), ((), ())), preferred_element_type=jnp.float32)
+
+
+def nn(left, right):
+    return lax.dot_general(left, right, (((1,), (0,)), ((), ())), preferred_element_type=jnp.float32)
+
+
+def nt(left, right):
+    return lax.dot_general(left, right, (((1,), (1,)), ((), ())), preferred_element_type=jnp.float32)
+
+
+def heads_kernel(qkv_ref, mixed_ref, log_ref, *, step):
+    length = qkv_ref.shape[-1]
+    keys = qkv_ref[1, 0].astype(jnp.float32).T.astype(jnp.bfloat16)
+    values_t = qkv_ref[2, 0]
+    for start in range(0, length, step):
+        queries_t = qkv_ref[0, 0, :, start : start + step]
+        scores = nn(keys, queries_t) * (SCORE_SCALE * LOG2E)
+        top = jnp.max(scores, axis=0, keepdims=True)
+        exponent = jnp.exp2(scores - top)
+        total = jnp.sum(exponent, axis=0, keepdims=True)
+        weights = (exponent * (1.0 / total)).astype(jnp.bfloat16)
+        mixed_ref[0, :, start : start + step] = nn(values_t, weights).astype(jnp.bfloat16)
+        log_ref[0, :, start : start + step] = top + jnp.log2(total)
+
+
+def heads_forward(qkv, step=256):
+    _, heads, width, length = qkv.shape
+    return pl.pallas_call(
+        functools.partial(heads_kernel, step=step),
+        grid=(heads,),
+        in_specs=[pl.BlockSpec((3, 1, width, length), lambda h: (0, h, 0, 0))],
+        out_specs=[
+            pl.BlockSpec((1, width, length), lambda h: (h, 0, 0)),
+            pl.BlockSpec((1, 1, length), lambda h: (h, 0, 0)),
+        ],
+        out_shape=[
+            jax.ShapeDtypeStruct((heads, width, length), jnp.bfloat16),
+            jax.ShapeDtypeStruct((heads, 1, length), jnp.float32),
+        ],
+        cost_estimate=pl.CostEstimate(
+            flops=4 * heads * length * length * 256,
+            bytes_accessed=10 * heads * width * length,
+            transcendentals=heads * length * length,
+        ),
+        compiler_params=pltpu.CompilerParams(vmem_limit_bytes=48 * 1024 * 1024),
+        name="heads_forward",
+    )(qkv)
+
+
+def heads_back_kernel(qkv_ref, grad_ref, log_ref, out_ref, key_acc, value_acc, *, step):
+    length = qkv_ref.shape[-1]
+    keys_t = qkv_ref[1, 0]
+    keys = keys_t.astype(jnp.float32).T.astype(jnp.bfloat16)
+    values = qkv_ref[2, 0].astype(jnp.float32).T.astype(jnp.bfloat16)
+    for start in range(0, length, step):
+        queries_t = qkv_ref[0, 0, :, start : start + step]
+        grad_t = grad_ref[0, :, start : start + step]
+        queries = queries_t.astype(jnp.float32).T.astype(jnp.bfloat16)
+        grad = grad_t.astype(jnp.float32).T.astype(jnp.bfloat16)
+        scores = nn(keys, queries_t) * (SCORE_SCALE * LOG2E)
+        probable = jnp.exp2(scores - log_ref[0, :, start : start + step])
+        d_weights = nn(values, grad_t)
+        inner_sum = jnp.sum(d_weights * probable, axis=0, keepdims=True)
+        d_scores = (probable * (d_weights - inner_sum)).astype(jnp.bfloat16)
+        d_values = nn(probable.astype(jnp.bfloat16), grad)
+        d_keys = nn(d_scores, queries)
+        if start == 0:
+            value_acc[...] = d_values
+            key_acc[...] = d_keys
+        else:
+            value_acc[...] += d_values
+            key_acc[...] += d_keys
+        out_ref[0, 0, :, start : start + step] = (nn(keys_t, d_scores) * SCORE_SCALE).astype(
+            jnp.bfloat16
+        )
+    out_ref[1, 0] = (key_acc[...] * SCORE_SCALE).T.astype(jnp.bfloat16)
+    out_ref[2, 0] = value_acc[...].T.astype(jnp.bfloat16)
+
+
+def heads_back(qkv, grad, log_total, step=256):
+    _, heads, width, length = qkv.shape
+    return pl.pallas_call(
+        functools.partial(heads_back_kernel, step=step),
+        grid=(heads,),
+        in_specs=[
+            pl.BlockSpec((3, 1, width, length), lambda h: (0, h, 0, 0)),
+            pl.BlockSpec((1, width, length), lambda h: (h, 0, 0)),
+            pl.BlockSpec((1, 1, length), lambda h: (h, 0, 0)),
+        ],
+        out_specs=pl.BlockSpec((3, 1, width, length), lambda h: (0, h, 0, 0)),
+        out_shape=jax.ShapeDtypeStruct((3, heads, width, length), jnp.bfloat16),
+        scratch_shapes=[
+            pltpu.VMEM((length, width), jnp.float32),
+            pltpu.VMEM((length, width), jnp.float32),
+        ],
+        cost_estimate=pl.CostEstimate(
+            flops=10 * heads * length * length * 256,
+            bytes_accessed=16 * heads * width * length,
+            transcendentals=heads * length * length,
+        ),
+        compiler_params=pltpu.CompilerParams(vmem_limit_bytes=48 * 1024 * 1024),
+        name="heads_back",
+    )(qkv, grad, log_total)
+
+
+RANK = ADAPTER_RANK
+LANES = 128
+PADDED = MODEL_WIDTH + LANES
+HALF = MODEL_WIDTH // 2
+MIB = 1024 * 1024
+
+
+def transposed(block):
+    return block.astype(jnp.float32).T
+
+
+def once(shape):
+    return pl.BlockSpec(shape, lambda *_: (0,) * len(shape), pipeline_mode=pl.Buffered(1))
+
+
+def rows_of(shape, axis):
+    return pl.BlockSpec(shape, lambda i: tuple(i if a == axis else 0 for a in range(len(shape))))
+
+
+def standard(stream):
+    center = stream - jnp.mean(stream, -1, keepdims=True)
+    inverse = lax.rsqrt(jnp.mean(center * center, -1, keepdims=True) + norm_eps)
+    return (center * inverse, inverse)
+
+
+def assemble_kernel(
+    place_ref, near_ref, far_ref, next_near_ref, next_far_ref, out_ref, sems, *, late_x
+):
+    z, x, core, y = (place_ref[i] for i in range(4))
+    depth = out_ref.shape[1]
+    copies = []
+    for side, pair in enumerate(((near_ref, far_ref), (next_near_ref, next_far_ref))):
+        source = core if side == 0 else 1 - core
+        for stage, ref in enumerate(pair):
+            for hop in range(2):
+                by_x = stage if late_x else jnp.where(source == 0, hop, stage)
+                by_y = hop + stage - by_x
+                for shift in range(depth):
+                    target = out_ref.at[
+                        lax.rem(y + by_y, 2),
+                        lax.rem(z + depth - shift, depth),
+                        lax.rem(x + by_x, 2),
+                        source,
+                    ]
+                    block = ref.at[shift, hop] if late_x else ref.at[hop, shift]
+                    copy = pltpu.make_async_copy(block, target, sems.at[len(copies)])
+                    copy.start()
+                    copies.append(copy)
+    for copy in copies:
+        copy.wait()
+
+
+def assemble(place, near, far, next_near, next_far, late_x):
+    rows, columns = near.shape[2:]
+    depth = near.shape[0] * near.shape[1] // 2
+    return pl.pallas_call(
+        functools.partial(assemble_kernel, late_x=late_x),
+        in_specs=[pl.BlockSpec(memory_space=pltpu.SMEM)]
+        + [pl.BlockSpec(memory_space=pltpu.VMEM)] * 4,
+        out_specs=pl.BlockSpec(memory_space=pl.ANY),
+        out_shape=jax.ShapeDtypeStruct((2, depth, 2, 2, rows, columns), near.dtype),
+        scratch_shapes=[pltpu.SemaphoreType.DMA((8 * depth,))],
+        cost_estimate=pl.CostEstimate(
+            flops=0, bytes_accessed=16 * near.size, transcendentals=0
+        ),
+        compiler_params=pltpu.CompilerParams(vmem_limit_bytes=32 * MIB),
+        name="assemble",
+    )(place, near, far, next_near, next_far)
+
+
+def entry_kernel(
+    token_ref, mod_ref, weight_ref, up_ref, down_ref, hidden_ref, middle_ref, qkv_ref, weight_aug
+):
+    half = 3 * HALF
+
+    @pl.when(pl.program_id(0) == 0)
+    def _():
+        weight_aug[:MODEL_WIDTH, :half] = weight_ref[0, :, HALF:]
+        weight_aug[:MODEL_WIDTH, half:] = weight_ref[1, :, HALF:]
+        weight_aug[MODEL_WIDTH:, :] = up_ref[...]
+
+    normed, _ = standard(token_ref[...].astype(jnp.float32))
+    hidden = (normed * (1.0 + mod_ref[1:2]) + mod_ref[0:1]).astype(jnp.bfloat16)
+    middle = nt(hidden, down_ref[...]).astype(jnp.bfloat16)
+    hidden_ref[...] = hidden
+    middle_ref[...] = middle
+    joined = jnp.concatenate([hidden, middle], 1)
+    for part in range(3):
+        columns = slice(part * MODEL_WIDTH, (part + 1) * MODEL_WIDTH)
+        packed = nn(joined, weight_aug[:, columns])
+        qkv_ref[part] = packed.T.reshape(qkv_ref.shape[1:]).astype(jnp.bfloat16)
+
+
+def entry(tokens, mods, weight, up, down, tile=256):
+    length = tokens.shape[0]
+    bf16 = jnp.bfloat16
+    return pl.pallas_call(
+        entry_kernel,
+        grid=(length // tile,),
+        in_specs=[
+            rows_of((tile, MODEL_WIDTH), 0),
+            once(mods.shape),
+            once(weight.shape),
+            once(up.shape),
+            once(down.shape),
+        ],
+        out_specs=[
+            rows_of((tile, MODEL_WIDTH), 0),
+            rows_of((tile, LANES), 0),
+            rows_of((3, HEADS, HD, tile), 3),
+        ],
+        out_shape=[
+            jax.ShapeDtypeStruct((length, MODEL_WIDTH), bf16),
+            jax.ShapeDtypeStruct((length, LANES), bf16),
+            jax.ShapeDtypeStruct((3, HEADS, HD, length), bf16),
+        ],
+        scratch_shapes=[pltpu.VMEM((PADDED, 3 * MODEL_WIDTH), bf16)],
+        cost_estimate=pl.CostEstimate(
+            flops=6 * length * MODEL_WIDTH * PADDED,
+            bytes_accessed=2 * weight.size + 12 * length * MODEL_WIDTH,
+            transcendentals=0,
+        ),
+        compiler_params=pltpu.CompilerParams(vmem_limit_bytes=56 * MIB),
+        name="entry",
+    )(tokens, mods, weight, up, down)
+
+
+def load_proj(proj_aug, weight_ref, up_ref):
+    @pl.when(pl.program_id(0) == 0)
+    def _():
+        proj_aug[:MODEL_WIDTH, :HALF] = weight_ref[0, :, :HALF]
+        proj_aug[:MODEL_WIDTH, HALF:] = weight_ref[1, :, :HALF]
+        proj_aug[MODEL_WIDTH:, :] = up_ref[...]
+
+
+def before_kernel(
+    mixed_ref,
+    token_ref,
+    cot_ref,
+    mod_ref,
+    weight_ref,
+    up_proj_ref,
+    down_proj_ref,
+    down_expand_ref,
+    up_shrink_ref,
+    bias_ref,
+    second_ref,
+    dfinal_ref,
+    branch_ref,
+    middle_ref,
+    proj_aug,
+):
+    bf16 = jnp.bfloat16
+    load_proj(proj_aug, weight_ref, up_proj_ref)
+    mixed = transposed(mixed_ref[...]).astype(bf16)
+    middle_proj = nt(mixed, down_proj_ref[...])
+    branch = nn(jnp.concatenate([mixed, middle_proj.astype(bf16)], 1), proj_aug[...])
+    branch = branch + bias_ref[...]
+    branch_ref[...] = branch
+    residual = token_ref[...].astype(jnp.float32) + mod_ref[2:3] * branch
+    normed, _ = standard(residual)
+    second = (normed * (1.0 + mod_ref[4:5]) + mod_ref[3:4]).astype(bf16)
+    middle_expand = nt(second, down_expand_ref[...])
+    second_ref[:, :MODEL_WIDTH] = second
+    second_ref[:, MODEL_WIDTH:] = middle_expand.astype(bf16)
+    d_final = (mod_ref[5:6] * cot_ref[...].astype(jnp.float32)).astype(bf16)
+    dmiddle_shrink = nt(d_final, up_shrink_ref[...])
+    dfinal_ref[:, :MODEL_WIDTH] = d_final
+    dfinal_ref[:, MODEL_WIDTH:] = dmiddle_shrink.astype(bf16)
+    middle_ref[0] = middle_proj.T[:RANK].astype(bf16)
+    middle_ref[1] = middle_expand.T[:RANK].astype(bf16)
+    middle_ref[2] = dmiddle_shrink.T[:RANK].astype(bf16)
+
+
+def before_feed(
+    mixed, tokens, cotangent, mods, weight, up_proj, down_proj, down_expand, up_shrink, bias, tile=256
+):
+    length = tokens.shape[0]
+    bf16 = jnp.bfloat16
+    return pl.pallas_call(
+        before_kernel,
+        grid=(length // tile,),
+        in_specs=[
+            rows_of((MODEL_WIDTH, tile), 1),
+            rows_of((tile, MODEL_WIDTH), 0),
+            rows_of((tile, MODEL_WIDTH), 0),
+            once(mods.shape),
+            once((2, MODEL_WIDTH, 5 * LANES)),
+            once(up_proj.shape),
+            once(down_proj.shape),
+            once(down_expand.shape),
+            once(up_shrink.shape),
+            once(bias.shape),
+        ],
+        out_specs=[
+            rows_of((tile, PADDED), 0),
+            rows_of((tile, PADDED), 0),
+            rows_of((tile, MODEL_WIDTH), 0),
+            rows_of((3, RANK, tile), 2),
+        ],
+        out_shape=[
+            jax.ShapeDtypeStruct((length, PADDED), bf16),
+            jax.ShapeDtypeStruct((length, PADDED), bf16),
+            jax.ShapeDtypeStruct((length, MODEL_WIDTH), jnp.float32),
+            jax.ShapeDtypeStruct((3, RANK, length), bf16),
+        ],
+        scratch_shapes=[pltpu.VMEM((PADDED, MODEL_WIDTH), bf16)],
+        cost_estimate=pl.CostEstimate(
+            flops=4 * length * MODEL_WIDTH * PADDED,
+            bytes_accessed=16 * length * MODEL_WIDTH,
+            transcendentals=0,
+        ),
+        compiler_params=pltpu.CompilerParams(vmem_limit_bytes=48 * MIB),
+        name="before_feed",
+    )(mixed, tokens, cotangent, mods, weight, up_proj, down_proj, down_expand, up_shrink, bias)
+
+
+GELU_RATE = 0.7978845608
+GELU_CUBE = 0.044715
+
+
+def gelu_pair(inner, d_active):
+    square = inner * inner
+    tanh = jnp.tanh(inner * (GELU_RATE + (GELU_RATE * GELU_CUBE) * square))
+    half = 0.5 + 0.5 * tanh
+    slope = half + inner * (half * (1.0 - tanh)) * (
+        GELU_RATE + (3.0 * GELU_CUBE * GELU_RATE) * square
+    )
+    return (inner * half).astype(jnp.bfloat16), (d_active * slope).astype(jnp.bfloat16)
+
+
+def feed_kernel(
+    second_ref, dfinal_ref, middle_ref, weight_ref, up_ref, down_ref, bias_ref,
+    final_in_ref, dsecond_in_ref, final_ref, dsecond_ref, up_grad_ref, down_grad_ref,
+    widen_aug, narrow_aug, *, rows, first, sub,
+):
+    width = MODEL_WIDTH
+    chunks = weight_ref.shape[-1] // width
+    for chunk in range(chunks):
+        for side in range(2):
+            part = slice(chunk * width + side * HALF, chunk * width + (side + 1) * HALF)
+            widen_aug[:width, part] = weight_ref[side, :, chunk * width : chunk * width + HALF]
+            narrow_aug[chunk * width : (chunk + 1) * width, side * HALF : (side + 1) * HALF] = weight_ref[side, :, chunk * width + HALF : (chunk + 1) * width]
+    widen_aug[width:, :] = up_ref[...]
+    narrow_aug[:, width:] = down_ref[...]
+    length = second_ref.shape[0]
+    for index in range(chunks * width // sub):
+        cols = slice(index * sub, (index + 1) * sub)
+        for start in range(0, length, rows):
+            at = slice(start, start + rows)
+            inner = nn(second_ref[at, :], widen_aug[:, cols]) + bias_ref[:, cols]
+            active, d_inner = gelu_pair(inner, nt(dfinal_ref[at, :], narrow_aug[cols, :]))
+            final = nn(active, narrow_aug[cols, :])
+            dsecond = nt(d_inner, widen_aug[:, cols])
+            if index == 0 and first:
+                final_ref[at, :] = final
+                dsecond_ref[at, :] = dsecond
+            elif index == 0:
+                final_ref[at, :] = final_in_ref[at, :] + final
+                dsecond_ref[at, :] = dsecond_in_ref[at, :] + dsecond
+            else:
+                final_ref[at, :] += final
+                dsecond_ref[at, :] += dsecond
+            up_grad = nn(middle_ref[1, :, at], d_inner)
+            down_grad = nn(middle_ref[2, :, at], active)
+            if start == 0:
+                up_grad_ref[:, cols] = up_grad
+                down_grad_ref[:, cols] = down_grad
+            else:
+                up_grad_ref[:, cols] += up_grad
+                down_grad_ref[:, cols] += down_grad
+
+
+def feed(second, dfinal, middles, weight, up, down, bias, sums, rows=1024, sub=768):
+    length, padded = second.shape
+    hidden = weight.shape[-1]
+    first = sums is None
+    if first:
+        sums = (jnp.zeros((8, LANES), jnp.float32),) * 2
+    return pl.pallas_call(
+        functools.partial(feed_kernel, rows=rows, first=first, sub=sub),
+        grid=(1,),
+        in_specs=[
+            once((length, padded)), once((length, padded)), once(middles.shape),
+            once(weight.shape), once(up.shape), once(down.shape), once(bias.shape),
+            once(sums[0].shape), once(sums[1].shape),
+        ],
+        out_specs=[once((length, padded)), once((length, padded)), once((RANK, hidden)), once((RANK, hidden))],
+        out_shape=[
+            jax.ShapeDtypeStruct((length, padded), jnp.float32),
+            jax.ShapeDtypeStruct((length, padded), jnp.float32),
+            jax.ShapeDtypeStruct((RANK, hidden), jnp.float32),
+            jax.ShapeDtypeStruct((RANK, hidden), jnp.float32),
+        ],
+        scratch_shapes=[pltpu.VMEM((padded, hidden), jnp.bfloat16), pltpu.VMEM((hidden, padded), jnp.bfloat16)],
+        input_output_aliases={} if first else {7: 0, 8: 1},
+        cost_estimate=pl.CostEstimate(
+            flops=8 * length * padded * hidden,
+            bytes_accessed=2 * weight.size + 12 * length * padded,
+            transcendentals=length * hidden,
+        ),
+        compiler_params=pltpu.CompilerParams(vmem_limit_bytes=63 * MIB),
+        name="feed",
+    )(second, dfinal, middles, weight, up, down, bias, *sums)
+
+
+def back_through(gradient, normed, inverse):
+    return inverse * (
+        gradient
+        - jnp.mean(gradient, -1, keepdims=True)
+        - normed * jnp.mean(gradient * normed, -1, keepdims=True)
+    )
+
+
+def total(values):
+    return jnp.sum(values, axis=0, keepdims=True)
+
+
+def after_kernel(
+    final_ref,
+    dsecond_ref,
+    token_ref,
+    cot_ref,
+    branch_ref,
+    second_ref,
+    dfinal_ref,
+    mixed_ref,
+    middle_ref,
+    mod_ref,
+    weight_ref,
+    up_proj_ref,
+    down_proj_ref,
+    down_expand_ref,
+    up_shrink_ref,
+    bias_ref,
+    block_ref,
+    dresidual_ref,
+    dmixed_ref,
+    sums_ref,
+    up_shrink_grad,
+    down_expand_grad,
+    up_proj_grad,
+    down_proj_grad,
+    proj_aug,
+):
+    bf16 = jnp.bfloat16
+    load_proj(proj_aug, weight_ref, up_proj_ref)
+    cot = cot_ref[...].astype(jnp.float32)
+    branch = branch_ref[...]
+    residual = token_ref[...].astype(jnp.float32) + mod_ref[2:3] * branch
+    normed, inverse = standard(residual)
+    middle_shrink = final_ref[:, MODEL_WIDTH:]
+    final = final_ref[:, :MODEL_WIDTH] + bias_ref[...]
+    final = final + nn(middle_shrink.astype(bf16), up_shrink_ref[...])
+    block_ref[...] = (residual + mod_ref[5:6] * final).astype(bf16)
+    dmiddle_expand = dsecond_ref[:, MODEL_WIDTH:]
+    d_second = dsecond_ref[:, :MODEL_WIDTH] + nn(dmiddle_expand.astype(bf16), down_expand_ref[...])
+    d_residual = cot + back_through(d_second * (1.0 + mod_ref[4:5]), normed, inverse)
+    dresidual_ref[...] = d_residual
+    d_branch = (mod_ref[2:3] * d_residual).astype(bf16)
+    joined = nt(d_branch, proj_aug[...])
+    dmiddle_proj = joined[:, MODEL_WIDTH:].astype(bf16)
+    d_mixed = joined[:, :MODEL_WIDTH] + nn(dmiddle_proj, down_proj_ref[...])
+    dmixed_ref[...] = d_mixed.T.astype(bf16)
+    sums = jnp.concatenate(
+        [
+            total(d_residual * branch),
+            total(d_second),
+            total(d_second * normed),
+            total(cot * final),
+            jnp.zeros((4, MODEL_WIDTH), jnp.float32),
+        ],
+        0,
+    )
+    grads = (
+        nn(middle_shrink.T[:RANK].astype(bf16), dfinal_ref[...]),
+        nn(dmiddle_expand.T[:RANK].astype(bf16), second_ref[...]),
+        nn(middle_ref[0], d_branch),
+        nn(mixed_ref[...], dmiddle_proj),
+    )
+    refs = (up_shrink_grad, down_expand_grad, up_proj_grad, down_proj_grad)
+
+    @pl.when(pl.program_id(0) == 0)
+    def _():
+        sums_ref[...] = sums
+        for ref, grad in zip(refs, grads):
+            ref[...] = grad
+
+    @pl.when(pl.program_id(0) > 0)
+    def _():
+        sums_ref[...] += sums
+        for ref, grad in zip(refs, grads):
+            ref[...] += grad
+
+
+def after_feed(
+    final,
+    dsecond,
+    tokens,
+    cotangent,
+    branch,
+    second,
+    dfinal,
+    mixed,
+    middles,
+    mods,
+    weight,
+    up_proj,
+    down_proj,
+    down_expand,
+    up_shrink,
+    bias,
+    tile=256,
+):
+    length = tokens.shape[0]
+    bf16, f32 = jnp.bfloat16, jnp.float32
+    low_rank = jax.ShapeDtypeStruct((RANK, MODEL_WIDTH), f32)
+    return pl.pallas_call(
+        after_kernel,
+        grid=(length // tile,),
+        in_specs=[
+            rows_of((tile, PADDED), 0),
+            rows_of((tile, PADDED), 0),
+            rows_of((tile, MODEL_WIDTH), 0),
+            rows_of((tile, MODEL_WIDTH), 0),
+            rows_of((tile, MODEL_WIDTH), 0),
+            rows_of((tile, MODEL_WIDTH), 0),
+            rows_of((tile, MODEL_WIDTH), 0),
+            rows_of((MODEL_WIDTH, tile), 1),
+            rows_of((3, RANK, tile), 2),
+            once(mods.shape),
+            once((2, MODEL_WIDTH, 5 * LANES)),
+            once(up_proj.shape),
+            once(down_proj.shape),
+            once(down_expand.shape),
+            once(up_shrink.shape),
+            once(bias.shape),
+        ],
+        out_specs=[
+            rows_of((tile, MODEL_WIDTH), 0),
+            rows_of((tile, MODEL_WIDTH), 0),
+            rows_of((MODEL_WIDTH, tile), 1),
+            once((8, MODEL_WIDTH)),
+            once((RANK, MODEL_WIDTH)),
+            once((RANK, MODEL_WIDTH)),
+            once((RANK, MODEL_WIDTH)),
+            once((MODEL_WIDTH, LANES)),
+        ],
+        out_shape=[
+            jax.ShapeDtypeStruct((length, MODEL_WIDTH), bf16),
+            jax.ShapeDtypeStruct((length, MODEL_WIDTH), f32),
+            jax.ShapeDtypeStruct((MODEL_WIDTH, length), bf16),
+            jax.ShapeDtypeStruct((8, MODEL_WIDTH), f32),
+            low_rank,
+            low_rank,
+            low_rank,
+            jax.ShapeDtypeStruct((MODEL_WIDTH, LANES), f32),
+        ],
+        scratch_shapes=[pltpu.VMEM((PADDED, MODEL_WIDTH), bf16)],
+        cost_estimate=pl.CostEstimate(
+            flops=5 * length * MODEL_WIDTH * PADDED,
+            bytes_accessed=32 * length * MODEL_WIDTH,
+            transcendentals=0,
+        ),
+        compiler_params=pltpu.CompilerParams(vmem_limit_bytes=60 * MIB),
+        name="after_feed",
+    )(
+        final,
+        dsecond,
+        tokens,
+        cotangent,
+        branch,
+        second,
+        dfinal,
+        mixed,
+        middles,
+        mods,
+        weight,
+        up_proj,
+        down_proj,
+        down_expand,
+        up_shrink,
+        bias,
+    )
+
+
+def leave_kernel(
+    dqkv_ref,
+    token_ref,
+    dresidual_ref,
+    hidden_ref,
+    middle_ref,
+    mod_ref,
+    weight_ref,
+    up_ref,
+    down_ref,
+    token_grad_ref,
+    sums_ref,
+    up_grad,
+    down_grad,
+    weight_aug,
+):
+    bf16 = jnp.bfloat16
+    half = 3 * HALF
+
+    @pl.when(pl.program_id(0) == 0)
+    def _():
+        weight_aug[:MODEL_WIDTH, :half] = weight_ref[0, :, HALF:]
+        weight_aug[:MODEL_WIDTH, half:] = weight_ref[1, :, HALF:]
+        weight_aug[MODEL_WIDTH:, :] = up_ref[...]
+
+    tile = token_ref.shape[0]
+    middle_t = transposed(middle_ref[...])[:RANK].astype(bf16)
+    joined = jnp.zeros((tile, PADDED), jnp.float32)
+    up_grads = []
+    for part in range(3):
+        columns = slice(part * MODEL_WIDTH, (part + 1) * MODEL_WIDTH)
+        packed_t = dqkv_ref[part].astype(jnp.float32).reshape(MODEL_WIDTH, tile)
+        packed = packed_t.T.astype(bf16)
+        joined = joined + nt(packed, weight_aug[:, columns])
+        up_grads.append(nn(middle_t, packed))
+    dmiddle = joined[:, MODEL_WIDTH:]
+    d_hidden = joined[:, :MODEL_WIDTH] + nn(dmiddle.astype(bf16), down_ref[...])
+    normed, inverse = standard(token_ref[...].astype(jnp.float32))
+    back = back_through(d_hidden * (1.0 + mod_ref[1:2]), normed, inverse)
+    token_grad_ref[...] = (dresidual_ref[...] + back).astype(bf16)
+    sums = jnp.concatenate(
+        [total(d_hidden), total(d_hidden * normed), jnp.zeros((6, MODEL_WIDTH), jnp.float32)], 0
+    )
+    down = nn(dmiddle.T[:RANK].astype(bf16), hidden_ref[...])
+
+    @pl.when(pl.program_id(0) == 0)
+    def _():
+        sums_ref[...] = sums
+        down_grad[...] = down
+        for part in range(3):
+            up_grad[:, part * MODEL_WIDTH : (part + 1) * MODEL_WIDTH] = up_grads[part]
+
+    @pl.when(pl.program_id(0) > 0)
+    def _():
+        sums_ref[...] += sums
+        down_grad[...] += down
+        for part in range(3):
+            up_grad[:, part * MODEL_WIDTH : (part + 1) * MODEL_WIDTH] += up_grads[part]
+
+
+def leave(dqkv, tokens, dresidual, hidden, middle, mods, weight, up, down, tile=256):
+    length = tokens.shape[0]
+    bf16, f32 = jnp.bfloat16, jnp.float32
+    return pl.pallas_call(
+        leave_kernel,
+        grid=(length // tile,),
+        in_specs=[
+            rows_of((3, HEADS, HD, tile), 3),
+            rows_of((tile, MODEL_WIDTH), 0),
+            rows_of((tile, MODEL_WIDTH), 0),
+            rows_of((tile, MODEL_WIDTH), 0),
+            rows_of((tile, LANES), 0),
+            once(mods.shape),
+            once(weight.shape),
+            once(up.shape),
+            once(down.shape),
+        ],
+        out_specs=[
+            rows_of((tile, MODEL_WIDTH), 0),
+            once((8, MODEL_WIDTH)),
+            once((RANK, 3 * MODEL_WIDTH)),
+            once((RANK, MODEL_WIDTH)),
+        ],
+        out_shape=[
+            jax.ShapeDtypeStruct((length, MODEL_WIDTH), bf16),
+            jax.ShapeDtypeStruct((8, MODEL_WIDTH), f32),
+            jax.ShapeDtypeStruct((RANK, 3 * MODEL_WIDTH), f32),
+            jax.ShapeDtypeStruct((RANK, MODEL_WIDTH), f32),
+        ],
+        scratch_shapes=[pltpu.VMEM((PADDED, 3 * MODEL_WIDTH), bf16)],
+        cost_estimate=pl.CostEstimate(
+            flops=7 * length * MODEL_WIDTH * PADDED,
+            bytes_accessed=2 * weight.size + 18 * length * MODEL_WIDTH,
+            transcendentals=0,
+        ),
+        compiler_params=pltpu.CompilerParams(vmem_limit_bytes=60 * MIB),
+        name="leave",
+    )(dqkv, tokens, dresidual, hidden, middle, mods, weight, up, down)
+
+
+def layout(n_fsdp):
+    return [(f // 4, f // 2 % 2, f % 2) for f in range(n_fsdp)]
+
+
+def moved(n_fsdp, step):
+    pairs = []
+    for f, (z, x, c) in enumerate(layout(n_fsdp)):
+        for y in range(2):
+            to_z, to_x, to_c, to_y = step(z, x, c, y)
+            pairs.append((2 * f + y, 2 * (4 * to_z + 2 * to_x + to_c) + to_y))
+    return pairs
+
+
+BOTH = ("fsdp", "seq")
+
+
+def step_z(block, n_fsdp):
+    depth = n_fsdp // 4
+    by_shift = [block]
+    for shift in range(1, depth):
+        pairs = moved(n_fsdp, lambda z, x, c, y: ((z + shift) % depth, x, c, y))
+        by_shift.append(lax.ppermute(block, BOTH, pairs))
+    return jnp.stack(by_shift)
+
+
+def step_first(block, n_fsdp):
+    return lax.ppermute(
+        block,
+        BOTH,
+        moved(n_fsdp, lambda z, x, c, y: (z, x, c, 1 - y) if c else (z, 1 - x, c, y)),
+    )
+
+
+def step_second(block, n_fsdp):
+    return lax.ppermute(
+        block,
+        BOTH,
+        moved(n_fsdp, lambda z, x, c, y: (z, 1 - x, c, y) if c else (z, x, c, 1 - y)),
+    )
+
+
+def step_x(block, n_fsdp):
+    return lax.ppermute(block, BOTH, moved(n_fsdp, lambda z, x, c, y: (z, 1 - x, c, y)))
+
+
+def step_core(block, n_fsdp):
+    return lax.ppermute(block, BOTH, moved(n_fsdp, lambda z, x, c, y: (z, x, 1 - c, y)))
+
+
+def behind(block, *earlier):
+    return lax.optimization_barrier((block, *earlier))[0]
+
+
+def complete(near, far, n_fsdp, place, late_x=False):
+    rows, columns = near.shape[2:]
+    gathered = assemble(
+        place, near, far, step_core(near, n_fsdp), step_core(far, n_fsdp), late_x
+    )
+    return gathered.reshape(2, n_fsdp * rows, columns)
+
+
+def gather_all(blocks, n_fsdp, place, told, mod_base, parts):
+    heads_block, low_block, high_block = blocks
+    heads_line = behind(step_z(heads_block, n_fsdp), told)
+    heads_near = jnp.stack([heads_line, step_first(heads_line, n_fsdp)])
+    heads_far = step_second(behind(heads_near, mod_base), n_fsdp)
+    low_line = step_z(behind(low_block, heads_line), n_fsdp)
+    low_line = behind(low_line, heads_far)
+    low_near = jnp.stack([low_line, step_first(low_line, n_fsdp)])
+    low_far = step_second(low_near, n_fsdp)
+    high_pair = jnp.stack([high_block, swap(behind(high_block, heads_line))])
+    high_near = step_z(behind(high_pair, low_line), n_fsdp)
+    high_far = step_x(behind(high_near, low_far), n_fsdp)
+    return (
+        complete(behind(heads_near, *parts), behind(heads_far, *parts), n_fsdp, place),
+        complete(low_near, low_far, n_fsdp, place),
+        complete(high_near, high_far, n_fsdp, place, True),
+        heads_far,
+        high_far,
+    )
+
+
+DOWN_EDGES = (0, 1152, 2304, 3456, 4608, 9216)
+UP_EDGES = (0, 6912, 10368, 11520, 16128, 17280)
+PIECES = FF // HD
+
+
+def piece_order(n_fsdp):
+    per = PIECES // n_fsdp
+    return [f * per + q for q in range(per) for f in range(n_fsdp)]
+
+
+def unpack_kernel(came_ref, *refs, order, down_chunk, up_chunk):
+    bf16 = jnp.bfloat16
+    outs, (down_all, up_all, mixed) = refs[:-3], refs[-3:]
+    down_outs, up_outs, shrink_t = outs[:4], outs[4:9], outs[9]
+    for f in range(came_ref.shape[0]):
+        block = came_ref[f].astype(jnp.float32)
+        down_all[:, f * down_chunk : (f + 1) * down_chunk] = block[:, :down_chunk]
+        up_all[:, f * up_chunk : (f + 1) * up_chunk] = block[:, down_chunk:]
+    for target, out in enumerate(down_outs):
+        out[...] = jnp.zeros_like(out)
+        out[:RANK] = down_all[:, DOWN_EDGES[target] : DOWN_EDGES[target + 1]].astype(bf16)
+    mixed[...] = jnp.zeros_like(mixed)
+    for target, out in enumerate(up_outs):
+        if target == 3:
+            for to, piece in enumerate(order):
+                at = UP_EDGES[3] + piece * HD
+                mixed[:RANK, to * HD : (to + 1) * HD] = up_all[:, at : at + HD]
+            out[...] = mixed[...].astype(bf16)
+        else:
+            out[...] = jnp.zeros_like(out)
+            out[:RANK] = up_all[:, UP_EDGES[target] : UP_EDGES[target + 1]].astype(bf16)
+    for to, piece in enumerate(order):
+        at = DOWN_EDGES[4] + piece * HD
+        mixed[:RANK, to * HD : (to + 1) * HD] = down_all[:, at : at + HD]
+    for start in range(0, FF, MODEL_WIDTH):
+        shrink_t[start : start + MODEL_WIDTH, :] = mixed[:, start : start + MODEL_WIDTH].T.astype(
+            bf16
+        )
+
+
+def unpack(came, order, down_chunk, up_chunk):
+    bf16 = jnp.bfloat16
+    widths = [DOWN_EDGES[t + 1] - DOWN_EDGES[t] for t in range(4)]
+    widths += [UP_EDGES[t + 1] - UP_EDGES[t] for t in range(5)]
+    return pl.pallas_call(
+        functools.partial(
+            unpack_kernel, order=order, down_chunk=down_chunk, up_chunk=up_chunk
+        ),
+        out_shape=[jax.ShapeDtypeStruct((LANES, w), bf16) for w in widths]
+        + [jax.ShapeDtypeStruct((FF, LANES), bf16)],
+        scratch_shapes=[
+            pltpu.VMEM((RANK, DOWN_EDGES[5]), jnp.float32),
+            pltpu.VMEM((RANK, UP_EDGES[5]), jnp.float32),
+            pltpu.VMEM((LANES, FF), jnp.float32),
+        ],
+        compiler_params=pltpu.CompilerParams(vmem_limit_bytes=48 * MIB),
+        name="unpack",
+    )(came)
+
+
+def pack_kernel(
+    leave_ref,
+    after_ref,
+    middle_ref,
+    cond_ref,
+    down_ada_ref,
+    up_ada_ref,
+    down_qkv,
+    up_qkv,
+    down_proj,
+    up_proj,
+    down_expand,
+    up_expand_low,
+    up_expand_high,
+    down_shrink_low,
+    down_shrink_high,
+    up_shrink,
+    sent_ref,
+    dmod_ref,
+    own_ref,
+    down_all,
+    up_all,
+    *,
+    order,
+    down_chunk,
+    up_chunk,
+):
+    bf16, f32 = jnp.bfloat16, jnp.float32
+    width = MODEL_WIDTH
+    dmiddle = jnp.zeros((RANK, 1), f32)
+    for block in range(6):
+        source = leave_ref if block < 2 else after_ref
+        line = source[block % 2 if block < 2 else block - 2, :].reshape(1, width)
+        line = line.astype(bf16).astype(f32)
+        columns = slice(block * width, (block + 1) * width)
+        side, at = block // 3, block % 3 * width
+        dmod_ref[side : side + 1, at : at + width] = line
+        up_all[:, columns] = middle_ref[...] * line
+        dmiddle += jnp.sum(up_ada_ref[:RANK, columns].astype(f32) * line, axis=1, keepdims=True)
+    dmiddle = dmiddle.astype(bf16).astype(f32)
+    down_all[:, :width] = dmiddle * cond_ref[...]
+    own_ref[...] = total(dmiddle * down_ada_ref[:RANK].astype(f32))
+    down_all[:, width : 2 * width] = down_qkv[...]
+    down_all[:, 2 * width : 3 * width] = down_proj[...].T[:RANK]
+    down_all[:, 3 * width : 4 * width] = down_expand[...]
+    up_all[:, UP_EDGES[1] : UP_EDGES[2]] = up_qkv[...]
+    up_all[:, UP_EDGES[2] : UP_EDGES[3]] = up_proj[...]
+    up_all[:, UP_EDGES[4] : UP_EDGES[5]] = up_shrink[...]
+    half = PIECES // 2
+    for at, piece in enumerate(order):
+        ups = up_expand_low if at < half else up_expand_high
+        downs = down_shrink_low if at < half else down_shrink_high
+        columns = slice((at % half) * HD, (at % half + 1) * HD)
+        to = UP_EDGES[3] + piece * HD
+        up_all[:, to : to + HD] = ups[:, columns]
+        to = DOWN_EDGES[4] + piece * HD
+        down_all[:, to : to + HD] = downs[:, columns]
+    for f in range(sent_ref.shape[0]):
+        sent_ref[f, :, :down_chunk] = down_all[:, f * down_chunk : (f + 1) * down_chunk].astype(bf16)
+        sent_ref[f, :, down_chunk:] = up_all[:, f * up_chunk : (f + 1) * up_chunk].astype(bf16)
+
+
+def pack(operands, n_fsdp, order, down_chunk, up_chunk):
+    bf16, f32 = jnp.bfloat16, jnp.float32
+    return pl.pallas_call(
+        functools.partial(pack_kernel, order=order, down_chunk=down_chunk, up_chunk=up_chunk),
+        out_shape=[
+            jax.ShapeDtypeStruct((n_fsdp, RANK, down_chunk + up_chunk), bf16),
+            jax.ShapeDtypeStruct((2, 3 * MODEL_WIDTH), f32),
+            jax.ShapeDtypeStruct((1, MODEL_WIDTH), f32),
+        ],
+        scratch_shapes=[
+            pltpu.VMEM((RANK, DOWN_EDGES[5]), f32),
+            pltpu.VMEM((RANK, UP_EDGES[5]), f32),
+        ],
+        compiler_params=pltpu.CompilerParams(vmem_limit_bytes=48 * MIB),
+        name="pack",
+    )(*operands)
+
+
+def owners_kernel(ids_ref, place_ref, came_ref, kept_ref, given_ref, sums):
+    sums[...] = jnp.zeros_like(sums)
+    for f in range(came_ref.shape[0]):
+        sums[ids_ref[f]] += came_ref[f].astype(jnp.float32)
+    held = kept_ref.shape[0]
+    mine = place_ref[3]
+    for index in range(held):
+        kept_ref[index] = sums[mine * held + index]
+        given_ref[index] = sums[(1 - mine) * held + index].astype(jnp.bfloat16)
+
+
+def owners(ids, place, came):
+    held = ADAPTER_COUNT // 2
+    shape = (held,) + came.shape[1:]
+    return pl.pallas_call(
+        owners_kernel,
+        in_specs=[
+            pl.BlockSpec(memory_space=pltpu.SMEM),
+            pl.BlockSpec(memory_space=pltpu.SMEM),
+            pl.BlockSpec(memory_space=pltpu.VMEM),
+        ],
+        out_shape=[
+            jax.ShapeDtypeStruct(shape, jnp.float32),
+            jax.ShapeDtypeStruct(shape, jnp.bfloat16),
+        ],
+        scratch_shapes=[pltpu.VMEM((ADAPTER_COUNT,) + came.shape[1:], jnp.float32)],
+        compiler_params=pltpu.CompilerParams(vmem_limit_bytes=32 * MIB),
+        name="owners",
+    )(ids, place, came)
+
+
+def update_kernel(gradient_ref, squared_ref, *refs):
+    down_chunk = refs[0].shape[-1]
+    grad_norm = jnp.sqrt(jnp.sum(squared_ref[:, :1], axis=0, keepdims=True))
+    clip_factor = jnp.minimum(1.0, clip_limit / (grad_norm + norm_eps))
+    ins, outs, norm_ref = refs[:6], refs[6:12], refs[12]
+    norm_ref[...] = jnp.broadcast_to(grad_norm, norm_ref.shape)
+    for kind in range(2):
+        part = slice(0, down_chunk) if kind == 0 else slice(down_chunk, None)
+        for index in range(gradient_ref.shape[0]):
+            gradient = gradient_ref[index, :, part] * clip_factor
+            params = ins[kind][index]
+            moment_new = beta_first * ins[2 + kind][index] + (1.0 - beta_first) * gradient
+            square_new = (
+                beta_second * ins[4 + kind][index] + (1.0 - beta_second) * gradient * gradient
+            )
+            direction = (
+                moment_new
+                / (1.0 - beta_first**STEP)
+                / (jnp.sqrt(square_new / (1.0 - beta_second**STEP)) + adam_eps)
+            )
+            outs[kind][index] = params - learn_rate * (direction + decay_rate * params)
+            outs[2 + kind][index] = moment_new
+            outs[4 + kind][index] = square_new
+
+
+def update(gradient, squared, states):
+    f32 = jnp.float32
+    outs = pl.pallas_call(
+        update_kernel,
+        out_shape=[jax.ShapeDtypeStruct(s.shape, f32) for s in states]
+        + [jax.ShapeDtypeStruct((8, LANES), f32)],
+        compiler_params=pltpu.CompilerParams(vmem_limit_bytes=32 * MIB),
+        name="update",
+    )(gradient, squared, *states)
+    return outs[:6], outs[6][0, 0]
+
+
+def fits(mesh):
+    return mesh.shape["seq"] == MB and mesh.shape["fsdp"] == 16
+
+
+def dot(equation, left, right):
+    return jnp.einsum(equation, left, right, preferred_element_type=jnp.float32)
+
+
+def swap(block):
+    return lax.ppermute(block, "seq", [(0, 1), (1, 0)])
+
+
+def by_seq(own, other, mine):
+    first = mine == 0
+    return jnp.stack([jnp.where(first, own, other), jnp.where(first, other, own)])
+
+
+def swap_rows(halves, mine):
+    sent = lax.dynamic_index_in_dim(halves, 1 - mine, 0, False)
+    return by_seq(lax.dynamic_index_in_dim(halves, mine, 0, False), swap(sent), mine)
+
+
+def to_all(block):
+    return lax.all_to_all(block, ("fsdp", "seq"), split_axis=0, concat_axis=0, tiled=True)
+
+
+def to_fsdp(block):
+    return lax.all_to_all(block, "fsdp", split_axis=0, concat_axis=0, tiled=True)
+
+
+def fast_shards(
+    tokens,
+    condition,
+    adapter,
+    cotangent,
+    modulation_weight,
+    modulation_bias,
+    query_key_value_weight,
+    attention_out_weight,
+    attention_out_bias,
+    widen_weight,
+    widen_bias,
+    narrow_weight,
+    narrow_bias,
+    lowrank_down,
+    lowrank_up,
+    first_moment_down,
+    first_moment_up,
+    second_moment_down,
+    second_moment_up,
+):
+    bf16 = jnp.bfloat16
+    n_fsdp = lax.axis_size("fsdp")
+    mine = lax.axis_index("seq")
+    row = lax.axis_index("fsdp")
+    place = jnp.stack([row // 4, row // 2 % 2, row % 2, mine]).astype(jnp.int32)
+    down_chunk, up_chunk = lowrank_down.shape[-1], lowrank_up.shape[-1]
+    depth = modulation_weight.shape[0]
+    order = piece_order(n_fsdp)
+    per = PIECES // n_fsdp
+
+    cond_act_pair = jax.nn.silu(condition).astype(bf16)
+    told = jnp.moveaxis(cond_act_pair.reshape(MB, n_fsdp, depth), 1, 0)
+    numbers = jnp.broadcast_to(adapter.astype(bf16)[None, :, None], (n_fsdp, MB, 8))
+    told = to_fsdp(jnp.concatenate([told, numbers], 2))
+    own_ids = lax.dynamic_index_in_dim(told[:, :, depth], mine, 1, False).astype(jnp.int32)
+
+    wide = jnp.moveaxis(widen_weight.reshape(depth, -1, per, HD), 2, 0).reshape(per, depth, HALF)
+    narrow = narrow_weight.reshape(per, depth, HALF)
+    joined = [jnp.concatenate([wide[q], narrow[q]], 1) for q in range(per)]
+    portions = jnp.concatenate([lowrank_down.astype(bf16), lowrank_up.astype(bf16)], -1)
+    others = swap(portions)
+    table = by_seq(portions, others, mine).reshape(ADAPTER_COUNT, RANK, -1)
+    picks = jax.nn.one_hot(own_ids, ADAPTER_COUNT, dtype=bf16)
+    chosen = dot("fa,arc->frc", picks, table).astype(bf16)
+    parts = unpack(to_fsdp(chosen), order, down_chunk, up_chunk)
+    down_ada, down_qkv, down_proj, down_expand = parts[:4]
+    up_ada, up_qkv, up_proj, up_expand, up_shrink = parts[4:9]
+    down_shrink_t = parts[9]
+
+    spoken = told[:, :, :depth].reshape(n_fsdp * MB, depth)
+    mod_part = to_all(dot("si,io->so", spoken, modulation_weight))
+    mod_base = jnp.sum(mod_part.reshape(n_fsdp, MB, -1), axis=0).reshape(1, -1)
+
+    heads_weight, low_weight, high_weight, arrived, ended = gather_all(
+        (
+            jnp.concatenate([attention_out_weight, query_key_value_weight], 1),
+            jnp.concatenate(joined[: per // 2], 1),
+            jnp.concatenate(joined[per // 2 :], 1),
+        ),
+        n_fsdp,
+        place,
+        told,
+        mod_base,
+        parts,
+    )
+    cond_act = lax.dynamic_slice_in_dim(cond_act_pair, mine, 1, 0)
+    middle_ada = dot("ti,ri->tr", cond_act, down_ada).astype(bf16)
+    modulation = mod_base + modulation_bias + dot("tr,ro->to", middle_ada, up_ada)
+    mods = jnp.pad(modulation.reshape(6, MODEL_WIDTH), ((0, 2), (0, 0)))
+
+    length = MB * tokens.shape[1]
+    token_rows = swap_rows(tokens, mine).reshape(length, MODEL_WIDTH)
+    cot_rows = swap_rows(behind(cotangent, arrived), mine).reshape(length, MODEL_WIDTH)
+
+    hidden, middle_qkv, qkv = entry(token_rows, mods, heads_weight, up_qkv, down_qkv)
+    mixed_heads, log_total = heads_forward(qkv, step=length)
+    mixed = mixed_heads.reshape(MODEL_WIDTH, length)
+    second, dfinal, branch, middles = before_feed(
+        mixed,
+        token_rows,
+        cot_rows,
+        mods,
+        heads_weight,
+        up_proj,
+        down_proj,
+        down_expand,
+        up_shrink,
+        attention_out_bias[None],
+    )
+    bias = jnp.moveaxis(widen_bias.reshape(n_fsdp, per, HD), 0, 1).reshape(1, FF)
+    cut = FF // 2
+    final, dsecond, up_expand_low, down_shrink_low = feed(
+        second,
+        dfinal,
+        middles,
+        low_weight,
+        up_expand[:, :cut],
+        down_shrink_t[:cut],
+        bias[:, :cut],
+        None,
+    )
+    final, dsecond, up_expand_high, down_shrink_high = feed(
+        second,
+        dfinal,
+        middles,
+        high_weight,
+        up_expand[:, cut:],
+        down_shrink_t[cut:],
+        bias[:, cut:],
+        (final, dsecond),
+    )
+    (
+        block_rows,
+        d_residual,
+        d_mixed,
+        after_sums,
+        up_shrink_grad,
+        down_expand_grad,
+        up_proj_grad,
+        down_proj_grad,
+    ) = after_feed(
+        final,
+        dsecond,
+        token_rows,
+        cot_rows,
+        branch,
+        second,
+        dfinal,
+        mixed,
+        middles,
+        mods,
+        heads_weight,
+        up_proj,
+        down_proj,
+        down_expand,
+        up_shrink,
+        narrow_bias[None],
+    )
+    block_out = swap_rows(block_rows.reshape(tokens.shape), mine)
+    d_qkv = heads_back(qkv, d_mixed.reshape(HEADS, HD, length), log_total, step=length // 2)
+    token_rows_grad, leave_sums, up_qkv_grad, down_qkv_grad = leave(
+        d_qkv, token_rows, d_residual, hidden, middle_qkv, mods, heads_weight, up_qkv, down_qkv
+    )
+
+    sent, d_modulation, own_cond = pack(
+        (
+            leave_sums,
+            after_sums,
+            middle_ada[:, :RANK].astype(jnp.float32).T,
+            cond_act.astype(jnp.float32),
+            down_ada,
+            up_ada,
+            down_qkv_grad,
+            up_qkv_grad,
+            down_proj_grad,
+            up_proj_grad,
+            down_expand_grad,
+            up_expand_low,
+            up_expand_high,
+            down_shrink_low,
+            down_shrink_high,
+            up_shrink_grad,
+        ),
+        n_fsdp,
+        order,
+        down_chunk,
+        up_chunk,
+    )
+    kept, given = owners(own_ids, place, to_fsdp(sent))
+    gradient = kept + swap(given).astype(jnp.float32)
+    squared = to_all(jnp.broadcast_to(jnp.sum(gradient * gradient), (n_fsdp * MB, LANES)))
+
+    half_weight = lax.all_gather(
+        behind(modulation_weight, ended), "fsdp", axis=0, tiled=True
+    )
+    both_mod = swap_rows(d_modulation.astype(bf16), mine)
+    d_cond = dot("so,io->si", both_mod, half_weight)
+    d_cond = d_cond + jnp.where(jnp.arange(MB)[:, None] == mine, own_cond, 0.0)
+    d_cond = d_cond + swap(d_cond)
+    cond_grad = jax.vjp(jax.nn.silu, condition)[1](d_cond)[0]
+    token_grad = swap_rows(token_rows_grad.reshape(tokens.shape), mine).astype(jnp.float32)
+
+    states = (
+        lowrank_down,
+        lowrank_up,
+        first_moment_down,
+        first_moment_up,
+        second_moment_down,
+        second_moment_up,
+    )
+    fresh, grad_norm = update(gradient, squared, states)
+    return (block_out, token_grad, cond_grad, grad_norm, *fresh)
+
+
 def solution(mesh):
     in_specs = (
         P("fsdp", "seq", None),
@@ -415,4 +1632,5 @@
         P("seq", None, "fsdp"),
         P("seq", None, "fsdp"),
     )
-    return jax.shard_map(shards, mesh=mesh, in_specs=in_specs, out_specs=out_specs, check_vma=False)
+    body = fast_shards if fits(mesh) else shards
+    return jax.shard_map(body, mesh=mesh, in_specs=in_specs, out_specs=out_specs, check_vma=False)

time: 2070 us -> 644 us (0.31)
  matrix products: 647 us -> 6.71 us
  waiting for transfers between devices: 553 us -> 162 us
  local copies, waits for them, and re-layouts: 374 us -> 52.1 us
  blocking collectives: 309 us -> 0 us
  Pallas kernels: 0 us -> 266 us
  other arithmetic: 108 us -> 42.3 us
  starting transfers between devices: 39.9 us -> 89.9 us
    dot_general x132 -> x5, matrix products: 647 us -> 6.71 us  [dot(): return jnp.einsum(equation, left, right, preferred_element_type=jnp.float32)]
    all_gather x7 -> x1, waiting for transfers between devices: 404 us -> 0.02 us  [fast_shards(): lax.all_gather(behind(modulation_weight, ended), 'fsdp', axis=0, tiled=True)]
    pallas_call x0 -> x15, Pallas kernels: none -> 266 us  [the longest x2 73.5 us: feed(): pl.pallas_call(functools.partial(feed_kernel, rows=rows, first=first, sub...]
    unnamed x1 -> x0, blocking collectives: 201 us -> none
    unnamed x465 -> x138, local copies, waits for them, and re-layouts: 168 us -> 20.1 us
    ppermute x0 -> x29, waiting for transfers between devices: none -> 133 us  [the longest x9 66.4 us: step_z(): by_shift.append(lax.ppermute(block, BOTH, pairs))]
    all_to_all x8 -> x5, waiting for transfers between devices: 140 us -> 28.3 us  [the longest x2 21.6 us: to_all(): lax.all_to_all(block, ('fsdp', 'seq'), split_axis=0, concat_axis=0, tiled...]
    slice x7, local copies, waits for them, and re-layouts: 71.3 us -> 6.46 us  [the longest x1 2.43 us: fast_shards(): up_expand[:, :cut]]
  transfers between devices with their start and end apart: 18 -> 35, of which waited for: 12 -> 13; matrix products, arithmetic and copies ran while one was open for 17% -> 12% of each run, Pallas kernels for 0% -> 42%
where the time goes in v2:
time: 644 us; the launch traced here: 634 us
  Pallas kernels  266 us (41%)
  waiting for transfers between devices  162 us (25%)
  starting transfers between devices  89.9 us (14%)
  local copies, waits for them, and re-layouts  52.1 us (8%)
  other arithmetic  42.3 us (7%)
  between operations  15.5 us (2%)
  matrix products  6.71 us (1%)
    pallas_call x2, Pallas kernels, feed(): pl.pallas_call(functools.partial(feed_kernel, rows=rows, first=first, sub...  73.5 us
    ppermute x9, waiting for transfers between devices, step_z(): by_shift.append(lax.ppermute(block, BOTH, pairs))  66.4 us
    pallas_call x1, Pallas kernels, heads_back(): pl.pallas_call(functools.partial(heads_back_kernel, step=step), grid=(hea...  54.6 us
    ppermute x9, waiting for transfers between devices, swap(): return lax.ppermute(block, 'seq', [(0, 1), (1, 0)])  42.5 us
    pallas_call x1, Pallas kernels, heads_forward(): pl.pallas_call(functools.partial(heads_kernel, step=step), grid=(heads,),...  29.5 us
    all_to_all x3, starting transfers between devices, to_fsdp(): lax.all_to_all(block, 'fsdp', split_axis=0, concat_axis=0, tiled=True)  26.6 us
    all_to_all x2, starting transfers between devices, to_all(): lax.all_to_all(block, ('fsdp', 'seq'), split_axis=0, concat_axis=0, tiled...  25.9 us
    pallas_call x1, Pallas kernels, leave(): pl.pallas_call(leave_kernel, grid=(length // tile,), in_specs=[rows_of((3...  24.6 us
  transfers between devices with their start and end apart: 35, of which 13 were waited for; matrix products, arithmetic and copies ran while one was open for 12% of the time, Pallas kernels for 42%

profile of v2, /device:TPU:0, one launch (start us, length us, event | category | flops | bytes accessed | tf_op | source)
XLA Modules:
  0.0 634.5 jit_solution(6133593230675551498)
XLA Ops:
  17.6 3.5 all-to-all-start
  22.3 13.4 %collective-permute-done.3 = bf16[72,2304]{1,0:T(8,128)(2,1)S(1)} collective-permute-done((bf16[72,2304]{1,0:T(8,128)(2,1)S(1)}, bf16[72,2304]{1,0:T(8,128)(2,1)S(1)}, u32[]{:S(2)}, u32[]{:S(2)}) %collective-permute-start.3) | collective-permute-done | bytes 331808 | tf_op jit(solution)/shard_map/ppermute | solution.py:1107
  36.9 6.8 %all-to-all-done = bf16[16,2,80]{2,1,0:T(2,128)(2,1)S(1)} async-done(((bf16[16,2,80]{2,1,0:T(2,128)(2,1)}), bf16[16,2,80]{2,1,0:T(2,128)(2,1)S(1)}, u32[]{:S(2)}, u32[]{:S(2)}) %all-to-all-start) | async-done | bytes 5152 | tf_op jit(solution)/shard_map/all_to_all | solution.py:1403
  44.2 17.4 %collective-permute-done.5 = bf16[4,72,2304]{2,1,0:T(8,128)(2,1)S(1)} collective-permute-done((bf16[4,72,2304]{2,1,0:T(8,128)(2,1)}, bf16[4,72,2304]{2,1,0:T(8,128)(2,1)S(1)}, u32[]{:S(2)}, u32[]{:S(2)}) %collective-permute-start.5) | collective-permute-done | bytes 1327136 | tf_op jit(solution)/shard_map/ppermute | solution.py:1112
  82.9 4.8 collective-permute-done.11
  89.1 10.2 %collective-permute-done.12 = bf16[72,2304]{1,0:T(8,128)(2,1)} collective-permute-done((bf16[72,2304]{1,0:T(8,128)(2,1)}, bf16[72,2304]{1,0:T(8,128)(2,1)}, u32[]{:S(2)}, u32[]{:S(2)}) %collective-permute-start.12) | collective-permute-done | bytes 331808 | tf_op jit(solution)/shard_map/ppermute | solution.py:1107
  101.9 6.9 %collective-permute-done.6.far_ref = bf16[2,4,72,2304]{3,2,1,0:T(8,128)(2,1)} collective-permute-done((bf16[2,4,72,2304]{3,2,1,0:T(8,128)(2,1)S(1)}, bf16[2,4,72,2304]{3,2,1,0:T(8,128)(2,1)}, u32[]{:S(2)}, u32[]{:S(2)}) %collective-permute-start.6) | collective-permute-done | bytes 2654240 | tf_op jit(solution)/shard_map/ppermute | solution.py:1120
  110.2 7.2 %all-to-all-start.1 = ((f32[32,1,3456]{2,1,0:T(1,128)}), f32[32,1,3456]{2,1,0:T(1,128)}, u32[]{:S(2)}, u32[]{:S(2)}) async-start(f32[32,1,3456]{2,1,0:T(1,128)} %copy.51), calls=%async_computation.1 | async-start | bytes 884736 | tf_op jit(solution)/shard_map/all_to_all | solution.py:1399
  122.3 21.6 %all-to-all-done.1 = f32[32,1,3456]{2,1,0:T(1,128)} async-done(((f32[32,1,3456]{2,1,0:T(1,128)}), f32[32,1,3456]{2,1,0:T(1,128)}, u32[]{:S(2)}, u32[]{:S(2)}) %all-to-all-start.1) | async-done | bytes 442400 | tf_op jit(solution)/shard_map/all_to_all | solution.py:1399
  143.8 4.5 all-to-all-start.2
  159.7 3.7 pad_maximum_fusion.2.near_ref
  179.4 11.5 %collective-permute-done.14 = bf16[2,72,2304]{2,1,0:T(8,128)(2,1)S(1)} collective-permute-done((bf16[2,72,2304]{2,1,0:T(8,128)(2,1)}, bf16[2,72,2304]{2,1,0:T(8,128)(2,1)S(1)}, u32[]{:S(2)}, u32[]{:S(2)}) %collective-permute-start.14) | collective-permute-done | bytes 663584 | tf_op jit(solution)/shard_map/ppermute | solution.py:1107
  192.4 26.4 %collective-permute-done.15 = bf16[2,72,2304]{2,1,0:T(8,128)(2,1)S(1)} collective-permute-done((bf16[2,72,2304]{2,1,0:T(8,128)(2,1)S(1)}, bf16[2,72,2304]{2,1,0:T(8,128)(2,1)S(1)}, u32[]{:S(2)}, u32[]{:S(2)}) %collective-permute-start.15) | collective-permute-done | bytes 663584 | tf_op jit(solution)/shard_map/ppermute | solution.py:1107
  227.3 19.9 %collective-permute-done.9 = bf16[512,1152]{1,0:T(8,128)(2,1)} collective-permute-done((bf16[512,1152]{1,0:T(8,128)(2,1)}, bf16[512,1152]{1,0:T(8,128)(2,1)}, u32[]{:S(2)}, u32[]{:S(2)}) %collective-permute-start.9) | collective-permute-done | bytes 1179680 | tf_op jit(solution)/shard_map/ppermute | solution.py:1385
  250.3 7.2 %assemble.3 = bf16[2,4,2,2,72,2304]{5,4,3,2,1,0:T(8,128)(2,1)S(1)} custom-call(s32[4]{0:T(128)S(1)} %pad_add_fusion.place_ref, bf16[2,4,72,2304]{3,2,1,0:T(8,128)(2,1)S(1)} %pad_maximum_fusion.near_ref, bf16[2,4,72,2304]{3,2,1,0:T(8,128)(2,1)} %collective-permute-done.6.far_ref, bf16[2,4,72,2304]{3,2,1,0:T(8,128)(2,1)} %collective-permute-done.7.next_near_ref, ...), custom_call_target="tpu_custom_call" | custom-call | bytes 21233664 | tf_op jit(solution)/shard_map/assemble/pallas_call | solution.py:555
  257.6 4.0 copy-done
  262.1 20.3 %entry.1 = (bf16[1024,1152]{1,0:T(8,128)(2,1)}, bf16[1024,128]{1,0:T(8,128)(2,1)}, bf16[3,16,72,1024]{3,2,1,0:T(8,128)(2,1)}) custom-call(bf16[1024,1152]{1,0:T(8,128)(2,1)} %bitcast.136, f32[8,1152]{1,0:T(8,128)} %pad.4.mod_ref, bf16[2,1152,2304]{2,1,0:T(8,128)(2,1)} %bitcast.130, bf16[128,3456]{1,0:T(8,128)(2,1)} %copy-done.47, bf16[128,1152]{1,0:T(8,128)(2,1)} %copy-done.48), custom_call_target="tpu_custom_call" | custom-call | flops 9059696640 | bytes 24772608 | tf_op jit(solution)/shard_map/entry/pallas_call | solution.py:596
  282.5 29.5 %heads_forward.1 = (bf16[16,72,1024]{2,1,0:T(8,128)(2,1)S(1)}, f32[16,1,1024]{2,1,0:T(1,128)S(1)}) custom-call(bf16[3,16,72,1024]{3,2,1,0:T(8,128)(2,1)} %get-tuple-element.84.qkv_ref), custom_call_target="tpu_custom_call" | custom-call | flops 17179869184 | bytes 11796480 | tf_op jit(solution)/shard_map/heads_forward/pallas_call | solution.py:422
  312.7 12.9 %before_feed.1 = (bf16[1024,1280]{1,0:T(8,128)(2,1)}, bf16[1024,1280]{1,0:T(8,128)(2,1)}, f32[1024,1152]{1,0:T(8,128)}, bf16[3,16,1024]{2,1,0:T(8,128)(2,1)S(1)}) custom-call(bf16[1152,1024]{1,0:T(8,128)(2,1)S(1)} %bitcast.140, bf16[1024,1152]{1,0:T(8,128)(2,1)S(1)} %bitcast.139, bf16[1024,1152]{1,0:T(8,128)(2,1)} %bitcast.144, f32[8,1152]{1,0:T(8,128)S(1)} %copy-done.28, ...), custom_call_target="tpu_custom_call" | custom-call | flops 6039797760 | bytes 18874368 | tf_op jit(solution)/shard_map/before_feed/pallas_call | solution.py:679
  325.7 7.4 %assemble.5 = bf16[2,4,2,2,72,2304]{5,4,3,2,1,0:T(8,128)(2,1)S(1)} custom-call(s32[4]{0:T(128)S(1)} %pad_add_fusion.place_ref, bf16[2,4,72,2304]{3,2,1,0:T(8,128)(2,1)} %pad_maximum_fusion.2.near_ref, bf16[2,4,72,2304]{3,2,1,0:T(8,128)(2,1)} %collective-permute-done.18.far_ref, bf16[2,4,72,2304]{3,2,1,0:T(8,128)(2,1)} %collective-permute-done.22.next_near_ref, ...), custom_call_target="tpu_custom_call" | custom-call | bytes 21233664 | tf_op jit(solution)/shard_map/assemble/pallas_call | solution.py:555
  333.1 3.9 copy-done.2
  337.7 35.2 %feed.2 = (f32[1024,1280]{1,0:T(8,128)}, f32[1024,1280]{1,0:T(8,128)}, f32[16,2304]{1,0:T(8,128)}, f32[16,2304]{1,0:T(8,128)}) custom-call(bf16[1024,1280]{1,0:T(8,128)(2,1)} %get-tuple-element.87.second_ref, bf16[1024,1280]{1,0:T(8,128)(2,1)} %get-tuple-element.88.dfinal_ref, bf16[3,16,1024]{2,1,0:T(8,128)(2,1)} %copy-done.33, ...), custom_call_target="tpu_custom_call" | custom-call | flops 24159191040 | bytes 26345472 | tf_op jit(solution)/shard_map/feed/pallas_call | solution.py:779
  372.8 8.4 %assemble.4 = bf16[2,4,2,2,72,2304]{5,4,3,2,1,0:T(8,128)(2,1)S(1)} custom-call(s32[4]{0:T(128)S(1)} %pad_add_fusion.place_ref, bf16[4,2,72,2304]{3,2,1,0:T(8,128)(2,1)} %pad_maximum_fusion.1.near_ref, bf16[4,2,72,2304]{3,2,1,0:T(8,128)(2,1)} %collective-permute-done.19.far_ref, bf16[4,2,72,2304]{3,2,1,0:T(8,128)(2,1)} %collective-permute-done.20.next_near_ref, ...), custom_call_target="tpu_custom_call" | custom-call | bytes 21233664 | tf_op jit(solution)/shard_map/assemble/pallas_call | solution.py:555
  381.2 3.9 copy-done.1
  385.1 38.4 %feed.3 = (f32[1024,1280]{1,0:T(8,128)}, f32[1024,1280]{1,0:T(8,128)}, f32[16,2304]{1,0:T(8,128)}, f32[16,2304]{1,0:T(8,128)}) custom-call(bf16[1024,1280]{1,0:T(8,128)(2,1)} %get-tuple-element.87.second_ref, bf16[1024,1280]{1,0:T(8,128)(2,1)} %get-tuple-element.88.dfinal_ref, ...), custom_call_target="tpu_custom_call", output_to_operand_aliasing={{0}: (7, {}), {1}: (8, {})} | custom-call | flops 24159191040 | bytes 26345472 | tf_op jit(solution)/shard_map/feed/pallas_call | solution.py:779
  423.5 21.4 %after_feed.1 = (bf16[1024,1152]{1,0:T(8,128)(2,1)}, f32[1024,1152]{1,0:T(8,128)}, bf16[1152,1024]{1,0:T(8,128)(2,1)}, f32[8,1152]{1,0:T(8,128)}, f32[16,1152]{1...) custom-call(f32[1024,1280]{1,0:T(8,128)} %get-tuple-element.97.final_ref, ...), custom_call_target="tpu_custom_call" | custom-call | flops 7549747200 | bytes 37748736 | tf_op jit(solution)/shard_map/after_feed/pallas_call | solution.py:917
  446.6 54.6 %heads_back.1.dqkv_ref = bf16[3,16,72,1024]{3,2,1,0:T(8,128)(2,1)} custom-call(bf16[3,16,72,1024]{3,2,1,0:T(8,128)(2,1)} %get-tuple-element.84.qkv_ref, bf16[16,72,1024]{2,1,0:T(8,128)(2,1)S(1)} %bitcast.143, f32[16,1,1024]{2,1,0:T(1,128)S(1)} %copy-done.50), custom_call_target="tpu_custom_call" | custom-call | flops 42949672960 | bytes 18874368 | tf_op jit(solution)/shard_map/heads_back/pallas_call | solution.py:476
  501.2 24.6 %leave.1 = (bf16[1024,1152]{1,0:T(8,128)(2,1)}, f32[8,1152]{1,0:T(8,128)}, f32[16,3456]{1,0:T(8,128)}, f32[16,1152]{1,0:T(8,128)}) custom-call(bf16[3,16,72,1024]{3,2,1,0:T(8,128)(2,1)} %heads_back.1.dqkv_ref, bf16[1024,1152]{1,0:T(8,128)(2,1)} %bitcast.138, f32[1024,1152]{1,0:T(8,128)} %get-tuple-element.103.dresidual_ref, ...), custom_call_target="tpu_custom_call" | custom-call | flops 10569646080 | bytes 31850496 | tf_op jit(solution)/shard_map/leave/pallas_call | solution.py:1049
  541.5 18.7 %all-to-all-start.3 = ((bf16[16,16,1656]{2,1,0:T(8,128)(2,1)}), bf16[16,16,1656]{2,1,0:T(8,128)(2,1)S(1)}, u32[]{:S(2)}, u32[]{:S(2)}) async-start(bf16[16,16,1656]{2,1,0:T(8,128)(2,1)} %get-tuple-element.122), calls=%async_computation.3 | async-start | bytes 1703936 | tf_op jit(solution)/shard_map/all_to_all | solution.py:1403
  563.5 18.5 %collective-permute-done.26 = bf16[3456]{0:T(1024)(128)(2,1)S(1)} collective-permute-done((bf16[3456]{0:T(1024)(128)(2,1)S(1)}, bf16[3456]{0:T(1024)(128)(2,1)S(1)}, u32[]{:S(2)}, u32[]{:S(2)}) %collective-permute-start.26) | collective-permute-done | bytes 6944 | tf_op jit(solution)/shard_map/ppermute | solution.py:1385
  596.6 18.7 %all-to-all-start.4 = ((f32[32,1,128]{2,1,0:T(1,128)}), f32[32,1,128]{2,1,0:T(1,128)S(1)}, u32[]{:S(2)}, u32[]{:S(2)}) async-start(f32[32,1,128]{2,1,0:T(1,128)} %broadcast_in_dim.52), calls=%async_computation.4 | async-start | bytes 32768 | tf_op jit(solution)/shard_map/all_to_all | solution.py:1399
  615.4 5.6 convolution_add_fusion
  (273 shorter events, 128.1 us)
Async XLA Ops:
  8.3 13.9 %collective-permute-start.2 = (bf16[72,2304]{1,0:T(8,128)(2,1)S(1)}, bf16[72,2304]{1,0:T(8,128)(2,1)S(1)}, u32[]{:S(2)}, u32[]{:S(2)}) collective-permute-start(bf16[72,2304]{1,0:T(8,128)(2,1)S(1)} %pad_maximum_fusion.10), channel_id=1, source_target_pairs={{0,8},{1,9},{2,10},{3,11},{4,12},{5,13},{6,14},{7,15},{8,16},{9,17... | collective-permute-start | bytes 995336 | tf_op jit(solution)/shard_map/ppermute | solution.py:1107
  11.4 24.2 %collective-permute-start.3 = (bf16[72,2304]{1,0:T(8,128)(2,1)S(1)}, bf16[72,2304]{1,0:T(8,128)(2,1)S(1)}, u32[]{:S(2)}, u32[]{:S(2)}) collective-permute-start(bf16[72,2304]{1,0:T(8,128)(2,1)S(1)} %pad_maximum_fusion.10), channel_id=1, source_target_pairs={{0,16},{1,17},{2,18},{3,19},{4,20},{5,21},{6,22},{7,23},{8,24},{9,... | collective-permute-start | bytes 995336 | tf_op jit(solution)/shard_map/ppermute | solution.py:1107
  14.0 21.6 %collective-permute-start.4 = (bf16[72,2304]{1,0:T(8,128)(2,1)S(1)}, bf16[72,2304]{1,0:T(8,128)(2,1)S(1)}, u32[]{:S(2)}, u32[]{:S(2)}) collective-permute-start(bf16[72,2304]{1,0:T(8,128)(2,1)S(1)} %pad_maximum_fusion.10), channel_id=1, source_target_pairs={{0,24},{1,25},{2,26},{3,27},{4,28},{5,29},{6,30},{7,31},{8,0},{9,1... | collective-permute-start | bytes 995336 | tf_op jit(solution)/shard_map/ppermute | solution.py:1107
  17.6 26.0 %all-to-all-start = ((bf16[16,2,80]{2,1,0:T(2,128)(2,1)}), bf16[16,2,80]{2,1,0:T(2,128)(2,1)S(1)}, u32[]{:S(2)}, u32[]{:S(2)}) async-start(bf16[16,2,80]{2,1,0:T(2,128)(2,1)} %copy.50), calls=%async_computation | async-start | bytes 16384 | tf_op jit(solution)/shard_map/all_to_all | solution.py:1403
  43.6 18.0 %collective-permute-start.5 = (bf16[4,72,2304]{2,1,0:T(8,128)(2,1)}, bf16[4,72,2304]{2,1,0:T(8,128)(2,1)S(1)}, u32[]{:S(2)}, u32[]{:S(2)}) collective-permute-start(bf16[4,72,2304]{2,1,0:T(8,128)(2,1)} %pad_maximum_fusion.6), channel_id=1, source_target_pairs={{0,4},{1,5},{2,3},{3,2},{4,0},{5,1},{6,7},{7,6},{8,12},{9,13},{10,... | collective-permute-start | bytes 3981320 | tf_op jit(solution)/shard_map/ppermute | solution.py:1112
  63.3 45.5 %collective-permute-start.6 = (bf16[2,4,72,2304]{3,2,1,0:T(8,128)(2,1)S(1)}, bf16[2,4,72,2304]{3,2,1,0:T(8,128)(2,1)}, u32[]{:S(2)}, u32[]{:S(2)}) collective-permute-start(bf16[2,4,72,2304]{3,2,1,0:T(8,128)(2,1)S(1)} %pad_maximum_fusion.near_ref), channel_id=1, source_target_pairs={{0,1},{1,0},{2,6},{3,7},{4,5},{5,4},{6,2},{7,3},{8,9},{9,8},{10,14... | collective-permute-start | bytes 7962632 | tf_op jit(solution)/shard_map/ppermute | solution.py:1120
  65.7 52.2 %collective-permute-start.1 = (bf16[4,16,1656]{2,1,0:T(8,128)(2,1)}, bf16[4,16,1656]{2,1,0:T(8,128)(2,1)}, u32[]{:S(2)}, u32[]{:S(2)}) collective-permute-start(bf16[4,16,1656]{2,1,0:T(8,128)(2,1)} %pad_maximum_fusion.11), channel_id=1, source_target_pairs={{0,1},{1,0},{2,3},{3,2},{4,5},{5,4},{6,7},{7,6},{8,9},{9,8},{10,11... | collective-permute-start | bytes 635912 | tf_op jit(solution)/shard_map/ppermute | solution.py:1385
  75.6 23.8 %collective-permute-start.12 = (bf16[72,2304]{1,0:T(8,128)(2,1)}, bf16[72,2304]{1,0:T(8,128)(2,1)}, u32[]{:S(2)}, u32[]{:S(2)}) collective-permute-start(bf16[72,2304]{1,0:T(8,128)(2,1)} %concatenate.19), channel_id=1, source_target_pairs={{0,16},{1,17},{2,18},{3,19},{4,20},{5,21},{6,22},{7,23},{8,24},{9,... | collective-permute-start | bytes 995336 | tf_op jit(solution)/shard_map/ppermute | solution.py:1107
  77.2 22.2 %collective-permute-start.13 = (bf16[72,2304]{1,0:T(8,128)(2,1)}, bf16[72,2304]{1,0:T(8,128)(2,1)}, u32[]{:S(2)}, u32[]{:S(2)}) collective-permute-start(bf16[72,2304]{1,0:T(8,128)(2,1)} %concatenate.19), channel_id=1, source_target_pairs={{0,24},{1,25},{2,26},{3,27},{4,28},{5,29},{6,30},{7,31},{8,0},{9,1... | collective-permute-start | bytes 995336 | tf_op jit(solution)/shard_map/ppermute | solution.py:1107
  87.7 77.7 %collective-permute-start = (bf16[512,1152]{1,0:T(8,128)(2,1)}, bf16[512,1152]{1,0:T(8,128)(2,1)}, u32[]{:S(2)}, u32[]{:S(2)}) collective-permute-start(bf16[512,1152]{1,0:T(8,128)(2,1)} %dynamic-slice_bitcast_fusion.3), channel_id=1, source_target_pairs={{0,1},{1,0},{2,3},{3,2},{4,5},{5,4},{6,7},{7,6},{8,9},{9,8},{10,11... | collective-permute-start | bytes 3538952 | tf_op jit(solution)/shard_map/ppermute | solution.py:1385
  108.7 50.9 %collective-permute-start.17 = (bf16[4,72,2304]{2,1,0:T(8,128)(2,1)}, bf16[4,72,2304]{2,1,0:T(8,128)(2,1)}, u32[]{:S(2)}, u32[]{:S(2)}) collective-permute-start(bf16[4,72,2304]{2,1,0:T(8,128)(2,1)} %pad_maximum_fusion.7), channel_id=1, source_target_pairs={{0,4},{1,5},{2,3},{3,2},{4,0},{5,1},{6,7},{7,6},{8,12},{9,13},{10,... | collective-permute-start | bytes 3981320 | tf_op jit(solution)/shard_map/ppermute | solution.py:1112
  110.2 33.6 %all-to-all-start.1 = ((f32[32,1,3456]{2,1,0:T(1,128)}), f32[32,1,3456]{2,1,0:T(1,128)}, u32[]{:S(2)}, u32[]{:S(2)}) async-start(f32[32,1,3456]{2,1,0:T(1,128)} %copy.51), calls=%async_computation.1 | async-start | bytes 884736 | tf_op jit(solution)/shard_map/all_to_all | solution.py:1399
  119.0 31.3 %collective-permute-start.10 = (bf16[72,2304]{1,0:T(8,128)(2,1)}, bf16[72,2304]{1,0:T(8,128)(2,1)}, u32[]{:S(2)}, u32[]{:S(2)}) collective-permute-start(bf16[72,2304]{1,0:T(8,128)(2,1)} %concatenate.18), channel_id=1, source_target_pairs={{0,1},{1,0},{2,3},{3,2},{4,5},{5,4},{6,7},{7,6},{8,9},{9,8},{10,11... | collective-permute-start | bytes 995336 | tf_op jit(solution)/shard_map/ppermute | solution.py:1385
  143.8 24.7 %all-to-all-start.2 = ((bf16[16,16,1656]{2,1,0:T(8,128)(2,1)}), bf16[16,16,1656]{2,1,0:T(8,128)(2,1)S(1)}, u32[]{:S(2)}, u32[]{:S(2)}) async-start(bf16[16,16,1656]{2,1,0:T(8,128)(2,1)} %copy.63), calls=%async_computation.2 | async-start | bytes 1703936 | tf_op jit(solution)/shard_map/all_to_all | solution.py:1403
  148.3 467.1 %all-gather.2.cloned.1.call-start = ((), (), s32[]{:S(2)}) async-start(), calls=%async_computation.5 | async-start | bytes 8460288 | tf_op jit(solution)/shard_map/all_gather | solution.py:1579
  163.3 59.3 %collective-permute-start.18 = (bf16[2,4,72,2304]{3,2,1,0:T(8,128)(2,1)}, bf16[2,4,72,2304]{3,2,1,0:T(8,128)(2,1)}, u32[]{:S(2)}, u32[]{:S(2)}) collective-permute-start(bf16[2,4,72,2304]{3,2,1,0:T(8,128)(2,1)} %pad_maximum_fusion.2.near_ref), channel_id=1, source_target_pairs={{0,1},{1,0},{2,6},{3,7},{4,5},{5,4},{6,2},{7,3},{8,9},{9,8},{10,14... | collective-permute-start | bytes 7962632 | tf_op jit(solution)/shard_map/ppermute | solution.py:1120
  170.9 79.4 %collective-permute-start.7 = (bf16[2,4,72,2304]{3,2,1,0:T(8,128)(2,1)S(1)}, bf16[2,4,72,2304]{3,2,1,0:T(8,128)(2,1)}, u32[]{:S(2)}, u32[]{:S(2)}) collective-permute-start(bf16[2,4,72,2304]{3,2,1,0:T(8,128)(2,1)S(1)} %pad_maximum_fusion.near_ref), channel_id=1, source_target_pairs={{0,2},{1,3},{2,0},{3,1},{4,6},{5,7},{6,4},{7,5},{8,10},{9,11},{10,... | collective-permute-start | bytes 7962632 | tf_op jit(solution)/shard_map/ppermute | solution.py:1132
  171.0 19.9 %collective-permute-start.14 = (bf16[2,72,2304]{2,1,0:T(8,128)(2,1)}, bf16[2,72,2304]{2,1,0:T(8,128)(2,1)S(1)}, u32[]{:S(2)}, u32[]{:S(2)}) collective-permute-start(bf16[2,72,2304]{2,1,0:T(8,128)(2,1)} %pad_maximum_fusion.8), channel_id=1, source_target_pairs={{0,8},{1,9},{2,10},{3,11},{4,12},{5,13},{6,14},{7,15},{8,16},{9,17... | collective-permute-start | bytes 1990664 | tf_op jit(solution)/shard_map/ppermute | solution.py:1107
  174.8 44.1 %collective-permute-start.15 = (bf16[2,72,2304]{2,1,0:T(8,128)(2,1)S(1)}, bf16[2,72,2304]{2,1,0:T(8,128)(2,1)S(1)}, u32[]{:S(2)}, u32[]{:S(2)}) collective-permute-start(bf16[2,72,2304]{2,1,0:T(8,128)(2,1)S(1)} %copy-done.53), channel_id=1, source_target_pairs={{0,16},{1,17},{2,18},{3,19},{4,20},{5,21},{6,22},{7,23},{8,24},{9,... | collective-permute-start | bytes 1990664 | tf_op jit(solution)/shard_map/ppermute | solution.py:1107
  175.8 45.0 %collective-permute-start.16 = (bf16[2,72,2304]{2,1,0:T(8,128)(2,1)S(1)}, bf16[2,72,2304]{2,1,0:T(8,128)(2,1)S(1)}, u32[]{:S(2)}, u32[]{:S(2)}) collective-permute-start(bf16[2,72,2304]{2,1,0:T(8,128)(2,1)S(1)} %copy-done.53), channel_id=1, source_target_pairs={{0,24},{1,25},{2,26},{3,27},{4,28},{5,29},{6,30},{7,31},{8,0},{9,1... | collective-permute-start | bytes 1990664 | tf_op jit(solution)/shard_map/ppermute | solution.py:1107
  190.9 59.4 %collective-permute-start.8 = (bf16[2,4,72,2304]{3,2,1,0:T(8,128)(2,1)}, bf16[2,4,72,2304]{3,2,1,0:T(8,128)(2,1)}, u32[]{:S(2)}, u32[]{:S(2)}) collective-permute-start(bf16[2,4,72,2304]{3,2,1,0:T(8,128)(2,1)} %collective-permute-done.6.far_ref), channel_id=1, source_target_pairs={{0,2},{1,3},{2,0},{3,1},{4,6},{5,7},{6,4},{7,5},{8,10},{9,11},{10,... | collective-permute-start | bytes 7962632 | tf_op jit(solution)/shard_map/ppermute | solution.py:1132
  218.9 28.3 %collective-permute-start.9 = (bf16[512,1152]{1,0:T(8,128)(2,1)}, bf16[512,1152]{1,0:T(8,128)(2,1)}, u32[]{:S(2)}, u32[]{:S(2)}) collective-permute-start(bf16[512,1152]{1,0:T(8,128)(2,1)} %dynamic-slice_bitcast_fusion.2), channel_id=1, source_target_pairs={{0,1},{1,0},{2,3},{3,2},{4,5},{5,4},{6,7},{7,6},{8,9},{9,8},{10,11... | collective-permute-start | bytes 3538952 | tf_op jit(solution)/shard_map/ppermute | solution.py:1385
  222.6 59.7 %collective-permute-start.19 = (bf16[4,2,72,2304]{3,2,1,0:T(8,128)(2,1)}, bf16[4,2,72,2304]{3,2,1,0:T(8,128)(2,1)}, u32[]{:S(2)}, u32[]{:S(2)}) collective-permute-start(bf16[4,2,72,2304]{3,2,1,0:T(8,128)(2,1)} %pad_maximum_fusion.1.near_ref), channel_id=1, source_target_pairs={{0,4},{1,5},{2,6},{3,7},{4,0},{5,1},{6,2},{7,3},{8,12},{9,13},{10,... | collective-permute-start | bytes 7962632 | tf_op jit(solution)/shard_map/ppermute | solution.py:1128
  227.3 145.5 %collective-permute-start.20 = (bf16[4,2,72,2304]{3,2,1,0:T(8,128)(2,1)}, bf16[4,2,72,2304]{3,2,1,0:T(8,128)(2,1)}, u32[]{:S(2)}, u32[]{:S(2)}) collective-permute-start(bf16[4,2,72,2304]{3,2,1,0:T(8,128)(2,1)} %pad_maximum_fusion.1.near_ref), channel_id=1, source_target_pairs={{0,2},{1,3},{2,0},{3,1},{4,6},{5,7},{6,4},{7,5},{8,10},{9,11},{10,... | collective-permute-start | bytes 7962632 | tf_op jit(solution)/shard_map/ppermute | solution.py:1132
  250.3 75.3 %collective-permute-start.22 = (bf16[2,4,72,2304]{3,2,1,0:T(8,128)(2,1)}, bf16[2,4,72,2304]{3,2,1,0:T(8,128)(2,1)}, u32[]{:S(2)}, u32[]{:S(2)}) collective-permute-start(bf16[2,4,72,2304]{3,2,1,0:T(8,128)(2,1)} %pad_maximum_fusion.2.near_ref), channel_id=1, source_target_pairs={{0,2},{1,3},{2,0},{3,1},{4,6},{5,7},{6,4},{7,5},{8,10},{9,11},{10,... | collective-permute-start | bytes 7962632 | tf_op jit(solution)/shard_map/ppermute | solution.py:1132
  261.6 64.1 %collective-permute-start.23 = (bf16[2,4,72,2304]{3,2,1,0:T(8,128)(2,1)}, bf16[2,4,72,2304]{3,2,1,0:T(8,128)(2,1)S(1)}, u32[]{:S(2)}, u32[]{:S(2)}) collective-permute-start(bf16[2,4,72,2304]{3,2,1,0:T(8,128)(2,1)} %collective-permute-done.18.far_ref), channel_id=1, source_target_pairs={{0,2},{1,3},{2,0},{3,1},{4,6},{5,7},{6,4},{7,5},{8,10},{9,11},{10,... | collective-permute-start | bytes 7962632 | tf_op jit(solution)/shard_map/ppermute | solution.py:1132
  312.6 60.2 %collective-permute-start.21 = (bf16[4,2,72,2304]{3,2,1,0:T(8,128)(2,1)}, bf16[4,2,72,2304]{3,2,1,0:T(8,128)(2,1)}, u32[]{:S(2)}, u32[]{:S(2)}) collective-permute-start(bf16[4,2,72,2304]{3,2,1,0:T(8,128)(2,1)} %collective-permute-done.19.far_ref), channel_id=1, source_target_pairs={{0,2},{1,3},{2,0},{3,1},{4,6},{5,7},{6,4},{7,5},{8,10},{9,11},{10,... | collective-permute-start | bytes 7962632 | tf_op jit(solution)/shard_map/ppermute | solution.py:1132
  528.5 53.6 %collective-permute-start.25 = (bf16[512,1152]{1,0:T(8,128)(2,1)}, bf16[512,1152]{1,0:T(8,128)(2,1)}, u32[]{:S(2)}, u32[]{:S(2)}) collective-permute-start(bf16[512,1152]{1,0:T(8,128)(2,1)} %dynamic-slice_bitcast_fusion), channel_id=1, source_target_pairs={{0,1},{1,0},{2,3},{3,2},{4,5},{5,4},{6,7},{7,6},{8,9},{9,8},{10,11... | collective-permute-start | bytes 3538952 | tf_op jit(solution)/shard_map/ppermute | solution.py:1385
  532.7 51.5 %collective-permute-start.24 = (bf16[512,1152]{1,0:T(8,128)(2,1)}, bf16[512,1152]{1,0:T(8,128)(2,1)}, u32[]{:S(2)}, u32[]{:S(2)}) collective-permute-start(bf16[512,1152]{1,0:T(8,128)(2,1)} %dynamic-slice_bitcast_fusion.1), channel_id=1, source_target_pairs={{0,1},{1,0},{2,3},{3,2},{4,5},{5,4},{6,7},{7,6},{8,9},{9,8},{10,11... | collective-permute-start | bytes 3538952 | tf_op jit(solution)/shard_map/ppermute | solution.py:1385
  541.5 45.9 %all-to-all-start.3 = ((bf16[16,16,1656]{2,1,0:T(8,128)(2,1)}), bf16[16,16,1656]{2,1,0:T(8,128)(2,1)S(1)}, u32[]{:S(2)}, u32[]{:S(2)}) async-start(bf16[16,16,1656]{2,1,0:T(8,128)(2,1)} %get-tuple-element.122), calls=%async_computation.3 | async-start | bytes 1703936 | tf_op jit(solution)/shard_map/all_to_all | solution.py:1403
  561.0 21.0 %collective-permute-start.26 = (bf16[3456]{0:T(1024)(128)(2,1)S(1)}, bf16[3456]{0:T(1024)(128)(2,1)S(1)}, u32[]{:S(2)}, u32[]{:S(2)}) collective-permute-start(bf16[3456]{0:T(1024)(128)(2,1)S(1)} %get-tuple-element.133), channel_id=1, source_target_pairs={{0,1},{1,0},{2,3},{3,2},{4,5},{5,4},{6,7},{7,6},{8,9},{9,8},{10,11... | collective-permute-start | bytes 20744 | tf_op jit(solution)/shard_map/ppermute | solution.py:1385
  596.6 27.8 %all-to-all-start.4 = ((f32[32,1,128]{2,1,0:T(1,128)}), f32[32,1,128]{2,1,0:T(1,128)S(1)}, u32[]{:S(2)}, u32[]{:S(2)}) async-start(f32[32,1,128]{2,1,0:T(1,128)} %broadcast_in_dim.52), calls=%async_computation.4 | async-start | bytes 32768 | tf_op jit(solution)/shard_map/all_to_all | solution.py:1399
  (72 other events, 1149.7 us)
Sparse Core Ops, SparseCore 0:
  282.5 86.1 all-gather.1

commit v3 on v2

--- a/solution.py
+++ b/solution.py
@@ -522,9 +522,7 @@
     return (center * inverse, inverse)
 
 
-def assemble_kernel(
-    place_ref, near_ref, far_ref, next_near_ref, next_far_ref, out_ref, sems, *, late_x
-):
+def assemble_kernel(place_ref, near_ref, far_ref, next_near_ref, next_far_ref, out_ref, sems):
     z, x, core, y = (place_ref[i] for i in range(4))
     depth = out_ref.shape[1]
     copies = []
@@ -532,7 +530,7 @@
         source = core if side == 0 else 1 - core
         for stage, ref in enumerate(pair):
             for hop in range(2):
-                by_x = stage if late_x else jnp.where(source == 0, hop, stage)
+                by_x = jnp.where(source == 0, hop, stage)
                 by_y = hop + stage - by_x
                 for shift in range(depth):
                     target = out_ref.at[
@@ -541,19 +539,19 @@
                         lax.rem(x + by_x, 2),
                         source,
                     ]
-                    block = ref.at[shift, hop] if late_x else ref.at[hop, shift]
-                    copy = pltpu.make_async_copy(block, target, sems.at[len(copies)])
+                    copy = pltpu.make_async_copy(
+                        ref.at[hop, shift], target, sems.at[len(copies)]
+                    )
                     copy.start()
                     copies.append(copy)
     for copy in copies:
         copy.wait()
 
 
-def assemble(place, near, far, next_near, next_far, late_x):
-    rows, columns = near.shape[2:]
-    depth = near.shape[0] * near.shape[1] // 2
+def assemble(place, near, far, next_near, next_far):
+    _, depth, rows, columns = near.shape
     return pl.pallas_call(
-        functools.partial(assemble_kernel, late_x=late_x),
+        assemble_kernel,
         in_specs=[pl.BlockSpec(memory_space=pltpu.SMEM)]
         + [pl.BlockSpec(memory_space=pltpu.VMEM)] * 4,
         out_specs=pl.BlockSpec(memory_space=pl.ANY),
@@ -570,12 +568,9 @@
 def entry_kernel(
     token_ref, mod_ref, weight_ref, up_ref, down_ref, hidden_ref, middle_ref, qkv_ref, weight_aug
 ):
-    half = 3 * HALF
-
     @pl.when(pl.program_id(0) == 0)
     def _():
-        weight_aug[:MODEL_WIDTH, :half] = weight_ref[0, :, HALF:]
-        weight_aug[:MODEL_WIDTH, half:] = weight_ref[1, :, HALF:]
+        weight_aug[:MODEL_WIDTH, :] = weight_ref[...]
         weight_aug[MODEL_WIDTH:, :] = up_ref[...]
 
     normed, _ = standard(token_ref[...].astype(jnp.float32))
@@ -599,7 +594,7 @@
         in_specs=[
             rows_of((tile, MODEL_WIDTH), 0),
             once(mods.shape),
-            once(weight.shape),
+            once((MODEL_WIDTH, 3 * MODEL_WIDTH)),
             once(up.shape),
             once(down.shape),
         ],
@@ -616,7 +611,7 @@
         scratch_shapes=[pltpu.VMEM((PADDED, 3 * MODEL_WIDTH), bf16)],
         cost_estimate=pl.CostEstimate(
             flops=6 * length * MODEL_WIDTH * PADDED,
-            bytes_accessed=2 * weight.size + 12 * length * MODEL_WIDTH,
+            bytes_accessed=6 * MODEL_WIDTH * MODEL_WIDTH + 12 * length * MODEL_WIDTH,
             transcendentals=0,
         ),
         compiler_params=pltpu.CompilerParams(vmem_limit_bytes=56 * MIB),
@@ -627,8 +622,7 @@
 def load_proj(proj_aug, weight_ref, up_ref):
     @pl.when(pl.program_id(0) == 0)
     def _():
-        proj_aug[:MODEL_WIDTH, :HALF] = weight_ref[0, :, :HALF]
-        proj_aug[:MODEL_WIDTH, HALF:] = weight_ref[1, :, :HALF]
+        proj_aug[:MODEL_WIDTH, :] = weight_ref[...]
         proj_aug[MODEL_WIDTH:, :] = up_ref[...]
 
 
@@ -684,7 +678,9 @@
             rows_of((tile, MODEL_WIDTH), 0),
             rows_of((tile, MODEL_WIDTH), 0),
             once(mods.shape),
-            once((2, MODEL_WIDTH, 5 * LANES)),
+            pl.BlockSpec(
+                (MODEL_WIDTH, MODEL_WIDTH), lambda *_: (0, 3), pipeline_mode=pl.Buffered(1)
+            ),
             once(up_proj.shape),
             once(down_proj.shape),
             once(down_expand.shape),
@@ -729,17 +725,20 @@
 
 
 def feed_kernel(
-    second_ref, dfinal_ref, middle_ref, weight_ref, up_ref, down_ref, bias_ref,
+    second_ref, dfinal_ref, middle_ref, left_ref, right_ref, up_ref, down_ref, bias_ref,
     final_in_ref, dsecond_in_ref, final_ref, dsecond_ref, up_grad_ref, down_grad_ref,
     widen_aug, narrow_aug, *, rows, first, sub,
 ):
     width = MODEL_WIDTH
-    chunks = weight_ref.shape[-1] // width
+    chunks = left_ref.shape[-1] // width
     for chunk in range(chunks):
-        for side in range(2):
-            part = slice(chunk * width + side * HALF, chunk * width + (side + 1) * HALF)
-            widen_aug[:width, part] = weight_ref[side, :, chunk * width : chunk * width + HALF]
-            narrow_aug[chunk * width : (chunk + 1) * width, side * HALF : (side + 1) * HALF] = weight_ref[side, :, chunk * width + HALF : (chunk + 1) * width]
+        rows_now = slice(chunk * width, (chunk + 1) * width)
+        for side, ref in enumerate((left_ref, right_ref)):
+            at = chunk * width + side * HALF
+            widen_aug[:width, at : at + HALF] = ref[:, chunk * width : chunk * width + HALF]
+            narrow_aug[rows_now, side * HALF : (side + 1) * HALF] = ref[
+                :, chunk * width + HALF : (chunk + 1) * width
+            ]
     widen_aug[width:, :] = up_ref[...]
     narrow_aug[:, width:] = down_ref[...]
     length = second_ref.shape[0]
@@ -770,9 +769,19 @@
                 down_grad_ref[:, cols] += down_grad
 
 
+def side_of(weight, side, width):
+    if weight.ndim == 2:
+        return pl.BlockSpec(
+            (MODEL_WIDTH, width), lambda *_: (0, 2 + side), pipeline_mode=pl.Buffered(1)
+        )
+    return pl.BlockSpec(
+        (None, MODEL_WIDTH, width), lambda *_: (side, 0, 0), pipeline_mode=pl.Buffered(1)
+    )
+
+
 def feed(second, dfinal, middles, weight, up, down, bias, sums, rows=1024, sub=768):
     length, padded = second.shape
-    hidden = weight.shape[-1]
+    hidden = 2 * MODEL_WIDTH
     first = sums is None
     if first:
         sums = (jnp.zeros((8, LANES), jnp.float32),) * 2
@@ -781,7 +790,8 @@
         grid=(1,),
         in_specs=[
             once((length, padded)), once((length, padded)), once(middles.shape),
-            once(weight.shape), once(up.shape), once(down.shape), once(bias.shape),
+            *(side_of(weight, side, hidden) for side in range(2)),
+            once(up.shape), once(down.shape), once(bias.shape),
             once(sums[0].shape), once(sums[1].shape),
         ],
         out_specs=[once((length, padded)), once((length, padded)), once((RANK, hidden)), once((RANK, hidden))],
@@ -792,15 +802,15 @@
             jax.ShapeDtypeStruct((RANK, hidden), jnp.float32),
         ],
         scratch_shapes=[pltpu.VMEM((padded, hidden), jnp.bfloat16), pltpu.VMEM((hidden, padded), jnp.bfloat16)],
-        input_output_aliases={} if first else {7: 0, 8: 1},
+        input_output_aliases={} if first else {8: 0, 9: 1},
         cost_estimate=pl.CostEstimate(
             flops=8 * length * padded * hidden,
-            bytes_accessed=2 * weight.size + 12 * length * padded,
+            bytes_accessed=4 * MODEL_WIDTH * hidden + 12 * length * padded,
             transcendentals=length * hidden,
         ),
         compiler_params=pltpu.CompilerParams(vmem_limit_bytes=63 * MIB),
         name="feed",
-    )(second, dfinal, middles, weight, up, down, bias, *sums)
+    )(second, dfinal, middles, weight, weight, up, down, bias, *sums)
 
 
 def back_through(gradient, normed, inverse):
@@ -928,7 +938,9 @@
             rows_of((MODEL_WIDTH, tile), 1),
             rows_of((3, RANK, tile), 2),
             once(mods.shape),
-            once((2, MODEL_WIDTH, 5 * LANES)),
+            pl.BlockSpec(
+                (MODEL_WIDTH, MODEL_WIDTH), lambda *_: (0, 3), pipeline_mode=pl.Buffered(1)
+            ),
             once(up_proj.shape),
             once(down_proj.shape),
             once(down_expand.shape),
@@ -1000,12 +1012,9 @@
     weight_aug,
 ):
     bf16 = jnp.bfloat16
-    half = 3 * HALF
-
     @pl.when(pl.program_id(0) == 0)
     def _():
-        weight_aug[:MODEL_WIDTH, :half] = weight_ref[0, :, HALF:]
-        weight_aug[:MODEL_WIDTH, half:] = weight_ref[1, :, HALF:]
+        weight_aug[:MODEL_WIDTH, :] = weight_ref[...]
         weight_aug[MODEL_WIDTH:, :] = up_ref[...]
 
     tile = token_ref.shape[0]
@@ -1056,7 +1065,7 @@
             rows_of((tile, MODEL_WIDTH), 0),
             rows_of((tile, LANES), 0),
             once(mods.shape),
-            once(weight.shape),
+            once((MODEL_WIDTH, 3 * MODEL_WIDTH)),
             once(up.shape),
             once(down.shape),
         ],
@@ -1075,7 +1084,7 @@
         scratch_shapes=[pltpu.VMEM((PADDED, 3 * MODEL_WIDTH), bf16)],
         cost_estimate=pl.CostEstimate(
             flops=7 * length * MODEL_WIDTH * PADDED,
-            bytes_accessed=2 * weight.size + 18 * length * MODEL_WIDTH,
+            bytes_accessed=6 * MODEL_WIDTH * MODEL_WIDTH + 18 * length * MODEL_WIDTH,
             transcendentals=0,
         ),
         compiler_params=pltpu.CompilerParams(vmem_limit_bytes=60 * MIB),
@@ -1124,45 +1133,24 @@
     )
 
 
-def step_x(block, n_fsdp):
-    return lax.ppermute(block, BOTH, moved(n_fsdp, lambda z, x, c, y: (z, 1 - x, c, y)))
-
-
 def step_core(block, n_fsdp):
     return lax.ppermute(block, BOTH, moved(n_fsdp, lambda z, x, c, y: (z, x, 1 - c, y)))
 
 
 def behind(block, *earlier):
-    return lax.optimization_barrier((block, *earlier))[0]
-
-
-def complete(near, far, n_fsdp, place, late_x=False):
-    rows, columns = near.shape[2:]
-    gathered = assemble(
-        place, near, far, step_core(near, n_fsdp), step_core(far, n_fsdp), late_x
-    )
-    return gathered.reshape(2, n_fsdp * rows, columns)
-
-
-def gather_all(blocks, n_fsdp, place, told, mod_base, parts):
-    heads_block, low_block, high_block = blocks
-    heads_line = behind(step_z(heads_block, n_fsdp), told)
-    heads_near = jnp.stack([heads_line, step_first(heads_line, n_fsdp)])
-    heads_far = step_second(behind(heads_near, mod_base), n_fsdp)
-    low_line = step_z(behind(low_block, heads_line), n_fsdp)
-    low_line = behind(low_line, heads_far)
-    low_near = jnp.stack([low_line, step_first(low_line, n_fsdp)])
-    low_far = step_second(low_near, n_fsdp)
-    high_pair = jnp.stack([high_block, swap(behind(high_block, heads_line))])
-    high_near = step_z(behind(high_pair, low_line), n_fsdp)
-    high_far = step_x(behind(high_near, low_far), n_fsdp)
-    return (
-        complete(behind(heads_near, *parts), behind(heads_far, *parts), n_fsdp, place),
-        complete(low_near, low_far, n_fsdp, place),
-        complete(high_near, high_far, n_fsdp, place, True),
-        heads_far,
-        high_far,
-    )
+    for array in earlier:
+        element = lax.slice(array, [n - 1 for n in array.shape], array.shape).reshape(())
+        element = element.astype(jnp.float32)
+        block = block + jnp.minimum(jnp.abs(element), 0.0).astype(block.dtype)
+    return block
+
+
+def gather_late(block, n_fsdp, place):
+    line = step_z(block, n_fsdp)
+    near = jnp.stack([line, step_first(line, n_fsdp)])
+    far = step_second(near, n_fsdp)
+    gathered = assemble(place, near, far, step_core(near, n_fsdp), step_core(far, n_fsdp))
+    return gathered.reshape(2, n_fsdp * block.shape[0], block.shape[1])
 
 
 DOWN_EDGES = (0, 1152, 2304, 3456, 4608, 9216)
@@ -1391,8 +1379,13 @@
 
 
 def swap_rows(halves, mine):
+    kept, came = send_row(halves, mine)
+    return by_seq(kept, came, mine)
+
+
+def send_row(halves, mine):
     sent = lax.dynamic_index_in_dim(halves, 1 - mine, 0, False)
-    return by_seq(lax.dynamic_index_in_dim(halves, mine, 0, False), swap(sent), mine)
+    return lax.dynamic_index_in_dim(halves, mine, 0, False), swap(sent)
 
 
 def to_all(block):
@@ -1443,6 +1436,21 @@
     wide = jnp.moveaxis(widen_weight.reshape(depth, -1, per, HD), 2, 0).reshape(per, depth, HALF)
     narrow = narrow_weight.reshape(per, depth, HALF)
     joined = [jnp.concatenate([wide[q], narrow[q]], 1) for q in range(per)]
+    early = jnp.concatenate(
+        [query_key_value_weight, attention_out_weight, *joined[: per // 2]], 1
+    )
+    early = by_seq(early, swap(early), mine)
+    edges = (0, 3 * HALF, 4 * HALF, early.shape[2])
+    early_weight = lax.all_gather(
+        jnp.concatenate(
+            [early[side, :, edges[i] : edges[i + 1]] for i in range(3) for side in range(2)], 1
+        ),
+        "fsdp",
+        axis=0,
+        tiled=True,
+    )
+    high_weight = gather_late(jnp.concatenate(joined[per // 2 :], 1), n_fsdp, place)
+
     portions = jnp.concatenate([lowrank_down.astype(bf16), lowrank_up.astype(bf16)], -1)
     others = swap(portions)
     table = by_seq(portions, others, mine).reshape(ADAPTER_COUNT, RANK, -1)
@@ -1457,18 +1465,6 @@
     mod_part = to_all(dot("si,io->so", spoken, modulation_weight))
     mod_base = jnp.sum(mod_part.reshape(n_fsdp, MB, -1), axis=0).reshape(1, -1)
 
-    heads_weight, low_weight, high_weight, arrived, ended = gather_all(
-        (
-            jnp.concatenate([attention_out_weight, query_key_value_weight], 1),
-            jnp.concatenate(joined[: per // 2], 1),
-            jnp.concatenate(joined[per // 2 :], 1),
-        ),
-        n_fsdp,
-        place,
-        told,
-        mod_base,
-        parts,
-    )
     cond_act = lax.dynamic_slice_in_dim(cond_act_pair, mine, 1, 0)
     middle_ada = dot("ti,ri->tr", cond_act, down_ada).astype(bf16)
     modulation = mod_base + modulation_bias + dot("tr,ro->to", middle_ada, up_ada)
@@ -1476,9 +1472,9 @@
 
     length = MB * tokens.shape[1]
     token_rows = swap_rows(tokens, mine).reshape(length, MODEL_WIDTH)
-    cot_rows = swap_rows(behind(cotangent, arrived), mine).reshape(length, MODEL_WIDTH)
-
-    hidden, middle_qkv, qkv = entry(token_rows, mods, heads_weight, up_qkv, down_qkv)
+    cot_rows = swap_rows(cotangent, mine).reshape(length, MODEL_WIDTH)
+
+    hidden, middle_qkv, qkv = entry(token_rows, mods, early_weight, up_qkv, down_qkv)
     mixed_heads, log_total = heads_forward(qkv, step=length)
     mixed = mixed_heads.reshape(MODEL_WIDTH, length)
     second, dfinal, branch, middles = before_feed(
@@ -1486,7 +1482,7 @@
         token_rows,
         cot_rows,
         mods,
-        heads_weight,
+        early_weight,
         up_proj,
         down_proj,
         down_expand,
@@ -1499,7 +1495,7 @@
         second,
         dfinal,
         middles,
-        low_weight,
+        early_weight,
         up_expand[:, :cut],
         down_shrink_t[:cut],
         bias[:, :cut],
@@ -1535,7 +1531,7 @@
         mixed,
         middles,
         mods,
-        heads_weight,
+        early_weight,
         up_proj,
         down_proj,
         down_expand,
@@ -1545,7 +1541,7 @@
     block_out = swap_rows(block_rows.reshape(tokens.shape), mine)
     d_qkv = heads_back(qkv, d_mixed.reshape(HEADS, HD, length), log_total, step=length // 2)
     token_rows_grad, leave_sums, up_qkv_grad, down_qkv_grad = leave(
-        d_qkv, token_rows, d_residual, hidden, middle_qkv, mods, heads_weight, up_qkv, down_qkv
+        d_qkv, token_rows, d_residual, hidden, middle_qkv, mods, early_weight, up_qkv, down_qkv
     )
 
     sent, d_modulation, own_cond = pack(
@@ -1577,14 +1573,15 @@
     squared = to_all(jnp.broadcast_to(jnp.sum(gradient * gradient), (n_fsdp * MB, LANES)))
 
     half_weight = lax.all_gather(
-        behind(modulation_weight, ended), "fsdp", axis=0, tiled=True
-    )
-    both_mod = swap_rows(d_modulation.astype(bf16), mine)
+        behind(modulation_weight, second), "fsdp", axis=0, tiled=True
+    )
+    both_mod = behind(swap_rows(d_modulation.astype(bf16), mine), kept)
     d_cond = dot("so,io->si", both_mod, half_weight)
     d_cond = d_cond + jnp.where(jnp.arange(MB)[:, None] == mine, own_cond, 0.0)
     d_cond = d_cond + swap(d_cond)
     cond_grad = jax.vjp(jax.nn.silu, condition)[1](d_cond)[0]
-    token_grad = swap_rows(token_rows_grad.reshape(tokens.shape), mine).astype(jnp.float32)
+    token_kept, token_came = send_row(token_rows_grad.reshape(tokens.shape), mine)
+    token_grad = by_seq(behind(token_kept, gradient), token_came, mine).astype(jnp.float32)
 
     states = (
         lowrank_down,

time: 644 us -> 563 us (0.87)
  starting transfers between devices: 89.9 us -> 49.1 us
  Pallas kernels: 266 us -> 248 us
  waiting for transfers between devices: 162 us -> 149 us
  other arithmetic: 42.3 us -> 32.1 us
    all_to_all x3, waiting for transfers between devices: 6.77 us -> 63 us  [to_fsdp(): lax.all_to_all(block, 'fsdp', split_axis=0, concat_axis=0, tiled=True)]
    ppermute x9 -> x3, waiting for transfers between devices: 66.4 us -> 22.8 us  [step_z(): by_shift.append(lax.ppermute(block, BOTH, pairs))]
    all_to_all x2, waiting for transfers between devices: 21.6 us -> 0.01 us  [to_all(): lax.all_to_all(block, ('fsdp', 'seq'), split_axis=0, concat_axis=0, tiled...]
    ppermute x2 -> x1, waiting for transfers between devices: 17.4 us -> 37.7 us  [step_first(): lax.ppermute(block, BOTH, moved(n_fsdp, lambda z, x, c, y: (z, x, c, 1 -...]
    ppermute x9, waiting for transfers between devices: 42.5 us -> 25.5 us  [swap(): return lax.ppermute(block, 'seq', [(0, 1), (1, 0)])]
    pallas_call x3 -> x1, Pallas kernels: 23 us -> 7.75 us  [assemble(): pl.pallas_call(assemble_kernel, in_specs=[pl.BlockSpec(memory_space=pltpu...]
    all_to_all x2, starting transfers between devices: 25.9 us -> 12.8 us  [to_all(): lax.all_to_all(block, ('fsdp', 'seq'), split_axis=0, concat_axis=0, tiled...]
    ppermute x9 -> x3, starting transfers between devices: 18 us -> 5.79 us  [step_z(): by_shift.append(lax.ppermute(block, BOTH, pairs))]
  transfers between devices with their start and end apart: 35 -> 23, of which waited for: 13 -> 8; matrix products, arithmetic and copies ran while one was open for 12% -> 12% of each run, Pallas kernels for 42% -> 45%
where the time goes in v3:
time: 563 us; the launch traced here: 554 us
  Pallas kernels  248 us (44%)
  waiting for transfers between devices  149 us (26%)
  starting transfers between devices  49.1 us (9%)
  local copies, waits for them, and re-layouts  49 us (9%)
  other arithmetic  32.1 us (6%)
  between operations  17.4 us (3%)
  matrix products  8.82 us (2%)
    pallas_call x2, Pallas kernels, feed(): pl.pallas_call(functools.partial(feed_kernel, rows=rows, first=first, sub...  74.2 us
    all_to_all x3, waiting for transfers between devices, to_fsdp(): lax.all_to_all(block, 'fsdp', split_axis=0, concat_axis=0, tiled=True)  63 us
    pallas_call x1, Pallas kernels, heads_back(): pl.pallas_call(functools.partial(heads_back_kernel, step=step), grid=(hea...  54.9 us
    ppermute x1, waiting for transfers between devices, step_first(): lax.ppermute(block, BOTH, moved(n_fsdp, lambda z, x, c, y: (z, x, c, 1 -...  37.7 us
    pallas_call x1, Pallas kernels, heads_forward(): pl.pallas_call(functools.partial(heads_kernel, step=step), grid=(heads,),...  29.5 us
    ppermute x9, waiting for transfers between devices, swap(): return lax.ppermute(block, 'seq', [(0, 1), (1, 0)])  25.5 us
    pallas_call x1, Pallas kernels, leave(): pl.pallas_call(leave_kernel, grid=(length // tile,), in_specs=[rows_of((3...  23 us
    ppermute x3, waiting for transfers between devices, step_z(): by_shift.append(lax.ppermute(block, BOTH, pairs))  22.8 us
  transfers between devices with their start and end apart: 23, of which 8 were waited for; matrix products, arithmetic and copies ran while one was open for 12% of the time, Pallas kernels for 45%

profile of v3, /device:TPU:0, one launch (start us, length us, event | category | flops | bytes accessed | tf_op | source)
XLA Modules:
  0.0 553.6 jit_solution(13916864389006561561)
XLA Ops:
  11.6 3.0 collective-permute-start.2
  14.7 14.9 %collective-permute-done.2 = bf16[72,4608]{1,0:T(8,128)(2,1)S(1)} collective-permute-done((bf16[72,4608]{1,0:T(8,128)(2,1)S(1)}, bf16[72,4608]{1,0:T(8,128)(2,1)S(1)}, u32[]{:S(2)}, u32[]{:S(2)}) %collective-permute-start.2) | collective-permute-done | bytes 663584 | tf_op jit(solution)/shard_map/ppermute | solution.py:1373
  36.4 2.6 collective-permute-start.5
  43.6 3.5 all-to-all-start
  53.0 14.0 %collective-permute-done.5 = bf16[72,2304]{1,0:T(8,128)(2,1)} collective-permute-done((bf16[72,2304]{1,0:T(8,128)(2,1)S(1)}, bf16[72,2304]{1,0:T(8,128)(2,1)}, u32[]{:S(2)}, u32[]{:S(2)}) %collective-permute-start.5) | collective-permute-done | bytes 331808 | tf_op jit(solution)/shard_map/ppermute | solution.py:1116
  66.9 8.8 %collective-permute-done.6 = bf16[72,2304]{1,0:T(8,128)(2,1)} collective-permute-done((bf16[72,2304]{1,0:T(8,128)(2,1)S(1)}, bf16[72,2304]{1,0:T(8,128)(2,1)}, u32[]{:S(2)}, u32[]{:S(2)}) %collective-permute-start.6) | collective-permute-done | bytes 331808 | tf_op jit(solution)/shard_map/ppermute | solution.py:1116
  75.8 2.5 fusion.23
  83.4 7.1 %all-to-all-start.1 = ((f32[32,1,3456]{2,1,0:T(1,128)}), f32[32,1,3456]{2,1,0:T(1,128)}, u32[]{:S(2)}, u32[]{:S(2)}) async-start(f32[32,1,3456]{2,1,0:T(1,128)} %copy.51), calls=%async_computation.1 | async-start | bytes 884736 | tf_op jit(solution)/shard_map/all_to_all | solution.py:1392
  92.2 37.7 %collective-permute-done.7 = bf16[4,72,2304]{2,1,0:T(8,128)(2,1)} collective-permute-done((bf16[4,72,2304]{2,1,0:T(8,128)(2,1)S(1)}, bf16[4,72,2304]{2,1,0:T(8,128)(2,1)}, u32[]{:S(2)}, u32[]{:S(2)}) %collective-permute-start.7) | collective-permute-done | bytes 1327136 | tf_op jit(solution)/shard_map/ppermute | solution.py:1121
  134.6 7.4 %all-to-all-start.2 = ((bf16[16,16,1656]{2,1,0:T(8,128)(2,1)}), bf16[16,16,1656]{2,1,0:T(8,128)(2,1)S(1)}, u32[]{:S(2)}, u32[]{:S(2)}) async-start(bf16[16,16,1656]{2,1,0:T(8,128)(2,1)} %copy.63), calls=%async_computation.2 | async-start | bytes 1703936 | tf_op jit(solution)/shard_map/all_to_all | solution.py:1396
  142.1 2.8 reduce
  157.5 50.4 %all-to-all-done.2.came_ref = bf16[16,16,1656]{2,1,0:T(8,128)(2,1)S(1)} async-done(((bf16[16,16,1656]{2,1,0:T(8,128)(2,1)}), bf16[16,16,1656]{2,1,0:T(8,128)(2,1)S(1)}, u32[]{:S(2)}, u32[]{:S(2)}) %all-to-all-start.2) | async-done | bytes 847904 | tf_op jit(solution)/shard_map/all_to_all | solution.py:1396
  220.3 19.0 %entry.1 = (bf16[1024,1152]{1,0:T(8,128)(2,1)}, bf16[1024,128]{1,0:T(8,128)(2,1)}, bf16[3,16,72,1024]{3,2,1,0:T(8,128)(2,1)}) custom-call(bf16[1024,1152]{1,0:T(8,128)(2,1)} %bitcast.135, f32[8,1152]{1,0:T(8,128)} %pad.4.mod_ref, bf16[1152,9216]{1,0:T(8,128)(2,1)} %all-gather.3.cloned.1.call-done.weight_ref.left_ref.right_ref, bf16[128,3456]{1,0:T(8,128)(2,1)} %copy-done.19, ...), custom_call_target="tpu_custom_call" | custom-call | flops 9059696640 | bytes 22118400 | tf_op jit(solution)/shard_map/entry/pallas_call | solution.py:591
  239.3 29.5 %heads_forward.1 = (bf16[16,72,1024]{2,1,0:T(8,128)(2,1)S(1)}, f32[16,1,1024]{2,1,0:T(1,128)S(1)}) custom-call(bf16[3,16,72,1024]{3,2,1,0:T(8,128)(2,1)} %get-tuple-element.65.qkv_ref), custom_call_target="tpu_custom_call" | custom-call | flops 17179869184 | bytes 11796480 | tf_op jit(solution)/shard_map/heads_forward/pallas_call | solution.py:422
  269.0 12.6 %before_feed.1 = (bf16[1024,1280]{1,0:T(8,128)(2,1)}, bf16[1024,1280]{1,0:T(8,128)(2,1)}, f32[1024,1152]{1,0:T(8,128)}, bf16[3,16,1024]{2,1,0:T(8,128)(2,1)S(1)}) custom-call(bf16[1152,1024]{1,0:T(8,128)(2,1)S(1)} %bitcast.141, bf16[1024,1152]{1,0:T(8,128)(2,1)S(1)} %bitcast.138, bf16[1024,1152]{1,0:T(8,128)(2,1)} %bitcast.145, f32[8,1152]{1,0:T(8,128)S(1)} %copy-done.22, ...), custom_call_target="tpu_custom_call" | custom-call | flops 6039797760 | bytes 18874368 | tf_op jit(solution)/shard_map/before_feed/pallas_call | solution.py:673
  288.6 7.7 %assemble.1 = bf16[2,4,2,2,72,2304]{5,4,3,2,1,0:T(8,128)(2,1)S(1)} custom-call(s32[4]{0:T(128)S(1)} %copy-done.41, bf16[2,4,72,2304]{3,2,1,0:T(8,128)(2,1)S(1)} %pad_maximum_fusion.near_ref, bf16[2,4,72,2304]{3,2,1,0:T(8,128)(2,1)} %collective-permute-done.8.far_ref, bf16[2,4,72,2304]{3,2,1,0:T(8,128)(2,1)} %collective-permute-done.9.next_near_ref, ...), custom_call_target="tpu_custom_call" | custom-call | bytes 21233664 | tf_op jit(solution)/shard_map/assemble/pallas_call | solution.py:553
  296.4 3.9 copy-done.1
  300.9 35.3 %feed.2 = (f32[1024,1280]{1,0:T(8,128)}, f32[1024,1280]{1,0:T(8,128)}, f32[16,2304]{1,0:T(8,128)}, f32[16,2304]{1,0:T(8,128)}) custom-call(bf16[1024,1280]{1,0:T(8,128)(2,1)} %get-tuple-element.71.second_ref, bf16[1024,1280]{1,0:T(8,128)(2,1)} %get-tuple-element.72.dfinal_ref, bf16[3,16,1024]{2,1,0:T(8,128)(2,1)} %copy-done.34, ...), custom_call_target="tpu_custom_call" | custom-call | flops 24159191040 | bytes 26345472 | tf_op jit(solution)/shard_map/feed/pallas_call | solution.py:788
  336.2 38.8 %feed.3 = (f32[1024,1280]{1,0:T(8,128)}, f32[1024,1280]{1,0:T(8,128)}, f32[16,2304]{1,0:T(8,128)}, f32[16,2304]{1,0:T(8,128)}) custom-call(bf16[1024,1280]{1,0:T(8,128)(2,1)} %get-tuple-element.71.second_ref, bf16[1024,1280]{1,0:T(8,128)(2,1)} %get-tuple-element.72.dfinal_ref, ...), custom_call_target="tpu_custom_call", output_to_operand_aliasing={{0}: (8, {}), {1}: (9, {})} | custom-call | flops 24159191040 | bytes 26345472 | tf_op jit(solution)/shard_map/feed/pallas_call | solution.py:788
  375.0 20.8 %after_feed.1 = (bf16[1024,1152]{1,0:T(8,128)(2,1)}, f32[1024,1152]{1,0:T(8,128)}, bf16[1152,1024]{1,0:T(8,128)(2,1)}, f32[8,1152]{1,0:T(8,128)}, f32[16,1152]{1...) custom-call(f32[1024,1280]{1,0:T(8,128)} %get-tuple-element.78.final_ref, ...), custom_call_target="tpu_custom_call" | custom-call | flops 7549747200 | bytes 37748736 | tf_op jit(solution)/shard_map/after_feed/pallas_call | solution.py:927
  395.8 2.5 dynamic-slice_bitcast_fusion.1
  399.8 54.9 %heads_back.1.dqkv_ref = bf16[3,16,72,1024]{3,2,1,0:T(8,128)(2,1)} custom-call(bf16[3,16,72,1024]{3,2,1,0:T(8,128)(2,1)} %get-tuple-element.65.qkv_ref, bf16[16,72,1024]{2,1,0:T(8,128)(2,1)S(1)} %bitcast.144, f32[16,1,1024]{2,1,0:T(1,128)S(1)} %copy-done.46), custom_call_target="tpu_custom_call" | custom-call | flops 42949672960 | bytes 18874368 | tf_op jit(solution)/shard_map/heads_back/pallas_call | solution.py:476
  454.8 23.0 %leave.1 = (bf16[1024,1152]{1,0:T(8,128)(2,1)}, f32[8,1152]{1,0:T(8,128)}, f32[16,3456]{1,0:T(8,128)}, f32[16,1152]{1,0:T(8,128)}) custom-call(bf16[3,16,72,1024]{3,2,1,0:T(8,128)(2,1)} %heads_back.1.dqkv_ref, bf16[1024,1152]{1,0:T(8,128)(2,1)} %bitcast.137, f32[1024,1152]{1,0:T(8,128)} %get-tuple-element.84.dresidual_ref, ...), custom_call_target="tpu_custom_call" | custom-call | flops 10569646080 | bytes 29196288 | tf_op jit(solution)/shard_map/leave/pallas_call | solution.py:1058
  482.4 3.6 all-to-all-start.3
  490.8 2.9 fusion.2
  493.7 12.1 %all-to-all-done.3.came_ref = bf16[16,16,1656]{2,1,0:T(8,128)(2,1)S(1)} async-done(((bf16[16,16,1656]{2,1,0:T(8,128)(2,1)}), bf16[16,16,1656]{2,1,0:T(8,128)(2,1)S(1)}, u32[]{:S(2)}, u32[]{:S(2)}) %all-to-all-start.3) | async-done | bytes 847904 | tf_op jit(solution)/shard_map/all_to_all | solution.py:1396
  507.2 2.9 pad_maximum_fusion.3
  511.4 10.5 %collective-permute-done.12 = bf16[4,16,1656]{2,1,0:T(8,128)(2,1)S(1)} collective-permute-done((bf16[4,16,1656]{2,1,0:T(8,128)(2,1)S(1)}, bf16[4,16,1656]{2,1,0:T(8,128)(2,1)S(1)}, u32[]{:S(2)}, u32[]{:S(2)}) %collective-permute-start.12) | collective-permute-done | bytes 212000 | tf_op jit(solution)/shard_map/ppermute | solution.py:1373
  523.9 5.7 %all-to-all-start.4 = ((f32[32,1,128]{2,1,0:T(1,128)}), f32[32,1,128]{2,1,0:T(1,128)S(1)}, u32[]{:S(2)}, u32[]{:S(2)}) async-start(f32[32,1,128]{2,1,0:T(1,128)} %broadcast_in_dim.52), calls=%async_computation.4 | async-start | bytes 32768 | tf_op jit(solution)/shard_map/all_to_all | solution.py:1392
  530.9 2.9 fusion
  533.8 5.5 convolution_add_fusion
  541.1 2.5 maximum_convert_fusion
  (245 shorter events, 84.7 us)
Async XLA Ops:
  7.2 213.1 %all-gather.3.cloned.1.call-start = ((), (), s32[]{:S(2)}) async-start(), calls=%async_computation.5 | async-start | bytes 22560768 | tf_op jit(solution)/shard_map/all_gather | solution.py:1444
  11.6 17.9 %collective-permute-start.2 = (bf16[72,4608]{1,0:T(8,128)(2,1)S(1)}, bf16[72,4608]{1,0:T(8,128)(2,1)S(1)}, u32[]{:S(2)}, u32[]{:S(2)}) collective-permute-start(bf16[72,4608]{1,0:T(8,128)(2,1)S(1)} %concatenate.17), channel_id=1, source_target_pairs={{0,1},{1,0},{2,3},{3,2},{4,5},{5,4},{6,7},{7,6},{8,9},{9,8},{10,11... | collective-permute-start | bytes 1990664 | tf_op jit(solution)/shard_map/ppermute | solution.py:1373
  34.5 16.9 %collective-permute-start.4 = (bf16[72,2304]{1,0:T(8,128)(2,1)S(1)}, bf16[72,2304]{1,0:T(8,128)(2,1)}, u32[]{:S(2)}, u32[]{:S(2)}) collective-permute-start(bf16[72,2304]{1,0:T(8,128)(2,1)S(1)} %concatenate.19), channel_id=1, source_target_pairs={{0,8},{1,9},{2,10},{3,11},{4,12},{5,13},{6,14},{7,15},{8,16},{9,17... | collective-permute-start | bytes 995336 | tf_op jit(solution)/shard_map/ppermute | solution.py:1116
  36.4 30.5 %collective-permute-start.5 = (bf16[72,2304]{1,0:T(8,128)(2,1)S(1)}, bf16[72,2304]{1,0:T(8,128)(2,1)}, u32[]{:S(2)}, u32[]{:S(2)}) collective-permute-start(bf16[72,2304]{1,0:T(8,128)(2,1)S(1)} %concatenate.19), channel_id=1, source_target_pairs={{0,16},{1,17},{2,18},{3,19},{4,20},{5,21},{6,22},{7,23},{8,24},{9,... | collective-permute-start | bytes 995336 | tf_op jit(solution)/shard_map/ppermute | solution.py:1116
  39.0 36.8 %collective-permute-start.6 = (bf16[72,2304]{1,0:T(8,128)(2,1)S(1)}, bf16[72,2304]{1,0:T(8,128)(2,1)}, u32[]{:S(2)}, u32[]{:S(2)}) collective-permute-start(bf16[72,2304]{1,0:T(8,128)(2,1)S(1)} %concatenate.19), channel_id=1, source_target_pairs={{0,24},{1,25},{2,26},{3,27},{4,28},{5,29},{6,30},{7,31},{8,0},{9,1... | collective-permute-start | bytes 995336 | tf_op jit(solution)/shard_map/ppermute | solution.py:1116
  41.2 49.8 %collective-permute-start.1 = (bf16[4,16,1656]{2,1,0:T(8,128)(2,1)}, bf16[4,16,1656]{2,1,0:T(8,128)(2,1)}, u32[]{:S(2)}, u32[]{:S(2)}) collective-permute-start(bf16[4,16,1656]{2,1,0:T(8,128)(2,1)} %pad_maximum_fusion.6), channel_id=1, source_target_pairs={{0,1},{1,0},{2,3},{3,2},{4,5},{5,4},{6,7},{7,6},{8,9},{9,8},{10,11... | collective-permute-start | bytes 635912 | tf_op jit(solution)/shard_map/ppermute | solution.py:1373
  42.7 37.5 %copy-start.56 = (bf16[2,1152]{1,0:T(2,128)(2,1)}, bf16[2,1152]{1,0:T(2,128)(2,1)S(1)}, u32[]{:S(2)}) copy-start(bf16[2,1152]{1,0:T(2,128)(2,1)S(1)} %multiply_convert_fusion) | copy-start | bytes 13828
  43.6 38.4 %all-to-all-start = ((bf16[16,2,80]{2,1,0:T(2,128)(2,1)}), bf16[16,2,80]{2,1,0:T(2,128)(2,1)S(1)}, u32[]{:S(2)}, u32[]{:S(2)}) async-start(bf16[16,2,80]{2,1,0:T(2,128)(2,1)} %copy.50), calls=%async_computation | async-start | bytes 16384 | tf_op jit(solution)/shard_map/all_to_all | solution.py:1396
  48.3 101.1 %collective-permute-start = (bf16[512,1152]{1,0:T(8,128)(2,1)}, bf16[512,1152]{1,0:T(8,128)(2,1)}, u32[]{:S(2)}, u32[]{:S(2)}) collective-permute-start(bf16[512,1152]{1,0:T(8,128)(2,1)} %dynamic-slice_bitcast_fusion.3), channel_id=1, source_target_pairs={{0,1},{1,0},{2,3},{3,2},{4,5},{5,4},{6,7},{7,6},{8,9},{9,8},{10,11... | collective-permute-start | bytes 3538952 | tf_op jit(solution)/shard_map/ppermute | solution.py:1373
  51.4 101.5 %collective-permute-start.3 = (bf16[512,1152]{1,0:T(8,128)(2,1)}, bf16[512,1152]{1,0:T(8,128)(2,1)}, u32[]{:S(2)}, u32[]{:S(2)}) collective-permute-start(bf16[512,1152]{1,0:T(8,128)(2,1)} %dynamic-slice_bitcast_fusion.2), channel_id=1, source_target_pairs={{0,1},{1,0},{2,3},{3,2},{4,5},{5,4},{6,7},{7,6},{8,9},{9,8},{10,11... | collective-permute-start | bytes 3538952 | tf_op jit(solution)/shard_map/ppermute | solution.py:1373
  78.3 51.6 %collective-permute-start.7 = (bf16[4,72,2304]{2,1,0:T(8,128)(2,1)S(1)}, bf16[4,72,2304]{2,1,0:T(8,128)(2,1)}, u32[]{:S(2)}, u32[]{:S(2)}) collective-permute-start(bf16[4,72,2304]{2,1,0:T(8,128)(2,1)S(1)} %get-tuple-element.125), channel_id=1, source_target_pairs={{0,4},{1,5},{2,3},{3,2},{4,0},{5,1},{6,7},{7,6},{8,12},{9,13},{10,... | collective-permute-start | bytes 3981320 | tf_op jit(solution)/shard_map/ppermute | solution.py:1121
  83.4 51.2 %all-to-all-start.1 = ((f32[32,1,3456]{2,1,0:T(1,128)}), f32[32,1,3456]{2,1,0:T(1,128)}, u32[]{:S(2)}, u32[]{:S(2)}) async-start(f32[32,1,3456]{2,1,0:T(1,128)} %copy.51), calls=%async_computation.1 | async-start | bytes 884736 | tf_op jit(solution)/shard_map/all_to_all | solution.py:1392
  90.5 39.4 %copy-start.47 = (bf16[1,4,72,2304]{3,2,1,0:T(8,128)(2,1)S(1)}, bf16[1,4,72,2304]{3,2,1,0:T(8,128)(2,1)}, u32[]{:S(2)}) copy-start(bf16[1,4,72,2304]{3,2,1,0:T(8,128)(2,1)} %get-tuple-element.124) | copy-start | bytes 3981316
  91.0 42.1 %copy-start.42 = (s32[16]{0:T(128)}, s32[16]{0:T(128)S(1)}, u32[]{:S(2)}) copy-start(s32[16]{0:T(128)S(1)} %convert_reduce_fusion.ids_ref) | copy-start | bytes 196
  131.5 88.8 %collective-permute-start.8 = (bf16[2,4,72,2304]{3,2,1,0:T(8,128)(2,1)S(1)}, bf16[2,4,72,2304]{3,2,1,0:T(8,128)(2,1)}, u32[]{:S(2)}, u32[]{:S(2)}) collective-permute-start(bf16[2,4,72,2304]{3,2,1,0:T(8,128)(2,1)S(1)} %pad_maximum_fusion.near_ref), channel_id=1, source_target_pairs={{0,1},{1,0},{2,6},{3,7},{4,5},{5,4},{6,2},{7,3},{8,9},{9,8},{10,14... | collective-permute-start | bytes 7962632 | tf_op jit(solution)/shard_map/ppermute | solution.py:1129
  134.6 73.3 %all-to-all-start.2 = ((bf16[16,16,1656]{2,1,0:T(8,128)(2,1)}), bf16[16,16,1656]{2,1,0:T(8,128)(2,1)S(1)}, u32[]{:S(2)}, u32[]{:S(2)}) async-start(bf16[16,16,1656]{2,1,0:T(8,128)(2,1)} %copy.63), calls=%async_computation.2 | async-start | bytes 1703936 | tf_op jit(solution)/shard_map/all_to_all | solution.py:1396
  142.0 391.7 %all-gather.5.cloned.1.call-start = ((), (), s32[]{:S(2)}) async-start(), calls=%async_computation.6 | async-start | bytes 8460288 | tf_op jit(solution)/shard_map/all_gather | solution.py:1575
  157.1 131.5 %collective-permute-start.9 = (bf16[2,4,72,2304]{3,2,1,0:T(8,128)(2,1)S(1)}, bf16[2,4,72,2304]{3,2,1,0:T(8,128)(2,1)}, u32[]{:S(2)}, u32[]{:S(2)}) collective-permute-start(bf16[2,4,72,2304]{3,2,1,0:T(8,128)(2,1)S(1)} %pad_maximum_fusion.near_ref), channel_id=1, source_target_pairs={{0,2},{1,3},{2,0},{3,1},{4,6},{5,7},{6,4},{7,5},{8,10},{9,11},{10,... | collective-permute-start | bytes 7962632 | tf_op jit(solution)/shard_map/ppermute | solution.py:1137
  220.3 68.3 %collective-permute-start.10 = (bf16[2,4,72,2304]{3,2,1,0:T(8,128)(2,1)}, bf16[2,4,72,2304]{3,2,1,0:T(8,128)(2,1)}, u32[]{:S(2)}, u32[]{:S(2)}) collective-permute-start(bf16[2,4,72,2304]{3,2,1,0:T(8,128)(2,1)} %collective-permute-done.8.far_ref), channel_id=1, source_target_pairs={{0,2},{1,3},{2,0},{3,1},{4,6},{5,7},{6,4},{7,5},{8,10},{9,11},{10,... | collective-permute-start | bytes 7962632 | tf_op jit(solution)/shard_map/ppermute | solution.py:1137
  239.3 29.6 %copy-start = (bf16[2,512,1152]{2,1,0:T(8,128)(2,1)S(1)}, bf16[2,512,1152]{2,1,0:T(8,128)(2,1)}, u32[]{:S(2)}) copy-start(bf16[2,512,1152]{2,1,0:T(8,128)(2,1)} %pad_maximum_fusion.1) | copy-start | bytes 7077892
  239.3 29.6 %copy-start.12 = (bf16[128,1152]{1,0:T(8,128)(2,1)S(1)}, bf16[128,1152]{1,0:T(8,128)(2,1)}, u32[]{:S(2)}) copy-start(bf16[128,1152]{1,0:T(8,128)(2,1)} %copy-done.11) | copy-start | bytes 884740
  239.3 29.6 %copy-start.14 = (bf16[128,1152]{1,0:T(8,128)(2,1)S(1)}, bf16[128,1152]{1,0:T(8,128)(2,1)}, u32[]{:S(2)}) copy-start(bf16[128,1152]{1,0:T(8,128)(2,1)} %copy-done.13) | copy-start | bytes 884740
  239.3 29.6 %copy-start.16 = (bf16[128,1152]{1,0:T(8,128)(2,1)S(1)}, bf16[128,1152]{1,0:T(8,128)(2,1)}, u32[]{:S(2)}) copy-start(bf16[128,1152]{1,0:T(8,128)(2,1)} %copy-done.15) | copy-start | bytes 884740
  239.3 29.6 %copy-start.18 = (bf16[128,1152]{1,0:T(8,128)(2,1)S(1)}, bf16[128,1152]{1,0:T(8,128)(2,1)}, u32[]{:S(2)}) copy-start(bf16[128,1152]{1,0:T(8,128)(2,1)} %copy-done.17) | copy-start | bytes 884740
  239.3 29.6 %copy-start.22 = (f32[8,1152]{1,0:T(8,128)S(1)}, f32[8,1152]{1,0:T(8,128)}, u32[]{:S(2)}) copy-start(f32[8,1152]{1,0:T(8,128)} %pad.4.mod_ref) | copy-start | bytes 110596
  398.4 92.4 %collective-permute-start.11 = (bf16[512,1152]{1,0:T(8,128)(2,1)}, bf16[512,1152]{1,0:T(8,128)(2,1)}, u32[]{:S(2)}, u32[]{:S(2)}) collective-permute-start(bf16[512,1152]{1,0:T(8,128)(2,1)} %dynamic-slice_bitcast_fusion.1), channel_id=1, source_target_pairs={{0,1},{1,0},{2,3},{3,2},{4,5},{5,4},{6,7},{7,6},{8,9},{9,8},{10,11... | collective-permute-start | bytes 3538952 | tf_op jit(solution)/shard_map/ppermute | solution.py:1373
  482.4 23.4 %all-to-all-start.3 = ((bf16[16,16,1656]{2,1,0:T(8,128)(2,1)}), bf16[16,16,1656]{2,1,0:T(8,128)(2,1)S(1)}, u32[]{:S(2)}, u32[]{:S(2)}) async-start(bf16[16,16,1656]{2,1,0:T(8,128)(2,1)} %get-tuple-element.100), calls=%async_computation.3 | async-start | bytes 1703936 | tf_op jit(solution)/shard_map/all_to_all | solution.py:1396
  486.2 4.6 collective-permute-start.14
  489.2 41.6 %collective-permute-start.13 = (bf16[512,1152]{1,0:T(8,128)(2,1)}, bf16[512,1152]{1,0:T(8,128)(2,1)}, u32[]{:S(2)}, u32[]{:S(2)}) collective-permute-start(bf16[512,1152]{1,0:T(8,128)(2,1)} %dynamic-slice_bitcast_fusion), channel_id=1, source_target_pairs={{0,1},{1,0},{2,3},{3,2},{4,5},{5,4},{6,7},{7,6},{8,9},{9,8},{10,11... | collective-permute-start | bytes 3538952 | tf_op jit(solution)/shard_map/ppermute | solution.py:1373
  506.6 15.4 %collective-permute-start.12 = (bf16[4,16,1656]{2,1,0:T(8,128)(2,1)S(1)}, bf16[4,16,1656]{2,1,0:T(8,128)(2,1)S(1)}, u32[]{:S(2)}, u32[]{:S(2)}) collective-permute-start(bf16[4,16,1656]{2,1,0:T(8,128)(2,1)S(1)} %get-tuple-element.102), channel_id=1, source_target_pairs={{0,1},{1,0},{2,3},{3,2},{4,5},{5,4},{6,7},{7,6},{8,9},{9,8},{10,11... | collective-permute-start | bytes 635912 | tf_op jit(solution)/shard_map/ppermute | solution.py:1373
  523.9 19.7 %all-to-all-start.4 = ((f32[32,1,128]{2,1,0:T(1,128)}), f32[32,1,128]{2,1,0:T(1,128)S(1)}, u32[]{:S(2)}, u32[]{:S(2)}) async-start(f32[32,1,128]{2,1,0:T(1,128)} %broadcast_in_dim.52), calls=%async_computation.4 | async-start | bytes 32768 | tf_op jit(solution)/shard_map/all_to_all | solution.py:1392
  539.3 6.4 %collective-permute-start.15 = (f32[2,1152]{1,0:T(2,128)S(1)}, f32[2,1152]{1,0:T(2,128)S(1)}, u32[]{:S(2)}, u32[]{:S(2)}) collective-permute-start(f32[2,1152]{1,0:T(2,128)S(1)} %convolution_add_fusion), channel_id=1, source_target_pairs={{0,1},{1,0},{2,3},{3,2},{4,5},{5,4},{6,7},{7,6},{8,9},{9,8},{10,11... | collective-permute-start | bytes 27656 | tf_op jit(solution)/shard_map/ppermute | solution.py:1373
  (57 other events, 501.3 us)
Sparse Core Ops, SparseCore 0:
  32.0 170.1 all-gather.2
  285.1 70.7 all-gather.4

commit v4 on v3

--- a/solution.py
+++ b/solution.py
@@ -441,7 +441,9 @@
     )(qkv)
 
 
-def heads_back_kernel(qkv_ref, grad_ref, log_ref, out_ref, key_acc, value_acc, *, step):
+def heads_back_kernel(
+    qkv_ref, grad_ref, mixed_ref, log_ref, out_ref, key_acc, value_acc, *, step
+):
     length = qkv_ref.shape[-1]
     keys_t = qkv_ref[1, 0]
     keys = keys_t.astype(jnp.float32).T.astype(jnp.bfloat16)
@@ -454,7 +456,11 @@
         scores = nn(keys, queries_t) * (SCORE_SCALE * LOG2E)
         probable = jnp.exp2(scores - log_ref[0, :, start : start + step])
         d_weights = nn(values, grad_t)
-        inner_sum = jnp.sum(d_weights * probable, axis=0, keepdims=True)
+        inner_sum = jnp.sum(
+            grad_t.astype(jnp.float32) * mixed_ref[0, :, start : start + step].astype(jnp.float32),
+            axis=0,
+            keepdims=True,
+        )
         d_scores = (probable * (d_weights - inner_sum)).astype(jnp.bfloat16)
         d_values = nn(probable.astype(jnp.bfloat16), grad)
         d_keys = nn(d_scores, queries)
@@ -471,7 +477,7 @@
     out_ref[2, 0] = value_acc[...].T.astype(jnp.bfloat16)
 
 
-def heads_back(qkv, grad, log_total, step=256):
+def heads_back(qkv, grad, mixed, log_total, step=256):
     _, heads, width, length = qkv.shape
     return pl.pallas_call(
         functools.partial(heads_back_kernel, step=step),
@@ -479,6 +485,7 @@
         in_specs=[
             pl.BlockSpec((3, 1, width, length), lambda h: (0, h, 0, 0)),
             pl.BlockSpec((1, width, length), lambda h: (h, 0, 0)),
+            pl.BlockSpec((1, width, length), lambda h: (h, 0, 0)),
             pl.BlockSpec((1, 1, length), lambda h: (h, 0, 0)),
         ],
         out_specs=pl.BlockSpec((3, 1, width, length), lambda h: (0, h, 0, 0)),
@@ -492,9 +499,9 @@
             bytes_accessed=16 * heads * width * length,
             transcendentals=heads * length * length,
         ),
-        compiler_params=pltpu.CompilerParams(vmem_limit_bytes=48 * 1024 * 1024),
+        compiler_params=pltpu.CompilerParams(vmem_limit_bytes=60 * 1024 * 1024),
         name="heads_back",
-    )(qkv, grad, log_total)
+    )(qkv, grad, mixed, log_total)
 
 
 RANK = ADAPTER_RANK
@@ -611,7 +618,7 @@
         scratch_shapes=[pltpu.VMEM((PADDED, 3 * MODEL_WIDTH), bf16)],
         cost_estimate=pl.CostEstimate(
             flops=6 * length * MODEL_WIDTH * PADDED,
-            bytes_accessed=6 * MODEL_WIDTH * MODEL_WIDTH + 12 * length * MODEL_WIDTH,
+            bytes_accessed=2 * weight.size + 12 * length * MODEL_WIDTH,
             transcendentals=0,
         ),
         compiler_params=pltpu.CompilerParams(vmem_limit_bytes=56 * MIB),
@@ -769,10 +776,11 @@
                 down_grad_ref[:, cols] += down_grad
 
 
-def side_of(weight, side, width):
+def side_of(weight, side):
+    width = weight.size // (2 * MODEL_WIDTH)
     if weight.ndim == 2:
         return pl.BlockSpec(
-            (MODEL_WIDTH, width), lambda *_: (0, 2 + side), pipeline_mode=pl.Buffered(1)
+            (MODEL_WIDTH, width), lambda *_: (0, side), pipeline_mode=pl.Buffered(1)
         )
     return pl.BlockSpec(
         (None, MODEL_WIDTH, width), lambda *_: (side, 0, 0), pipeline_mode=pl.Buffered(1)
@@ -781,7 +789,7 @@
 
 def feed(second, dfinal, middles, weight, up, down, bias, sums, rows=1024, sub=768):
     length, padded = second.shape
-    hidden = 2 * MODEL_WIDTH
+    hidden = weight.size // (2 * MODEL_WIDTH)
     first = sums is None
     if first:
         sums = (jnp.zeros((8, LANES), jnp.float32),) * 2
@@ -790,7 +798,7 @@
         grid=(1,),
         in_specs=[
             once((length, padded)), once((length, padded)), once(middles.shape),
-            *(side_of(weight, side, hidden) for side in range(2)),
+            *(side_of(weight, side) for side in range(2)),
             once(up.shape), once(down.shape), once(bias.shape),
             once(sums[0].shape), once(sums[1].shape),
         ],
@@ -805,7 +813,7 @@
         input_output_aliases={} if first else {8: 0, 9: 1},
         cost_estimate=pl.CostEstimate(
             flops=8 * length * padded * hidden,
-            bytes_accessed=4 * MODEL_WIDTH * hidden + 12 * length * padded,
+            bytes_accessed=weight.size + 12 * length * padded,
             transcendentals=length * hidden,
         ),
         compiler_params=pltpu.CompilerParams(vmem_limit_bytes=63 * MIB),
@@ -1084,7 +1092,7 @@
         scratch_shapes=[pltpu.VMEM((PADDED, 3 * MODEL_WIDTH), bf16)],
         cost_estimate=pl.CostEstimate(
             flops=7 * length * MODEL_WIDTH * PADDED,
-            bytes_accessed=6 * MODEL_WIDTH * MODEL_WIDTH + 18 * length * MODEL_WIDTH,
+            bytes_accessed=2 * weight.size + 18 * length * MODEL_WIDTH,
             transcendentals=0,
         ),
         compiler_params=pltpu.CompilerParams(vmem_limit_bytes=60 * MIB),
@@ -1435,20 +1443,20 @@
 
     wide = jnp.moveaxis(widen_weight.reshape(depth, -1, per, HD), 2, 0).reshape(per, depth, HALF)
     narrow = narrow_weight.reshape(per, depth, HALF)
+
+    def whole(block):
+        return lax.all_gather(block, "fsdp", axis=0, tiled=True)
+
+    heads = jnp.concatenate([query_key_value_weight, attention_out_weight], 1)
+    heads = by_seq(heads, swap(heads), mine)
+    cut = query_key_value_weight.shape[1]
+    heads_weight = whole(
+        jnp.concatenate([heads[0, :, :cut], heads[1, :, :cut], heads[0, :, cut:], heads[1, :, cut:]], 1)
+    )
     joined = [jnp.concatenate([wide[q], narrow[q]], 1) for q in range(per)]
-    early = jnp.concatenate(
-        [query_key_value_weight, attention_out_weight, *joined[: per // 2]], 1
-    )
-    early = by_seq(early, swap(early), mine)
-    edges = (0, 3 * HALF, 4 * HALF, early.shape[2])
-    early_weight = lax.all_gather(
-        jnp.concatenate(
-            [early[side, :, edges[i] : edges[i + 1]] for i in range(3) for side in range(2)], 1
-        ),
-        "fsdp",
-        axis=0,
-        tiled=True,
-    )
+    low = jnp.concatenate(joined[: per // 2], 1)
+    low = by_seq(low, swap(low), mine)
+    low_weight = whole(jnp.concatenate([low[0], low[1]], 1))
     high_weight = gather_late(jnp.concatenate(joined[per // 2 :], 1), n_fsdp, place)
 
     portions = jnp.concatenate([lowrank_down.astype(bf16), lowrank_up.astype(bf16)], -1)
@@ -1474,7 +1482,7 @@
     token_rows = swap_rows(tokens, mine).reshape(length, MODEL_WIDTH)
     cot_rows = swap_rows(cotangent, mine).reshape(length, MODEL_WIDTH)
 
-    hidden, middle_qkv, qkv = entry(token_rows, mods, early_weight, up_qkv, down_qkv)
+    hidden, middle_qkv, qkv = entry(token_rows, mods, heads_weight, up_qkv, down_qkv)
     mixed_heads, log_total = heads_forward(qkv, step=length)
     mixed = mixed_heads.reshape(MODEL_WIDTH, length)
     second, dfinal, branch, middles = before_feed(
@@ -1482,7 +1490,7 @@
         token_rows,
         cot_rows,
         mods,
-        early_weight,
+        heads_weight,
         up_proj,
         down_proj,
         down_expand,
@@ -1495,7 +1503,7 @@
         second,
         dfinal,
         middles,
-        early_weight,
+        low_weight,
         up_expand[:, :cut],
         down_shrink_t[:cut],
         bias[:, :cut],
@@ -1531,7 +1539,7 @@
         mixed,
         middles,
         mods,
-        early_weight,
+        heads_weight,
         up_proj,
         down_proj,
         down_expand,
@@ -1539,9 +1547,11 @@
         narrow_bias[None],
     )
     block_out = swap_rows(block_rows.reshape(tokens.shape), mine)
-    d_qkv = heads_back(qkv, d_mixed.reshape(HEADS, HD, length), log_total, step=length // 2)
+    d_qkv = heads_back(
+        qkv, d_mixed.reshape(HEADS, HD, length), mixed_heads, log_total, step=length
+    )
     token_rows_grad, leave_sums, up_qkv_grad, down_qkv_grad = leave(
-        d_qkv, token_rows, d_residual, hidden, middle_qkv, mods, early_weight, up_qkv, down_qkv
+        d_qkv, token_rows, d_residual, hidden, middle_qkv, mods, heads_weight, up_qkv, down_qkv
     )
 
     sent, d_modulation, own_cond = pack(

time: 563 us -> 522 us (0.927)
  waiting for transfers between devices: 149 us -> 106 us
  starting transfers between devices: 49.1 us -> 61.5 us
  Pallas kernels: 248 us -> 240 us
    all_to_all x3, waiting for transfers between devices: 63 us -> 23.4 us  [to_fsdp(): lax.all_to_all(block, 'fsdp', split_axis=0, concat_axis=0, tiled=True)]
    all_to_all x3, starting transfers between devices: 14.5 us -> 24.9 us  [to_fsdp(): lax.all_to_all(block, 'fsdp', split_axis=0, concat_axis=0, tiled=True)]
    pallas_call x1, Pallas kernels: 54.9 us -> 47.1 us  [heads_back(): pl.pallas_call(functools.partial(heads_back_kernel, step=step), grid=(hea...]
    ppermute x1, waiting for transfers between devices: 37.7 us -> 32 us  [step_first(): lax.ppermute(block, BOTH, moved(n_fsdp, lambda z, x, c, y: (z, x, c, 1 -...]
    ppermute x9 -> x10, starting transfers between devices: 12.6 us -> 14.3 us  [swap(): return lax.ppermute(block, 'seq', [(0, 1), (1, 0)])]
    ppermute x9 -> x10, waiting for transfers between devices: 25.5 us -> 27 us  [swap(): return lax.ppermute(block, 'seq', [(0, 1), (1, 0)])]
    unnamed x132 -> x122, local copies, waits for them, and re-layouts: 15.5 us -> 15.5 us
  transfers between devices with their start and end apart: 23 -> 25, of which waited for: 8 -> 9; matrix products, arithmetic and copies ran while one was open for 12% -> 13% of each run, Pallas kernels for 45% -> 47%
where the time goes in v4:
time: 522 us; the launch traced here: 513 us
  Pallas kernels  240 us (46%)
  waiting for transfers between devices  106 us (20%)
  starting transfers between devices  61.5 us (12%)
  local copies, waits for them, and re-layouts  47.2 us (9%)
  other arithmetic  32.2 us (6%)
  between operations  17.1 us (3%)
  matrix products  8.84 us (2%)
    pallas_call x2, Pallas kernels, feed(): pl.pallas_call(functools.partial(feed_kernel, rows=rows, first=first, sub...  73.9 us
    pallas_call x1, Pallas kernels, heads_back(): pl.pallas_call(functools.partial(heads_back_kernel, step=step), grid=(hea...  47.1 us
    ppermute x1, waiting for transfers between devices, step_first(): lax.ppermute(block, BOTH, moved(n_fsdp, lambda z, x, c, y: (z, x, c, 1 -...  32 us
    pallas_call x1, Pallas kernels, heads_forward(): pl.pallas_call(functools.partial(heads_kernel, step=step), grid=(heads,),...  29.5 us
    ppermute x10, waiting for transfers between devices, swap(): return lax.ppermute(block, 'seq', [(0, 1), (1, 0)])  27 us
    all_to_all x3, starting transfers between devices, to_fsdp(): lax.all_to_all(block, 'fsdp', split_axis=0, concat_axis=0, tiled=True)  24.9 us
    all_to_all x3, waiting for transfers between devices, to_fsdp(): lax.all_to_all(block, 'fsdp', split_axis=0, concat_axis=0, tiled=True)  23.4 us
    pallas_call x1, Pallas kernels, leave(): pl.pallas_call(leave_kernel, grid=(length // tile,), in_specs=[rows_of((3...  23.3 us
  transfers between devices with their start and end apart: 25, of which 9 were waited for; matrix products, arithmetic and copies ran while one was open for 13% of the time, Pallas kernels for 47%

profile of v4, /device:TPU:0, one launch (start us, length us, event | category | flops | bytes accessed | tf_op | source)
XLA Modules:
  0.0 512.5 jit_solution(11787880882242092101)
XLA Ops:
  8.3 3.0 collective-permute-start.2
  11.3 7.8 %collective-permute-done.2 = bf16[72,2304]{1,0:T(8,128)(2,1)S(1)} collective-permute-done((bf16[72,2304]{1,0:T(8,128)(2,1)S(1)}, bf16[72,2304]{1,0:T(8,128)(2,1)S(1)}, u32[]{:S(2)}, u32[]{:S(2)}) %collective-permute-start.2) | collective-permute-done | bytes 331808 | tf_op jit(solution)/shard_map/ppermute | solution.py:1381
  26.3 7.2 %collective-permute-done.11 = bf16[72,2304]{1,0:T(8,128)(2,1)S(1)} collective-permute-done((bf16[72,2304]{1,0:T(8,128)(2,1)S(1)}, bf16[72,2304]{1,0:T(8,128)(2,1)S(1)}, u32[]{:S(2)}, u32[]{:S(2)}) %collective-permute-start.11) | collective-permute-done | bytes 331808 | tf_op jit(solution)/shard_map/ppermute | solution.py:1381
  38.9 2.6 collective-permute-start.5
  46.1 3.5 all-to-all-start
  53.8 3.2 collective-permute-done.4
  58.4 20.0 %collective-permute-done.5 = bf16[72,2304]{1,0:T(8,128)(2,1)} collective-permute-done((bf16[72,2304]{1,0:T(8,128)(2,1)S(1)}, bf16[72,2304]{1,0:T(8,128)(2,1)}, u32[]{:S(2)}, u32[]{:S(2)}) %collective-permute-start.5) | collective-permute-done | bytes 331808 | tf_op jit(solution)/shard_map/ppermute | solution.py:1124
  78.5 2.5 fusion.23
  88.1 8.1 %all-to-all-start.1 = ((f32[32,1,3456]{2,1,0:T(1,128)}), f32[32,1,3456]{2,1,0:T(1,128)}, u32[]{:S(2)}, u32[]{:S(2)}) async-start(f32[32,1,3456]{2,1,0:T(1,128)} %copy.51), calls=%async_computation.1 | async-start | bytes 884736 | tf_op jit(solution)/shard_map/all_to_all | solution.py:1400
  97.8 32.0 %collective-permute-done.7 = bf16[4,72,2304]{2,1,0:T(8,128)(2,1)} collective-permute-done((bf16[4,72,2304]{2,1,0:T(8,128)(2,1)S(1)}, bf16[4,72,2304]{2,1,0:T(8,128)(2,1)}, u32[]{:S(2)}, u32[]{:S(2)}) %collective-permute-start.7) | collective-permute-done | bytes 1327136 | tf_op jit(solution)/shard_map/ppermute | solution.py:1129
  134.0 12.1 %all-to-all-start.2 = ((bf16[16,16,1656]{2,1,0:T(8,128)(2,1)}), bf16[16,16,1656]{2,1,0:T(8,128)(2,1)S(1)}, u32[]{:S(2)}, u32[]{:S(2)}) async-start(bf16[16,16,1656]{2,1,0:T(8,128)(2,1)} %copy.63), calls=%async_computation.2 | async-start | bytes 1703936 | tf_op jit(solution)/shard_map/all_to_all | solution.py:1404
  146.2 2.8 reduce
  161.6 7.9 %all-to-all-done.2.came_ref = bf16[16,16,1656]{2,1,0:T(8,128)(2,1)S(1)} async-done(((bf16[16,16,1656]{2,1,0:T(8,128)(2,1)}), bf16[16,16,1656]{2,1,0:T(8,128)(2,1)S(1)}, u32[]{:S(2)}, u32[]{:S(2)}) %all-to-all-start.2) | async-done | bytes 847904 | tf_op jit(solution)/shard_map/all_to_all | solution.py:1404
  182.0 18.9 %entry.1 = (bf16[1024,1152]{1,0:T(8,128)(2,1)}, bf16[1024,128]{1,0:T(8,128)(2,1)}, bf16[3,16,72,1024]{3,2,1,0:T(8,128)(2,1)}) custom-call(bf16[1024,1152]{1,0:T(8,128)(2,1)} %bitcast.133, f32[8,1152]{1,0:T(8,128)} %pad.4.mod_ref, bf16[1152,4608]{1,0:T(8,128)(2,1)} %all-gather.4.cloned.1.call-done.weight_ref, bf16[128,3456]{1,0:T(8,128)(2,1)} %copy-done.42, ...), custom_call_target="tpu_custom_call" | custom-call | flops 9059696640 | bytes 24772608 | tf_op jit(solution)/shard_map/entry/pallas_call | solution.py:598
  200.9 29.5 %heads_forward.1 = (bf16[16,72,1024]{2,1,0:T(8,128)(2,1)S(1)}, f32[16,1,1024]{2,1,0:T(1,128)S(1)}) custom-call(bf16[3,16,72,1024]{3,2,1,0:T(8,128)(2,1)} %get-tuple-element.65.qkv_ref), custom_call_target="tpu_custom_call" | custom-call | flops 17179869184 | bytes 11796480 | tf_op jit(solution)/shard_map/heads_forward/pallas_call | solution.py:422
  230.6 12.6 %before_feed.1 = (bf16[1024,1280]{1,0:T(8,128)(2,1)}, bf16[1024,1280]{1,0:T(8,128)(2,1)}, f32[1024,1152]{1,0:T(8,128)}, bf16[3,16,1024]{2,1,0:T(8,128)(2,1)S(1)}) custom-call(bf16[1152,1024]{1,0:T(8,128)(2,1)S(1)} %bitcast.137, bf16[1024,1152]{1,0:T(8,128)(2,1)S(1)} %bitcast.136, bf16[1024,1152]{1,0:T(8,128)(2,1)} %bitcast.140, f32[8,1152]{1,0:T(8,128)S(1)} %copy-done.27, ...), custom_call_target="tpu_custom_call" | custom-call | flops 6039797760 | bytes 18874368 | tf_op jit(solution)/shard_map/before_feed/pallas_call | solution.py:680
  246.7 2.4 fusion.24
  250.2 7.5 %assemble.1 = bf16[2,4,2,2,72,2304]{5,4,3,2,1,0:T(8,128)(2,1)S(1)} custom-call(s32[4]{0:T(128)S(1)} %pad_add_fusion.place_ref, bf16[2,4,72,2304]{3,2,1,0:T(8,128)(2,1)S(1)} %pad_maximum_fusion.near_ref, bf16[2,4,72,2304]{3,2,1,0:T(8,128)(2,1)} %collective-permute-done.8.far_ref, bf16[2,4,72,2304]{3,2,1,0:T(8,128)(2,1)} %collective-permute-done.9.next_near_ref, ...), custom_call_target="tpu_custom_call" | custom-call | bytes 21233664 | tf_op jit(solution)/shard_map/assemble/pallas_call | solution.py:560
  257.7 3.9 copy-done
  262.2 35.3 %feed.2 = (f32[1024,1280]{1,0:T(8,128)}, f32[1024,1280]{1,0:T(8,128)}, f32[16,2304]{1,0:T(8,128)}, f32[16,2304]{1,0:T(8,128)}) custom-call(bf16[1024,1280]{1,0:T(8,128)(2,1)} %get-tuple-element.71.second_ref, bf16[1024,1280]{1,0:T(8,128)(2,1)} %get-tuple-element.72.dfinal_ref, bf16[3,16,1024]{2,1,0:T(8,128)(2,1)} %copy-done.32, ...), custom_call_target="tpu_custom_call" | custom-call | flops 24159191040 | bytes 21037056 | tf_op jit(solution)/shard_map/feed/pallas_call | solution.py:796
  297.5 38.6 %feed.3 = (f32[1024,1280]{1,0:T(8,128)}, f32[1024,1280]{1,0:T(8,128)}, f32[16,2304]{1,0:T(8,128)}, f32[16,2304]{1,0:T(8,128)}) custom-call(bf16[1024,1280]{1,0:T(8,128)(2,1)} %get-tuple-element.71.second_ref, bf16[1024,1280]{1,0:T(8,128)(2,1)} %get-tuple-element.72.dfinal_ref, ...), custom_call_target="tpu_custom_call", output_to_operand_aliasing={{0}: (8, {}), {1}: (9, {})} | custom-call | flops 24159191040 | bytes 21037056 | tf_op jit(solution)/shard_map/feed/pallas_call | solution.py:796
  336.1 20.8 %after_feed.1 = (bf16[1024,1152]{1,0:T(8,128)(2,1)}, f32[1024,1152]{1,0:T(8,128)}, bf16[1152,1024]{1,0:T(8,128)(2,1)}, f32[8,1152]{1,0:T(8,128)}, f32[16,1152]{1...) custom-call(f32[1024,1280]{1,0:T(8,128)} %get-tuple-element.78.final_ref, ...), custom_call_target="tpu_custom_call" | custom-call | flops 7549747200 | bytes 37748736 | tf_op jit(solution)/shard_map/after_feed/pallas_call | solution.py:935
  356.9 2.4 dynamic-slice_bitcast_fusion.1
  360.8 47.1 %heads_back.1.dqkv_ref = bf16[3,16,72,1024]{3,2,1,0:T(8,128)(2,1)} custom-call(bf16[3,16,72,1024]{3,2,1,0:T(8,128)(2,1)} %get-tuple-element.65.qkv_ref, bf16[16,72,1024]{2,1,0:T(8,128)(2,1)} %bitcast.153, bf16[16,72,1024]{2,1,0:T(8,128)(2,1)} %copy-done.3, f32[16,1,1024]{2,1,0:T(1,128)} %copy-done.44), custom_call_target="tpu_custom_call" | custom-call | flops 42949672960 | bytes 18874368 | tf_op jit(solution)/shard_map/heads_back/pallas_call | solution.py:482
  408.0 23.3 %leave.1 = (bf16[1024,1152]{1,0:T(8,128)(2,1)}, f32[8,1152]{1,0:T(8,128)}, f32[16,3456]{1,0:T(8,128)}, f32[16,1152]{1,0:T(8,128)}) custom-call(bf16[3,16,72,1024]{3,2,1,0:T(8,128)(2,1)} %heads_back.1.dqkv_ref, bf16[1024,1152]{1,0:T(8,128)(2,1)} %bitcast.135, f32[1024,1152]{1,0:T(8,128)} %get-tuple-element.84.dresidual_ref, ...), custom_call_target="tpu_custom_call" | custom-call | flops 10569646080 | bytes 31850496 | tf_op jit(solution)/shard_map/leave/pallas_call | solution.py:1066
  435.9 9.3 %all-to-all-start.3 = ((bf16[16,16,1656]{2,1,0:T(8,128)(2,1)}), bf16[16,16,1656]{2,1,0:T(8,128)(2,1)S(1)}, u32[]{:S(2)}, u32[]{:S(2)}) async-start(bf16[16,16,1656]{2,1,0:T(8,128)(2,1)} %get-tuple-element.100), calls=%async_computation.3 | async-start | bytes 1703936 | tf_op jit(solution)/shard_map/all_to_all | solution.py:1404
  451.8 13.1 %all-to-all-done.3.came_ref = bf16[16,16,1656]{2,1,0:T(8,128)(2,1)S(1)} async-done(((bf16[16,16,1656]{2,1,0:T(8,128)(2,1)}), bf16[16,16,1656]{2,1,0:T(8,128)(2,1)S(1)}, u32[]{:S(2)}, u32[]{:S(2)}) %all-to-all-start.3) | async-done | bytes 847904 | tf_op jit(solution)/shard_map/all_to_all | solution.py:1404
  469.3 11.9 %collective-permute-done.13 = bf16[4,16,1656]{2,1,0:T(8,128)(2,1)S(1)} collective-permute-done((bf16[4,16,1656]{2,1,0:T(8,128)(2,1)S(1)}, bf16[4,16,1656]{2,1,0:T(8,128)(2,1)S(1)}, u32[]{:S(2)}, u32[]{:S(2)}) %collective-permute-start.13) | collective-permute-done | bytes 212000 | tf_op jit(solution)/shard_map/ppermute | solution.py:1381
  483.2 5.6 %all-to-all-start.4 = ((f32[32,1,128]{2,1,0:T(1,128)}), f32[32,1,128]{2,1,0:T(1,128)S(1)}, u32[]{:S(2)}, u32[]{:S(2)}) async-start(f32[32,1,128]{2,1,0:T(1,128)} %broadcast_in_dim.52), calls=%async_computation.4 | async-start | bytes 32768 | tf_op jit(solution)/shard_map/all_to_all | solution.py:1400
  490.1 2.9 fusion
  493.0 5.5 %convolution_add_fusion = f32[2,1152]{1,0:T(2,128)S(1)} fusion(bf16[1152,3456]{1,0:T(8,128)(2,1)} %all-gather.8.cloned.1.call-done, bf16[1,3456]{1,0:T(2,128)(2,1)S(1)} %stack.130, bf16[1,3456]{1,0:T(2,128)(2,1)S(1)} %stack.129, pred[2]{0:T(512)(128)(4,1)S(1)} %iota_compare_fusion.1, bf16[]{:T(256)} %bitcast.53, f32[1152]{0:T(1024)S(1)} %reduce.5), kind=kOutput, calls=%fused_computation.6 | convolution fusion | flops 15971328 | bytes 7990276 | tf_op jit(solution)/shard_map/so,io->si/dot_general | solution.py:1377
  500.3 2.5 maximum_convert_fusion
  (242 shorter events, 89.5 us)
Async XLA Ops:
  7.2 174.8 %all-gather.4.cloned.1.call-start = ((), (), s32[]{:S(2)}) async-start(), calls=%async_computation.5 | async-start | bytes 11280384 | tf_op jit(solution)/shard_map/all_gather | solution.py:1448
  8.3 10.8 %collective-permute-start.2 = (bf16[72,2304]{1,0:T(8,128)(2,1)S(1)}, bf16[72,2304]{1,0:T(8,128)(2,1)S(1)}, u32[]{:S(2)}, u32[]{:S(2)}) collective-permute-start(bf16[72,2304]{1,0:T(8,128)(2,1)S(1)} %pad_maximum_fusion.7), channel_id=1, source_target_pairs={{0,1},{1,0},{2,3},{3,2},{4,5},{5,4},{6,7},{7,6},{8,9},{9,8},{10,11... | collective-permute-start | bytes 995336 | tf_op jit(solution)/shard_map/ppermute | solution.py:1381
  22.0 239.6 %all-gather.6.cloned.1.call-start = ((), (), s32[]{:S(2)}) async-start(), calls=%async_computation.6 | async-start | bytes 11280384 | tf_op jit(solution)/shard_map/all_gather | solution.py:1448
  24.5 9.1 %collective-permute-start.11 = (bf16[72,2304]{1,0:T(8,128)(2,1)S(1)}, bf16[72,2304]{1,0:T(8,128)(2,1)S(1)}, u32[]{:S(2)}, u32[]{:S(2)}) collective-permute-start(bf16[72,2304]{1,0:T(8,128)(2,1)S(1)} %concatenate.26), channel_id=1, source_target_pairs={{0,1},{1,0},{2,3},{3,2},{4,5},{5,4},{6,7},{7,6},{8,9},{9,8},{10,11... | collective-permute-start | bytes 995336 | tf_op jit(solution)/shard_map/ppermute | solution.py:1381
  37.3 19.7 %collective-permute-start.4 = (bf16[72,2304]{1,0:T(8,128)(2,1)S(1)}, bf16[72,2304]{1,0:T(8,128)(2,1)}, u32[]{:S(2)}, u32[]{:S(2)}) collective-permute-start(bf16[72,2304]{1,0:T(8,128)(2,1)S(1)} %concatenate.25), channel_id=1, source_target_pairs={{0,8},{1,9},{2,10},{3,11},{4,12},{5,13},{6,14},{7,15},{8,16},{9,17... | collective-permute-start | bytes 995336 | tf_op jit(solution)/shard_map/ppermute | solution.py:1124
  38.9 39.6 %collective-permute-start.5 = (bf16[72,2304]{1,0:T(8,128)(2,1)S(1)}, bf16[72,2304]{1,0:T(8,128)(2,1)}, u32[]{:S(2)}, u32[]{:S(2)}) collective-permute-start(bf16[72,2304]{1,0:T(8,128)(2,1)S(1)} %concatenate.25), channel_id=1, source_target_pairs={{0,16},{1,17},{2,18},{3,19},{4,20},{5,21},{6,22},{7,23},{8,24},{9,... | collective-permute-start | bytes 995336 | tf_op jit(solution)/shard_map/ppermute | solution.py:1124
  41.4 37.0 %collective-permute-start.6 = (bf16[72,2304]{1,0:T(8,128)(2,1)S(1)}, bf16[72,2304]{1,0:T(8,128)(2,1)}, u32[]{:S(2)}, u32[]{:S(2)}) collective-permute-start(bf16[72,2304]{1,0:T(8,128)(2,1)S(1)} %concatenate.25), channel_id=1, source_target_pairs={{0,24},{1,25},{2,26},{3,27},{4,28},{5,29},{6,30},{7,31},{8,0},{9,1... | collective-permute-start | bytes 995336 | tf_op jit(solution)/shard_map/ppermute | solution.py:1124
  43.6 53.0 %collective-permute-start.1 = (bf16[4,16,1656]{2,1,0:T(8,128)(2,1)}, bf16[4,16,1656]{2,1,0:T(8,128)(2,1)}, u32[]{:S(2)}, u32[]{:S(2)}) collective-permute-start(bf16[4,16,1656]{2,1,0:T(8,128)(2,1)} %pad_maximum_fusion.8), channel_id=1, source_target_pairs={{0,1},{1,0},{2,3},{3,2},{4,5},{5,4},{6,7},{7,6},{8,9},{9,8},{10,11... | collective-permute-start | bytes 635912 | tf_op jit(solution)/shard_map/ppermute | solution.py:1381
  45.2 37.8 %copy-start.53 = (bf16[2,1152]{1,0:T(2,128)(2,1)}, bf16[2,1152]{1,0:T(2,128)(2,1)S(1)}, u32[]{:S(2)}) copy-start(bf16[2,1152]{1,0:T(2,128)(2,1)S(1)} %multiply_convert_fusion) | copy-start | bytes 13828
  46.1 40.6 %all-to-all-start = ((bf16[16,2,80]{2,1,0:T(2,128)(2,1)}), bf16[16,2,80]{2,1,0:T(2,128)(2,1)S(1)}, u32[]{:S(2)}, u32[]{:S(2)}) async-start(bf16[16,2,80]{2,1,0:T(2,128)(2,1)} %copy.50), calls=%async_computation | async-start | bytes 16384 | tf_op jit(solution)/shard_map/all_to_all | solution.py:1404
  50.7 103.0 %collective-permute-start = (bf16[512,1152]{1,0:T(8,128)(2,1)}, bf16[512,1152]{1,0:T(8,128)(2,1)}, u32[]{:S(2)}, u32[]{:S(2)}) collective-permute-start(bf16[512,1152]{1,0:T(8,128)(2,1)} %dynamic-slice_bitcast_fusion.3), channel_id=1, source_target_pairs={{0,1},{1,0},{2,3},{3,2},{4,5},{5,4},{6,7},{7,6},{8,9},{9,8},{10,11... | collective-permute-start | bytes 3538952 | tf_op jit(solution)/shard_map/ppermute | solution.py:1381
  57.0 100.1 %collective-permute-start.3 = (bf16[512,1152]{1,0:T(8,128)(2,1)}, bf16[512,1152]{1,0:T(8,128)(2,1)}, u32[]{:S(2)}, u32[]{:S(2)}) collective-permute-start(bf16[512,1152]{1,0:T(8,128)(2,1)} %dynamic-slice_bitcast_fusion.2), channel_id=1, source_target_pairs={{0,1},{1,0},{2,3},{3,2},{4,5},{5,4},{6,7},{7,6},{8,9},{9,8},{10,11... | collective-permute-start | bytes 3538952 | tf_op jit(solution)/shard_map/ppermute | solution.py:1381
  81.0 48.8 %collective-permute-start.7 = (bf16[4,72,2304]{2,1,0:T(8,128)(2,1)S(1)}, bf16[4,72,2304]{2,1,0:T(8,128)(2,1)}, u32[]{:S(2)}, u32[]{:S(2)}) collective-permute-start(bf16[4,72,2304]{2,1,0:T(8,128)(2,1)S(1)} %get-tuple-element.125), channel_id=1, source_target_pairs={{0,4},{1,5},{2,3},{3,2},{4,0},{5,1},{6,7},{7,6},{8,12},{9,13},{10,... | collective-permute-start | bytes 3981320 | tf_op jit(solution)/shard_map/ppermute | solution.py:1129
  88.1 45.9 %all-to-all-start.1 = ((f32[32,1,3456]{2,1,0:T(1,128)}), f32[32,1,3456]{2,1,0:T(1,128)}, u32[]{:S(2)}, u32[]{:S(2)}) async-start(f32[32,1,3456]{2,1,0:T(1,128)} %copy.51), calls=%async_computation.1 | async-start | bytes 884736 | tf_op jit(solution)/shard_map/all_to_all | solution.py:1400
  96.2 33.6 %copy-start.45 = (bf16[1,4,72,2304]{3,2,1,0:T(8,128)(2,1)S(1)}, bf16[1,4,72,2304]{3,2,1,0:T(8,128)(2,1)}, u32[]{:S(2)}) copy-start(bf16[1,4,72,2304]{3,2,1,0:T(8,128)(2,1)} %get-tuple-element.124) | copy-start | bytes 3981316
  96.6 35.9 %copy-start.40 = (s32[16]{0:T(128)}, s32[16]{0:T(128)S(1)}, u32[]{:S(2)}) copy-start(s32[16]{0:T(128)S(1)} %convert_reduce_fusion.ids_ref) | copy-start | bytes 196
  131.3 50.5 %collective-permute-start.8 = (bf16[2,4,72,2304]{3,2,1,0:T(8,128)(2,1)S(1)}, bf16[2,4,72,2304]{3,2,1,0:T(8,128)(2,1)}, u32[]{:S(2)}, u32[]{:S(2)}) collective-permute-start(bf16[2,4,72,2304]{3,2,1,0:T(8,128)(2,1)S(1)} %pad_maximum_fusion.near_ref), channel_id=1, source_target_pairs={{0,1},{1,0},{2,6},{3,7},{4,5},{5,4},{6,2},{7,3},{8,9},{9,8},{10,14... | collective-permute-start | bytes 7962632 | tf_op jit(solution)/shard_map/ppermute | solution.py:1137
  134.0 35.5 %all-to-all-start.2 = ((bf16[16,16,1656]{2,1,0:T(8,128)(2,1)}), bf16[16,16,1656]{2,1,0:T(8,128)(2,1)S(1)}, u32[]{:S(2)}, u32[]{:S(2)}) async-start(bf16[16,16,1656]{2,1,0:T(8,128)(2,1)} %copy.63), calls=%async_computation.2 | async-start | bytes 1703936 | tf_op jit(solution)/shard_map/all_to_all | solution.py:1404
  146.2 346.8 %all-gather.8.cloned.1.call-start = ((), (), s32[]{:S(2)}) async-start(), calls=%async_computation.7 | async-start | bytes 8460288 | tf_op jit(solution)/shard_map/all_gather | solution.py:1585
  161.3 88.9 %collective-permute-start.9 = (bf16[2,4,72,2304]{3,2,1,0:T(8,128)(2,1)S(1)}, bf16[2,4,72,2304]{3,2,1,0:T(8,128)(2,1)}, u32[]{:S(2)}, u32[]{:S(2)}) collective-permute-start(bf16[2,4,72,2304]{3,2,1,0:T(8,128)(2,1)S(1)} %pad_maximum_fusion.near_ref), channel_id=1, source_target_pairs={{0,2},{1,3},{2,0},{3,1},{4,6},{5,7},{6,4},{7,5},{8,10},{9,11},{10,... | collective-permute-start | bytes 7962632 | tf_op jit(solution)/shard_map/ppermute | solution.py:1145
  181.9 68.3 %collective-permute-start.10 = (bf16[2,4,72,2304]{3,2,1,0:T(8,128)(2,1)}, bf16[2,4,72,2304]{3,2,1,0:T(8,128)(2,1)}, u32[]{:S(2)}, u32[]{:S(2)}) collective-permute-start(bf16[2,4,72,2304]{3,2,1,0:T(8,128)(2,1)} %collective-permute-done.8.far_ref), channel_id=1, source_target_pairs={{0,2},{1,3},{2,0},{3,1},{4,6},{5,7},{6,4},{7,5},{8,10},{9,11},{10,... | collective-permute-start | bytes 7962632 | tf_op jit(solution)/shard_map/ppermute | solution.py:1145
  200.9 29.6 %copy-start.19 = (bf16[128,1152]{1,0:T(8,128)(2,1)S(1)}, bf16[128,1152]{1,0:T(8,128)(2,1)}, u32[]{:S(2)}) copy-start(bf16[128,1152]{1,0:T(8,128)(2,1)} %copy-done.18) | copy-start | bytes 884740
  200.9 29.6 %copy-start.21 = (bf16[128,1152]{1,0:T(8,128)(2,1)S(1)}, bf16[128,1152]{1,0:T(8,128)(2,1)}, u32[]{:S(2)}) copy-start(bf16[128,1152]{1,0:T(8,128)(2,1)} %copy-done.20) | copy-start | bytes 884740
  200.9 29.6 %copy-start.23 = (bf16[128,1152]{1,0:T(8,128)(2,1)S(1)}, bf16[128,1152]{1,0:T(8,128)(2,1)}, u32[]{:S(2)}) copy-start(bf16[128,1152]{1,0:T(8,128)(2,1)} %copy-done.22) | copy-start | bytes 884740
  200.9 29.6 %copy-start.27 = (f32[8,1152]{1,0:T(8,128)S(1)}, f32[8,1152]{1,0:T(8,128)}, u32[]{:S(2)}) copy-start(f32[8,1152]{1,0:T(8,128)} %pad.4.mod_ref) | copy-start | bytes 110596
  359.4 90.6 %collective-permute-start.12 = (bf16[512,1152]{1,0:T(8,128)(2,1)}, bf16[512,1152]{1,0:T(8,128)(2,1)}, u32[]{:S(2)}, u32[]{:S(2)}) collective-permute-start(bf16[512,1152]{1,0:T(8,128)(2,1)} %dynamic-slice_bitcast_fusion.1), channel_id=1, source_target_pairs={{0,1},{1,0},{2,3},{3,2},{4,5},{5,4},{6,7},{7,6},{8,9},{9,8},{10,11... | collective-permute-start | bytes 3538952 | tf_op jit(solution)/shard_map/ppermute | solution.py:1381
  435.9 29.1 %all-to-all-start.3 = ((bf16[16,16,1656]{2,1,0:T(8,128)(2,1)}), bf16[16,16,1656]{2,1,0:T(8,128)(2,1)S(1)}, u32[]{:S(2)}, u32[]{:S(2)}) async-start(bf16[16,16,1656]{2,1,0:T(8,128)(2,1)} %get-tuple-element.100), calls=%async_computation.3 | async-start | bytes 1703936 | tf_op jit(solution)/shard_map/all_to_all | solution.py:1404
  445.3 4.6 collective-permute-start.15
  448.4 41.7 %collective-permute-start.14 = (bf16[512,1152]{1,0:T(8,128)(2,1)}, bf16[512,1152]{1,0:T(8,128)(2,1)}, u32[]{:S(2)}, u32[]{:S(2)}) collective-permute-start(bf16[512,1152]{1,0:T(8,128)(2,1)} %dynamic-slice_bitcast_fusion), channel_id=1, source_target_pairs={{0,1},{1,0},{2,3},{3,2},{4,5},{5,4},{6,7},{7,6},{8,9},{9,8},{10,11... | collective-permute-start | bytes 3538952 | tf_op jit(solution)/shard_map/ppermute | solution.py:1381
  465.8 15.5 %collective-permute-start.13 = (bf16[4,16,1656]{2,1,0:T(8,128)(2,1)S(1)}, bf16[4,16,1656]{2,1,0:T(8,128)(2,1)S(1)}, u32[]{:S(2)}, u32[]{:S(2)}) collective-permute-start(bf16[4,16,1656]{2,1,0:T(8,128)(2,1)S(1)} %get-tuple-element.102), channel_id=1, source_target_pairs={{0,1},{1,0},{2,3},{3,2},{4,5},{5,4},{6,7},{7,6},{8,9},{9,8},{10,11... | collective-permute-start | bytes 635912 | tf_op jit(solution)/shard_map/ppermute | solution.py:1381
  483.2 19.6 %all-to-all-start.4 = ((f32[32,1,128]{2,1,0:T(1,128)}), f32[32,1,128]{2,1,0:T(1,128)S(1)}, u32[]{:S(2)}, u32[]{:S(2)}) async-start(f32[32,1,128]{2,1,0:T(1,128)} %broadcast_in_dim.52), calls=%async_computation.4 | async-start | bytes 32768 | tf_op jit(solution)/shard_map/all_to_all | solution.py:1400
  498.5 6.4 %collective-permute-start.16 = (f32[2,1152]{1,0:T(2,128)S(1)}, f32[2,1152]{1,0:T(2,128)S(1)}, u32[]{:S(2)}, u32[]{:S(2)}) collective-permute-start(f32[2,1152]{1,0:T(2,128)S(1)} %convolution_add_fusion), channel_id=1, source_target_pairs={{0,1},{1,0},{2,3},{3,2},{4,5},{5,4},{6,7},{7,6},{8,9},{9,8},{10,11... | collective-permute-start | bytes 27656 | tf_op jit(solution)/shard_map/ppermute | solution.py:1381
  (54 other events, 539.7 us)
Sparse Core Ops, SparseCore 0:
  22.1 136.4 all-gather.3
  160.8 87.0 all-gather.5
  250.1 73.0 all-gather.7

commit v5 on v4

--- a/solution.py
+++ b/solution.py
@@ -1153,8 +1153,8 @@
     return block
 
 
-def gather_late(block, n_fsdp, place):
-    line = step_z(block, n_fsdp)
+def gather_late(block, n_fsdp, place, told):
+    line = behind(step_z(block, n_fsdp), told)
     near = jnp.stack([line, step_first(line, n_fsdp)])
     far = step_second(near, n_fsdp)
     gathered = assemble(place, near, far, step_core(near, n_fsdp), step_core(far, n_fsdp))
@@ -1171,14 +1171,21 @@
     return [f * per + q for q in range(per) for f in range(n_fsdp)]
 
 
-def unpack_kernel(came_ref, *refs, order, down_chunk, up_chunk):
+def unpack_kernel(came_ref, cond_ref, base_ref, *refs, order, down_chunk, up_chunk):
     bf16 = jnp.bfloat16
     outs, (down_all, up_all, mixed) = refs[:-3], refs[-3:]
-    down_outs, up_outs, shrink_t = outs[:4], outs[4:9], outs[9]
+    down_outs, up_outs, shrink_t, mod_ref, middle_ref = outs[:4], outs[4:9], *outs[9:]
     for f in range(came_ref.shape[0]):
         block = came_ref[f].astype(jnp.float32)
         down_all[:, f * down_chunk : (f + 1) * down_chunk] = block[:, :down_chunk]
         up_all[:, f * up_chunk : (f + 1) * up_chunk] = block[:, down_chunk:]
+    middle = jnp.sum(down_all[:, :MODEL_WIDTH] * cond_ref[...], axis=1, keepdims=True)
+    middle = middle.astype(bf16).astype(jnp.float32)
+    middle_ref[...] = middle
+    mod_ref[...] = jnp.zeros_like(mod_ref)
+    for block in range(6):
+        columns = slice(block * MODEL_WIDTH, (block + 1) * MODEL_WIDTH)
+        mod_ref[block : block + 1] = base_ref[:, columns] + total(middle * up_all[:, columns])
     for target, out in enumerate(down_outs):
         out[...] = jnp.zeros_like(out)
         out[:RANK] = down_all[:, DOWN_EDGES[target] : DOWN_EDGES[target + 1]].astype(bf16)
@@ -1201,7 +1208,7 @@
         )
 
 
-def unpack(came, order, down_chunk, up_chunk):
+def unpack(came, cond, base, order, down_chunk, up_chunk):
     bf16 = jnp.bfloat16
     widths = [DOWN_EDGES[t + 1] - DOWN_EDGES[t] for t in range(4)]
     widths += [UP_EDGES[t + 1] - UP_EDGES[t] for t in range(5)]
@@ -1210,7 +1217,11 @@
             unpack_kernel, order=order, down_chunk=down_chunk, up_chunk=up_chunk
         ),
         out_shape=[jax.ShapeDtypeStruct((LANES, w), bf16) for w in widths]
-        + [jax.ShapeDtypeStruct((FF, LANES), bf16)],
+        + [
+            jax.ShapeDtypeStruct((FF, LANES), bf16),
+            jax.ShapeDtypeStruct((8, MODEL_WIDTH), jnp.float32),
+            jax.ShapeDtypeStruct((RANK, 1), jnp.float32),
+        ],
         scratch_shapes=[
             pltpu.VMEM((RANK, DOWN_EDGES[5]), jnp.float32),
             pltpu.VMEM((RANK, UP_EDGES[5]), jnp.float32),
@@ -1218,7 +1229,7 @@
         ],
         compiler_params=pltpu.CompilerParams(vmem_limit_bytes=48 * MIB),
         name="unpack",
-    )(came)
+    )(came, cond, base)
 
 
 def pack_kernel(
@@ -1457,26 +1468,23 @@
     low = jnp.concatenate(joined[: per // 2], 1)
     low = by_seq(low, swap(low), mine)
     low_weight = whole(jnp.concatenate([low[0], low[1]], 1))
-    high_weight = gather_late(jnp.concatenate(joined[per // 2 :], 1), n_fsdp, place)
+    high_weight = gather_late(jnp.concatenate(joined[per // 2 :], 1), n_fsdp, place, told)
 
     portions = jnp.concatenate([lowrank_down.astype(bf16), lowrank_up.astype(bf16)], -1)
     others = swap(portions)
     table = by_seq(portions, others, mine).reshape(ADAPTER_COUNT, RANK, -1)
     picks = jax.nn.one_hot(own_ids, ADAPTER_COUNT, dtype=bf16)
     chosen = dot("fa,arc->frc", picks, table).astype(bf16)
-    parts = unpack(to_fsdp(chosen), order, down_chunk, up_chunk)
-    down_ada, down_qkv, down_proj, down_expand = parts[:4]
-    up_ada, up_qkv, up_proj, up_expand, up_shrink = parts[4:9]
-    down_shrink_t = parts[9]
-
     spoken = told[:, :, :depth].reshape(n_fsdp * MB, depth)
     mod_part = to_all(dot("si,io->so", spoken, modulation_weight))
     mod_base = jnp.sum(mod_part.reshape(n_fsdp, MB, -1), axis=0).reshape(1, -1)
-
-    cond_act = lax.dynamic_slice_in_dim(cond_act_pair, mine, 1, 0)
-    middle_ada = dot("ti,ri->tr", cond_act, down_ada).astype(bf16)
-    modulation = mod_base + modulation_bias + dot("tr,ro->to", middle_ada, up_ada)
-    mods = jnp.pad(modulation.reshape(6, MODEL_WIDTH), ((0, 2), (0, 0)))
+    cond_act = lax.dynamic_slice_in_dim(cond_act_pair, mine, 1, 0).astype(jnp.float32)
+    parts = unpack(
+        to_fsdp(chosen), cond_act, mod_base + modulation_bias, order, down_chunk, up_chunk
+    )
+    down_ada, down_qkv, down_proj, down_expand = parts[:4]
+    up_ada, up_qkv, up_proj, up_expand, up_shrink = parts[4:9]
+    down_shrink_t, mods, middle_ada = parts[9:]
 
     length = MB * tokens.shape[1]
     token_rows = swap_rows(tokens, mine).reshape(length, MODEL_WIDTH)
@@ -1558,8 +1566,8 @@
         (
             leave_sums,
             after_sums,
-            middle_ada[:, :RANK].astype(jnp.float32).T,
-            cond_act.astype(jnp.float32),
+            middle_ada,
+            cond_act,
             down_ada,
             up_ada,
             down_qkv_grad,

time: 522 us -> 564 us (1.080)
  waiting for transfers between devices: 106 us -> 152 us
  starting transfers between devices: 61.5 us -> 54.2 us
    all_to_all x3, waiting for transfers between devices: 23.4 us -> 63.6 us  [to_fsdp(): lax.all_to_all(block, 'fsdp', split_axis=0, concat_axis=0, tiled=True)]
    all_to_all x2, waiting for transfers between devices: 0.01 us -> 29.8 us  [to_all(): lax.all_to_all(block, ('fsdp', 'seq'), split_axis=0, concat_axis=0, tiled...]
    ppermute x3, waiting for transfers between devices: 23.2 us -> 0.01 us  [step_z(): by_shift.append(lax.ppermute(block, BOTH, pairs))]
    unnamed x122 -> x150, local copies, waits for them, and re-layouts: 15.5 us -> 19.4 us
  transfers between devices with their start and end apart: 25 -> 25, of which waited for: 9 -> 8; matrix products, arithmetic and copies ran while one was open for 13% -> 12% of each run, Pallas kernels for 47% -> 43%
where the time goes in v5:
time: 564 us; the launch traced here: 554 us
  Pallas kernels  241 us (43%)
  waiting for transfers between devices  152 us (27%)
  starting transfers between devices  54.2 us (10%)
  local copies, waits for them, and re-layouts  47.5 us (8%)
  other arithmetic  35.5 us (6%)
  between operations  17.9 us (3%)
  matrix products  6.91 us (1%)
    pallas_call x2, Pallas kernels, feed(): pl.pallas_call(functools.partial(feed_kernel, rows=rows, first=first, sub...  74.5 us
    all_to_all x3, waiting for transfers between devices, to_fsdp(): lax.all_to_all(block, 'fsdp', split_axis=0, concat_axis=0, tiled=True)  63.6 us
    pallas_call x1, Pallas kernels, heads_back(): pl.pallas_call(functools.partial(heads_back_kernel, step=step), grid=(hea...  47.2 us
    ppermute x1, waiting for transfers between devices, step_first(): lax.ppermute(block, BOTH, moved(n_fsdp, lambda z, x, c, y: (z, x, c, 1 -...  32.6 us
    all_to_all x2, waiting for transfers between devices, to_all(): lax.all_to_all(block, ('fsdp', 'seq'), split_axis=0, concat_axis=0, tiled...  29.8 us
    pallas_call x1, Pallas kernels, heads_forward(): pl.pallas_call(functools.partial(heads_kernel, step=step), grid=(heads,),...  29.6 us
    ppermute x10, waiting for transfers between devices, swap(): return lax.ppermute(block, 'seq', [(0, 1), (1, 0)])  25.7 us
    pallas_call x1, Pallas kernels, leave(): pl.pallas_call(leave_kernel, grid=(length // tile,), in_specs=[rows_of((3...  23.3 us
  transfers between devices with their start and end apart: 25, of which 8 were waited for; matrix products, arithmetic and copies ran while one was open for 12% of the time, Pallas kernels for 43%

profile of v5, /device:TPU:0, one launch (start us, length us, event | category | flops | bytes accessed | tf_op | source)
XLA Modules:
  0.0 554.2 jit_solution(2978556572827739450)
XLA Ops:
  8.3 3.0 collective-permute-start.2
  11.3 7.8 %collective-permute-done.2 = bf16[72,2304]{1,0:T(8,128)(2,1)S(1)} collective-permute-done((bf16[72,2304]{1,0:T(8,128)(2,1)S(1)}, bf16[72,2304]{1,0:T(8,128)(2,1)S(1)}, u32[]{:S(2)}, u32[]{:S(2)}) %collective-permute-start.2) | collective-permute-done | bytes 331808 | tf_op jit(solution)/shard_map/ppermute | solution.py:1392
  26.3 7.2 %collective-permute-done.11 = bf16[72,2304]{1,0:T(8,128)(2,1)S(1)} collective-permute-done((bf16[72,2304]{1,0:T(8,128)(2,1)S(1)}, bf16[72,2304]{1,0:T(8,128)(2,1)S(1)}, u32[]{:S(2)}, u32[]{:S(2)}) %collective-permute-start.11) | collective-permute-done | bytes 331808 | tf_op jit(solution)/shard_map/ppermute | solution.py:1392
  36.6 2.6 collective-permute-start.5
  41.5 3.5 all-to-all-start
  45.0 41.7 %all-to-all-done = bf16[16,2,80]{2,1,0:T(2,128)(2,1)S(1)} async-done(((bf16[16,2,80]{2,1,0:T(2,128)(2,1)}), bf16[16,2,80]{2,1,0:T(2,128)(2,1)S(1)}, u32[]{:S(2)}, u32[]{:S(2)}) %all-to-all-start) | async-done | bytes 5152 | tf_op jit(solution)/shard_map/all_to_all | solution.py:1415
  101.5 3.3 all-to-all-start.2
  106.6 32.6 %collective-permute-done.7 = bf16[4,72,2304]{2,1,0:T(8,128)(2,1)S(1)} collective-permute-done((bf16[4,72,2304]{2,1,0:T(8,128)(2,1)S(1)}, bf16[4,72,2304]{2,1,0:T(8,128)(2,1)S(1)}, u32[]{:S(2)}, u32[]{:S(2)}) %collective-permute-start.7) | collective-permute-done | bytes 1327136 | tf_op jit(solution)/shard_map/ppermute | solution.py:1129
  146.0 29.8 %all-to-all-done.2 = f32[32,1,3456]{2,1,0:T(1,128)} async-done(((f32[32,1,3456]{2,1,0:T(1,128)}), f32[32,1,3456]{2,1,0:T(1,128)}, u32[]{:S(2)}, u32[]{:S(2)}) %all-to-all-start.2) | async-done | bytes 442400 | tf_op jit(solution)/shard_map/all_to_all | solution.py:1411
  175.8 3.6 all-to-all-start.1
  179.5 2.8 reduce.1
  195.5 9.8 %all-to-all-done.1.came_ref = bf16[16,16,1656]{2,1,0:T(8,128)(2,1)S(1)} async-done(((bf16[16,16,1656]{2,1,0:T(8,128)(2,1)}), bf16[16,16,1656]{2,1,0:T(8,128)(2,1)S(1)}, u32[]{:S(2)}, u32[]{:S(2)}) %all-to-all-start.1) | async-done | bytes 847904 | tf_op jit(solution)/shard_map/all_to_all | solution.py:1415
  215.3 18.9 %entry.1 = (bf16[1024,1152]{1,0:T(8,128)(2,1)}, bf16[1024,128]{1,0:T(8,128)(2,1)}, bf16[3,16,72,1024]{3,2,1,0:T(8,128)(2,1)}) custom-call(bf16[1024,1152]{1,0:T(8,128)(2,1)} %bitcast.122, f32[8,1152]{1,0:T(8,128)} %copy-done.38, bf16[1152,4608]{1,0:T(8,128)(2,1)} %all-gather.4.cloned.1.call-done.weight_ref, bf16[128,3456]{1,0:T(8,128)(2,1)} %copy-done.45, ...), custom_call_target="tpu_custom_call" | custom-call | flops 9059696640 | bytes 24772608 | tf_op jit(solution)/shard_map/entry/pallas_call | solution.py:598
  234.2 29.6 %heads_forward.1 = (bf16[16,72,1024]{2,1,0:T(8,128)(2,1)S(1)}, f32[16,1,1024]{2,1,0:T(1,128)S(1)}) custom-call(bf16[3,16,72,1024]{3,2,1,0:T(8,128)(2,1)} %get-tuple-element.66.qkv_ref), custom_call_target="tpu_custom_call" | custom-call | flops 17179869184 | bytes 11796480 | tf_op jit(solution)/shard_map/heads_forward/pallas_call | solution.py:422
  264.0 12.6 %before_feed.1 = (bf16[1024,1280]{1,0:T(8,128)(2,1)}, bf16[1024,1280]{1,0:T(8,128)(2,1)}, f32[1024,1152]{1,0:T(8,128)}, bf16[3,16,1024]{2,1,0:T(8,128)(2,1)S(1)}) custom-call(bf16[1152,1024]{1,0:T(8,128)(2,1)S(1)} %bitcast.126, bf16[1024,1152]{1,0:T(8,128)(2,1)S(1)} %bitcast.125, bf16[1024,1152]{1,0:T(8,128)(2,1)} %bitcast.129, f32[8,1152]{1,0:T(8,128)S(1)} %copy-done.39, ...), custom_call_target="tpu_custom_call" | custom-call | flops 6039797760 | bytes 18874368 | tf_op jit(solution)/shard_map/before_feed/pallas_call | solution.py:680
  281.3 2.4 fusion.19
  284.8 7.5 %assemble.1 = bf16[2,4,2,2,72,2304]{5,4,3,2,1,0:T(8,128)(2,1)S(1)} custom-call(s32[4]{0:T(128)S(1)} %pad_add_fusion.place_ref, bf16[2,4,72,2304]{3,2,1,0:T(8,128)(2,1)S(1)} %pad_maximum_fusion.near_ref, bf16[2,4,72,2304]{3,2,1,0:T(8,128)(2,1)} %collective-permute-done.8.far_ref, bf16[2,4,72,2304]{3,2,1,0:T(8,128)(2,1)} %collective-permute-done.9.next_near_ref, ...), custom_call_target="tpu_custom_call" | custom-call | bytes 21233664 | tf_op jit(solution)/shard_map/assemble/pallas_call | solution.py:560
  292.3 3.9 copy-done
  296.8 35.8 %feed.2 = (f32[1024,1280]{1,0:T(8,128)}, f32[1024,1280]{1,0:T(8,128)}, f32[16,2304]{1,0:T(8,128)}, f32[16,2304]{1,0:T(8,128)}) custom-call(bf16[1024,1280]{1,0:T(8,128)(2,1)} %get-tuple-element.72.second_ref, bf16[1024,1280]{1,0:T(8,128)(2,1)} %get-tuple-element.73.dfinal_ref, bf16[3,16,1024]{2,1,0:T(8,128)(2,1)} %copy-done.31, ...), custom_call_target="tpu_custom_call" | custom-call | flops 24159191040 | bytes 21037056 | tf_op jit(solution)/shard_map/feed/pallas_call | solution.py:796
  332.5 38.7 %feed.3 = (f32[1024,1280]{1,0:T(8,128)}, f32[1024,1280]{1,0:T(8,128)}, f32[16,2304]{1,0:T(8,128)}, f32[16,2304]{1,0:T(8,128)}) custom-call(bf16[1024,1280]{1,0:T(8,128)(2,1)} %get-tuple-element.72.second_ref, bf16[1024,1280]{1,0:T(8,128)(2,1)} %get-tuple-element.73.dfinal_ref, ...), custom_call_target="tpu_custom_call", output_to_operand_aliasing={{0}: (8, {}), {1}: (9, {})} | custom-call | flops 24159191040 | bytes 21037056 | tf_op jit(solution)/shard_map/feed/pallas_call | solution.py:796
  371.2 20.8 %after_feed.1 = (bf16[1024,1152]{1,0:T(8,128)(2,1)}, f32[1024,1152]{1,0:T(8,128)}, bf16[1152,1024]{1,0:T(8,128)(2,1)}, f32[8,1152]{1,0:T(8,128)}, f32[16,1152]{1...) custom-call(f32[1024,1280]{1,0:T(8,128)} %get-tuple-element.79.final_ref, ...), custom_call_target="tpu_custom_call" | custom-call | flops 7549747200 | bytes 37748736 | tf_op jit(solution)/shard_map/after_feed/pallas_call | solution.py:935
  395.9 47.2 %heads_back.1.dqkv_ref = bf16[3,16,72,1024]{3,2,1,0:T(8,128)(2,1)} custom-call(bf16[3,16,72,1024]{3,2,1,0:T(8,128)(2,1)} %get-tuple-element.66.qkv_ref, bf16[16,72,1024]{2,1,0:T(8,128)(2,1)} %bitcast.149, bf16[16,72,1024]{2,1,0:T(8,128)(2,1)} %copy-done.2, f32[16,1,1024]{2,1,0:T(1,128)} %copy-done.47), custom_call_target="tpu_custom_call" | custom-call | flops 42949672960 | bytes 18874368 | tf_op jit(solution)/shard_map/heads_back/pallas_call | solution.py:482
  443.2 23.3 %leave.1 = (bf16[1024,1152]{1,0:T(8,128)(2,1)}, f32[8,1152]{1,0:T(8,128)}, f32[16,3456]{1,0:T(8,128)}, f32[16,1152]{1,0:T(8,128)}) custom-call(bf16[3,16,72,1024]{3,2,1,0:T(8,128)(2,1)} %heads_back.1.dqkv_ref, bf16[1024,1152]{1,0:T(8,128)(2,1)} %bitcast.124, f32[1024,1152]{1,0:T(8,128)} %get-tuple-element.85.dresidual_ref, ...), custom_call_target="tpu_custom_call" | custom-call | flops 10569646080 | bytes 31850496 | tf_op jit(solution)/shard_map/leave/pallas_call | solution.py:1066
  471.1 15.8 %all-to-all-start.3 = ((bf16[16,16,1656]{2,1,0:T(8,128)(2,1)}), bf16[16,16,1656]{2,1,0:T(8,128)(2,1)S(1)}, u32[]{:S(2)}, u32[]{:S(2)}) async-start(bf16[16,16,1656]{2,1,0:T(8,128)(2,1)} %get-tuple-element.104), calls=%async_computation.3 | async-start | bytes 1703936 | tf_op jit(solution)/shard_map/all_to_all | solution.py:1415
  491.6 2.9 fusion.2
  494.5 12.1 %all-to-all-done.3.came_ref = bf16[16,16,1656]{2,1,0:T(8,128)(2,1)S(1)} async-done(((bf16[16,16,1656]{2,1,0:T(8,128)(2,1)}), bf16[16,16,1656]{2,1,0:T(8,128)(2,1)S(1)}, u32[]{:S(2)}, u32[]{:S(2)}) %all-to-all-start.3) | async-done | bytes 847904 | tf_op jit(solution)/shard_map/all_to_all | solution.py:1415
  507.8 2.9 pad_maximum_fusion.3
  512.0 10.7 %collective-permute-done.13 = bf16[4,16,1656]{2,1,0:T(8,128)(2,1)S(1)} collective-permute-done((bf16[4,16,1656]{2,1,0:T(8,128)(2,1)S(1)}, bf16[4,16,1656]{2,1,0:T(8,128)(2,1)S(1)}, u32[]{:S(2)}, u32[]{:S(2)}) %collective-permute-start.13) | collective-permute-done | bytes 212000 | tf_op jit(solution)/shard_map/ppermute | solution.py:1392
  524.6 5.8 %all-to-all-start.4 = ((f32[32,1,128]{2,1,0:T(1,128)}), f32[32,1,128]{2,1,0:T(1,128)S(1)}, u32[]{:S(2)}, u32[]{:S(2)}) async-start(f32[32,1,128]{2,1,0:T(1,128)} %broadcast_in_dim.52), calls=%async_computation.4 | async-start | bytes 32768 | tf_op jit(solution)/shard_map/all_to_all | solution.py:1411
  531.7 2.9 fusion
  534.6 5.5 convolution_add_fusion
  542.0 2.5 maximum_convert_fusion
  (267 shorter events, 86.8 us)
Async XLA Ops:
  7.2 208.1 %all-gather.4.cloned.1.call-start = ((), (), s32[]{:S(2)}) async-start(), calls=%async_computation.5 | async-start | bytes 11280384 | tf_op jit(solution)/shard_map/all_gather | solution.py:1459
  8.3 10.8 %collective-permute-start.2 = (bf16[72,2304]{1,0:T(8,128)(2,1)S(1)}, bf16[72,2304]{1,0:T(8,128)(2,1)S(1)}, u32[]{:S(2)}, u32[]{:S(2)}) collective-permute-start(bf16[72,2304]{1,0:T(8,128)(2,1)S(1)} %pad_maximum_fusion.6), channel_id=1, source_target_pairs={{0,1},{1,0},{2,3},{3,2},{4,5},{5,4},{6,7},{7,6},{8,9},{9,8},{10,11... | collective-permute-start | bytes 995336 | tf_op jit(solution)/shard_map/ppermute | solution.py:1392
  22.0 274.2 %all-gather.6.cloned.1.call-start = ((), (), s32[]{:S(2)}) async-start(), calls=%async_computation.6 | async-start | bytes 11280384 | tf_op jit(solution)/shard_map/all_gather | solution.py:1459
  24.5 9.1 %collective-permute-start.11 = (bf16[72,2304]{1,0:T(8,128)(2,1)S(1)}, bf16[72,2304]{1,0:T(8,128)(2,1)S(1)}, u32[]{:S(2)}, u32[]{:S(2)}) collective-permute-start(bf16[72,2304]{1,0:T(8,128)(2,1)S(1)} %concatenate.33), channel_id=1, source_target_pairs={{0,1},{1,0},{2,3},{3,2},{4,5},{5,4},{6,7},{7,6},{8,9},{9,8},{10,11... | collective-permute-start | bytes 995336 | tf_op jit(solution)/shard_map/ppermute | solution.py:1392
  35.1 52.8 %collective-permute-start.4 = (bf16[72,2304]{1,0:T(8,128)(2,1)S(1)}, bf16[72,2304]{1,0:T(8,128)(2,1)S(1)}, u32[]{:S(2)}, u32[]{:S(2)}) collective-permute-start(bf16[72,2304]{1,0:T(8,128)(2,1)S(1)} %concatenate.32), channel_id=1, source_target_pairs={{0,8},{1,9},{2,10},{3,11},{4,12},{5,13},{6,14},{7,15},{8,16},{9,17... | collective-permute-start | bytes 995336 | tf_op jit(solution)/shard_map/ppermute | solution.py:1124
  36.6 51.3 %collective-permute-start.5 = (bf16[72,2304]{1,0:T(8,128)(2,1)S(1)}, bf16[72,2304]{1,0:T(8,128)(2,1)S(1)}, u32[]{:S(2)}, u32[]{:S(2)}) collective-permute-start(bf16[72,2304]{1,0:T(8,128)(2,1)S(1)} %concatenate.32), channel_id=1, source_target_pairs={{0,16},{1,17},{2,18},{3,19},{4,20},{5,21},{6,22},{7,23},{8,24},{9,... | collective-permute-start | bytes 995336 | tf_op jit(solution)/shard_map/ppermute | solution.py:1124
  39.2 48.7 %collective-permute-start.6 = (bf16[72,2304]{1,0:T(8,128)(2,1)S(1)}, bf16[72,2304]{1,0:T(8,128)(2,1)S(1)}, u32[]{:S(2)}, u32[]{:S(2)}) collective-permute-start(bf16[72,2304]{1,0:T(8,128)(2,1)S(1)} %concatenate.32), channel_id=1, source_target_pairs={{0,24},{1,25},{2,26},{3,27},{4,28},{5,29},{6,30},{7,31},{8,0},{9,1... | collective-permute-start | bytes 995336 | tf_op jit(solution)/shard_map/ppermute | solution.py:1124
  41.5 45.2 %all-to-all-start = ((bf16[16,2,80]{2,1,0:T(2,128)(2,1)}), bf16[16,2,80]{2,1,0:T(2,128)(2,1)S(1)}, u32[]{:S(2)}, u32[]{:S(2)}) async-start(bf16[16,2,80]{2,1,0:T(2,128)(2,1)} %pad_maximum_fusion.8), calls=%async_computation | async-start | bytes 16384 | tf_op jit(solution)/shard_map/all_to_all | solution.py:1415
  89.1 50.0 %collective-permute-start.7 = (bf16[4,72,2304]{2,1,0:T(8,128)(2,1)S(1)}, bf16[4,72,2304]{2,1,0:T(8,128)(2,1)S(1)}, u32[]{:S(2)}, u32[]{:S(2)}) collective-permute-start(bf16[4,72,2304]{2,1,0:T(8,128)(2,1)S(1)} %maximum_add_fusion.1), channel_id=1, source_target_pairs={{0,4},{1,5},{2,3},{3,2},{4,0},{5,1},{6,7},{7,6},{8,12},{9,13},{10,... | collective-permute-start | bytes 3981320 | tf_op jit(solution)/shard_map/ppermute | solution.py:1129
  91.6 96.0 %collective-permute-start = (bf16[512,1152]{1,0:T(8,128)(2,1)}, bf16[512,1152]{1,0:T(8,128)(2,1)}, u32[]{:S(2)}, u32[]{:S(2)}) collective-permute-start(bf16[512,1152]{1,0:T(8,128)(2,1)} %dynamic-slice_bitcast_fusion.3), channel_id=1, source_target_pairs={{0,1},{1,0},{2,3},{3,2},{4,5},{5,4},{6,7},{7,6},{8,9},{9,8},{10,11... | collective-permute-start | bytes 3538952 | tf_op jit(solution)/shard_map/ppermute | solution.py:1392
  94.0 49.3 %collective-permute-start.1 = (bf16[4,16,1656]{2,1,0:T(8,128)(2,1)}, bf16[4,16,1656]{2,1,0:T(8,128)(2,1)}, u32[]{:S(2)}, u32[]{:S(2)}) collective-permute-start(bf16[4,16,1656]{2,1,0:T(8,128)(2,1)} %pad_maximum_fusion.7), channel_id=1, source_target_pairs={{0,1},{1,0},{2,3},{3,2},{4,5},{5,4},{6,7},{7,6},{8,9},{9,8},{10,11... | collective-permute-start | bytes 635912 | tf_op jit(solution)/shard_map/ppermute | solution.py:1392
  95.7 95.5 %collective-permute-start.3 = (bf16[512,1152]{1,0:T(8,128)(2,1)}, bf16[512,1152]{1,0:T(8,128)(2,1)}, u32[]{:S(2)}, u32[]{:S(2)}) collective-permute-start(bf16[512,1152]{1,0:T(8,128)(2,1)} %dynamic-slice_bitcast_fusion.2), channel_id=1, source_target_pairs={{0,1},{1,0},{2,3},{3,2},{4,5},{5,4},{6,7},{7,6},{8,9},{9,8},{10,11... | collective-permute-start | bytes 3538952 | tf_op jit(solution)/shard_map/ppermute | solution.py:1392
  99.3 106.1 %copy-start.36 = (f32[1,1152]{1,0:T(1,128)}, f32[1,1152]{1,0:T(1,128)S(1)}, u32[]{:S(2)}) copy-start(f32[1,1152]{1,0:T(1,128)S(1)} %dynamic-slice_convert_fusion.cond_ref) | copy-start | bytes 13828
  101.5 74.3 %all-to-all-start.2 = ((f32[32,1,3456]{2,1,0:T(1,128)}), f32[32,1,3456]{2,1,0:T(1,128)}, u32[]{:S(2)}, u32[]{:S(2)}) async-start(f32[32,1,3456]{2,1,0:T(1,128)} %copy.42), calls=%async_computation.2 | async-start | bytes 884736 | tf_op jit(solution)/shard_map/all_to_all | solution.py:1411
  105.3 39.1 %copy-start.43 = (s32[16]{0:T(128)}, s32[16]{0:T(128)S(1)}, u32[]{:S(2)}) copy-start(s32[16]{0:T(128)S(1)} %convert_reduce_fusion.ids_ref) | copy-start | bytes 196
  141.8 73.5 %collective-permute-start.8 = (bf16[2,4,72,2304]{3,2,1,0:T(8,128)(2,1)S(1)}, bf16[2,4,72,2304]{3,2,1,0:T(8,128)(2,1)}, u32[]{:S(2)}, u32[]{:S(2)}) collective-permute-start(bf16[2,4,72,2304]{3,2,1,0:T(8,128)(2,1)S(1)} %pad_maximum_fusion.near_ref), channel_id=1, source_target_pairs={{0,1},{1,0},{2,6},{3,7},{4,5},{5,4},{6,2},{7,3},{8,9},{9,8},{10,14... | collective-permute-start | bytes 7962632 | tf_op jit(solution)/shard_map/ppermute | solution.py:1137
  175.8 29.5 %all-to-all-start.1 = ((bf16[16,16,1656]{2,1,0:T(8,128)(2,1)}), bf16[16,16,1656]{2,1,0:T(8,128)(2,1)S(1)}, u32[]{:S(2)}, u32[]{:S(2)}) async-start(bf16[16,16,1656]{2,1,0:T(8,128)(2,1)} %copy.52), calls=%async_computation.1 | async-start | bytes 1703936 | tf_op jit(solution)/shard_map/all_to_all | solution.py:1415
  179.4 355.2 %all-gather.8.cloned.1.call-start = ((), (), s32[]{:S(2)}) async-start(), calls=%async_computation.7 | async-start | bytes 8460288 | tf_op jit(solution)/shard_map/all_gather | solution.py:1593
  195.2 89.6 %collective-permute-start.9 = (bf16[2,4,72,2304]{3,2,1,0:T(8,128)(2,1)S(1)}, bf16[2,4,72,2304]{3,2,1,0:T(8,128)(2,1)}, u32[]{:S(2)}, u32[]{:S(2)}) collective-permute-start(bf16[2,4,72,2304]{3,2,1,0:T(8,128)(2,1)S(1)} %pad_maximum_fusion.near_ref), channel_id=1, source_target_pairs={{0,2},{1,3},{2,0},{3,1},{4,6},{5,7},{6,4},{7,5},{8,10},{9,11},{10,... | collective-permute-start | bytes 7962632 | tf_op jit(solution)/shard_map/ppermute | solution.py:1145
  215.3 69.5 %collective-permute-start.10 = (bf16[2,4,72,2304]{3,2,1,0:T(8,128)(2,1)}, bf16[2,4,72,2304]{3,2,1,0:T(8,128)(2,1)}, u32[]{:S(2)}, u32[]{:S(2)}) collective-permute-start(bf16[2,4,72,2304]{3,2,1,0:T(8,128)(2,1)} %collective-permute-done.8.far_ref), channel_id=1, source_target_pairs={{0,2},{1,3},{2,0},{3,1},{4,6},{5,7},{6,4},{7,5},{8,10},{9,11},{10,... | collective-permute-start | bytes 7962632 | tf_op jit(solution)/shard_map/ppermute | solution.py:1145
  234.2 29.7 %copy-start.19 = (bf16[128,1152]{1,0:T(8,128)(2,1)S(1)}, bf16[128,1152]{1,0:T(8,128)(2,1)}, u32[]{:S(2)}) copy-start(bf16[128,1152]{1,0:T(8,128)(2,1)} %copy-done.18) | copy-start | bytes 884740
  234.2 29.7 %copy-start.21 = (bf16[128,1152]{1,0:T(8,128)(2,1)S(1)}, bf16[128,1152]{1,0:T(8,128)(2,1)}, u32[]{:S(2)}) copy-start(bf16[128,1152]{1,0:T(8,128)(2,1)} %copy-done.20) | copy-start | bytes 884740
  234.2 29.7 %copy-start.23 = (bf16[128,1152]{1,0:T(8,128)(2,1)S(1)}, bf16[128,1152]{1,0:T(8,128)(2,1)}, u32[]{:S(2)}) copy-start(bf16[128,1152]{1,0:T(8,128)(2,1)} %copy-done.22) | copy-start | bytes 884740
  234.2 29.7 %copy-start.39 = (f32[8,1152]{1,0:T(8,128)S(1)}, f32[8,1152]{1,0:T(8,128)}, u32[]{:S(2)}) copy-start(f32[8,1152]{1,0:T(8,128)} %copy-done.38) | copy-start | bytes 110596
  234.2 29.7 %copy-start.42 = (f32[1,1152]{1,0:T(1,128)S(1)}, f32[1,1152]{1,0:T(1,128)}, u32[]{:S(2)}) copy-start(f32[1,1152]{1,0:T(1,128)} %broadcast_in_dim.45.bias_ref) | copy-start | bytes 13828
  394.4 97.2 %collective-permute-start.12 = (bf16[512,1152]{1,0:T(8,128)(2,1)}, bf16[512,1152]{1,0:T(8,128)(2,1)}, u32[]{:S(2)}, u32[]{:S(2)}) collective-permute-start(bf16[512,1152]{1,0:T(8,128)(2,1)} %dynamic-slice_bitcast_fusion.1), channel_id=1, source_target_pairs={{0,1},{1,0},{2,3},{3,2},{4,5},{5,4},{6,7},{7,6},{8,9},{9,8},{10,11... | collective-permute-start | bytes 3538952 | tf_op jit(solution)/shard_map/ppermute | solution.py:1392
  471.1 35.5 %all-to-all-start.3 = ((bf16[16,16,1656]{2,1,0:T(8,128)(2,1)}), bf16[16,16,1656]{2,1,0:T(8,128)(2,1)S(1)}, u32[]{:S(2)}, u32[]{:S(2)}) async-start(bf16[16,16,1656]{2,1,0:T(8,128)(2,1)} %get-tuple-element.104), calls=%async_computation.3 | async-start | bytes 1703936 | tf_op jit(solution)/shard_map/all_to_all | solution.py:1415
  487.0 4.6 collective-permute-start.15
  489.8 41.9 %collective-permute-start.14 = (bf16[512,1152]{1,0:T(8,128)(2,1)}, bf16[512,1152]{1,0:T(8,128)(2,1)}, u32[]{:S(2)}, u32[]{:S(2)}) collective-permute-start(bf16[512,1152]{1,0:T(8,128)(2,1)} %dynamic-slice_bitcast_fusion), channel_id=1, source_target_pairs={{0,1},{1,0},{2,3},{3,2},{4,5},{5,4},{6,7},{7,6},{8,9},{9,8},{10,11... | collective-permute-start | bytes 3538952 | tf_op jit(solution)/shard_map/ppermute | solution.py:1392
  507.4 15.2 %collective-permute-start.13 = (bf16[4,16,1656]{2,1,0:T(8,128)(2,1)S(1)}, bf16[4,16,1656]{2,1,0:T(8,128)(2,1)S(1)}, u32[]{:S(2)}, u32[]{:S(2)}) collective-permute-start(bf16[4,16,1656]{2,1,0:T(8,128)(2,1)S(1)} %get-tuple-element.106), channel_id=1, source_target_pairs={{0,1},{1,0},{2,3},{3,2},{4,5},{5,4},{6,7},{7,6},{8,9},{9,8},{10,11... | collective-permute-start | bytes 635912 | tf_op jit(solution)/shard_map/ppermute | solution.py:1392
  524.6 19.9 %all-to-all-start.4 = ((f32[32,1,128]{2,1,0:T(1,128)}), f32[32,1,128]{2,1,0:T(1,128)S(1)}, u32[]{:S(2)}, u32[]{:S(2)}) async-start(f32[32,1,128]{2,1,0:T(1,128)} %broadcast_in_dim.52), calls=%async_computation.4 | async-start | bytes 32768 | tf_op jit(solution)/shard_map/all_to_all | solution.py:1411
  540.1 6.4 %collective-permute-start.16 = (f32[2,1152]{1,0:T(2,128)S(1)}, f32[2,1152]{1,0:T(2,128)S(1)}, u32[]{:S(2)}, u32[]{:S(2)}) collective-permute-start(f32[2,1152]{1,0:T(2,128)S(1)} %convolution_add_fusion), channel_id=1, source_target_pairs={{0,1},{1,0},{2,3},{3,2},{4,5},{5,4},{6,7},{7,6},{8,9},{9,8},{10,11... | collective-permute-start | bytes 27656 | tf_op jit(solution)/shard_map/ppermute | solution.py:1392
  (68 other events, 520.3 us)
Sparse Core Ops, SparseCore 0:
  22.1 133.5 all-gather.3
  157.9 95.0 all-gather.5
  280.1 83.5 all-gather.7

commit v6 on v4

--- a/solution.py
+++ b/solution.py
@@ -1554,6 +1554,11 @@
         d_qkv, token_rows, d_residual, hidden, middle_qkv, mods, heads_weight, up_qkv, down_qkv
     )
 
+    halves = token_rows_grad.reshape(tokens.shape)
+    token_sent = lax.dynamic_index_in_dim(halves, 1 - mine, 0, False)
+    token_came = swap(token_sent)
+    leave_sums = behind(leave_sums, token_sent)
+
     sent, d_modulation, own_cond = pack(
         (
             leave_sums,
@@ -1591,6 +1596,7 @@
     d_cond = d_cond + swap(d_cond)
     cond_grad = jax.vjp(jax.nn.silu, condition)[1](d_cond)[0]
     token_kept, token_came = send_row(token_rows_grad.reshape(tokens.shape), mine)
+    token_kept = lax.dynamic_index_in_dim(halves, mine, 0, False)
     token_grad = by_seq(behind(token_kept, gradient), token_came, mine).astype(jnp.float32)
 
     states = (

time: 522 us -> 524 us (level)
  waiting for transfers between devices: 106 us -> 125 us
  starting transfers between devices: 61.5 us -> 44.7 us
    ppermute x10, waiting for transfers between devices: 27 us -> 56.8 us  [swap(): return lax.ppermute(block, 'seq', [(0, 1), (1, 0)])]
    ppermute x3, waiting for transfers between devices: 23.2 us -> 0.01 us  [step_z(): by_shift.append(lax.ppermute(block, BOTH, pairs))]
    ppermute x1, waiting for transfers between devices: 32 us -> 11.3 us  [step_first(): lax.ppermute(block, BOTH, moved(n_fsdp, lambda z, x, c, y: (z, x, c, 1 -...]
    all_to_all x2, waiting for transfers between devices: 0.01 us -> 16.1 us  [to_all(): lax.all_to_all(block, ('fsdp', 'seq'), split_axis=0, concat_axis=0, tiled...]
    all_to_all x3, starting transfers between devices: 24.9 us -> 12.8 us  [to_fsdp(): lax.all_to_all(block, 'fsdp', split_axis=0, concat_axis=0, tiled=True)]
    ppermute x1, waiting for transfers between devices: 0.01 us -> 9.54 us  [step_second(): lax.ppermute(block, BOTH, moved(n_fsdp, lambda z, x, c, y: (z, 1 - x, c,...]
    all_to_all x3, waiting for transfers between devices: 23.4 us -> 31.1 us  [to_fsdp(): lax.all_to_all(block, 'fsdp', split_axis=0, concat_axis=0, tiled=True)]
    all_to_all x2, starting transfers between devices: 13.6 us -> 8.1 us  [to_all(): lax.all_to_all(block, ('fsdp', 'seq'), split_axis=0, concat_axis=0, tiled...]
where the time goes in v6:
time: 524 us; the launch traced here: 514 us
  Pallas kernels  241 us (46%)
  waiting for transfers between devices  125 us (24%)
  local copies, waits for them, and re-layouts  45.4 us (9%)
  starting transfers between devices  44.7 us (9%)
  other arithmetic  31.7 us (6%)
  between operations  17.8 us (3%)
  matrix products  8.82 us (2%)
    pallas_call x2, Pallas kernels, feed(): pl.pallas_call(functools.partial(feed_kernel, rows=rows, first=first, sub...  74.5 us
    ppermute x10, waiting for transfers between devices, swap(): return lax.ppermute(block, 'seq', [(0, 1), (1, 0)])  56.8 us
    pallas_call x1, Pallas kernels, heads_back(): pl.pallas_call(functools.partial(heads_back_kernel, step=step), grid=(hea...  47.2 us
    all_to_all x3, waiting for transfers between devices, to_fsdp(): lax.all_to_all(block, 'fsdp', split_axis=0, concat_axis=0, tiled=True)  31.1 us
    pallas_call x1, Pallas kernels, heads_forward(): pl.pallas_call(functools.partial(heads_kernel, step=step), grid=(heads,),...  29.5 us
    pallas_call x1, Pallas kernels, leave(): pl.pallas_call(leave_kernel, grid=(length // tile,), in_specs=[rows_of((3...  23.2 us
    pallas_call x1, Pallas kernels, after_feed(): pl.pallas_call(after_kernel, grid=(length // tile,), in_specs=[rows_of((t...  20.7 us
    pallas_call x1, Pallas kernels, entry(): pl.pallas_call(entry_kernel, grid=(length // tile,), in_specs=[rows_of((t...  18.8 us
  transfers between devices with their start and end apart: 25, of which 9 were waited for; matrix products, arithmetic and copies ran while one was open for 13% of the time, Pallas kernels for 47%

profile of v6, /device:TPU:0, one launch (start us, length us, event | category | flops | bytes accessed | tf_op | source)
XLA Modules:
  0.0 514.1 jit_solution(2476303417942901578)
XLA Ops:
  8.3 3.0 collective-permute-start.2
  11.3 7.8 %collective-permute-done.2 = bf16[72,2304]{1,0:T(8,128)(2,1)S(1)} collective-permute-done((bf16[72,2304]{1,0:T(8,128)(2,1)S(1)}, bf16[72,2304]{1,0:T(8,128)(2,1)S(1)}, u32[]{:S(2)}, u32[]{:S(2)}) %collective-permute-start.2) | collective-permute-done | bytes 331808 | tf_op jit(solution)/shard_map/ppermute | solution.py:1381
  26.4 7.2 %collective-permute-done.11 = bf16[72,2304]{1,0:T(8,128)(2,1)S(1)} collective-permute-done((bf16[72,2304]{1,0:T(8,128)(2,1)S(1)}, bf16[72,2304]{1,0:T(8,128)(2,1)S(1)}, u32[]{:S(2)}, u32[]{:S(2)}) %collective-permute-start.11) | collective-permute-done | bytes 331808 | tf_op jit(solution)/shard_map/ppermute | solution.py:1381
  38.9 2.6 collective-permute-start.5
  46.1 3.5 all-to-all-start
  51.5 2.5 dynamic-slice_bitcast_fusion.2
  56.0 30.7 %all-to-all-done = bf16[16,2,80]{2,1,0:T(2,128)(2,1)S(1)} async-done(((bf16[16,2,80]{2,1,0:T(2,128)(2,1)}), bf16[16,2,80]{2,1,0:T(2,128)(2,1)S(1)}, u32[]{:S(2)}, u32[]{:S(2)}) %all-to-all-start) | async-done | bytes 5152 | tf_op jit(solution)/shard_map/all_to_all | solution.py:1404
  88.1 3.3 all-to-all-start.1
  93.6 2.9 fusion.23
  100.6 16.1 %all-to-all-done.1 = f32[32,1,3456]{2,1,0:T(1,128)} async-done(((f32[32,1,3456]{2,1,0:T(1,128)}), f32[32,1,3456]{2,1,0:T(1,128)}, u32[]{:S(2)}, u32[]{:S(2)}) %all-to-all-start.1) | async-done | bytes 442400 | tf_op jit(solution)/shard_map/all_to_all | solution.py:1400
  116.7 3.8 all-to-all-start.2
  120.5 2.8 reduce
  128.2 11.3 %collective-permute-done.7 = bf16[4,72,2304]{2,1,0:T(8,128)(2,1)} collective-permute-done((bf16[4,72,2304]{2,1,0:T(8,128)(2,1)}, bf16[4,72,2304]{2,1,0:T(8,128)(2,1)}, u32[]{:S(2)}, u32[]{:S(2)}) %collective-permute-start.7) | collective-permute-done | bytes 1327136 | tf_op jit(solution)/shard_map/ppermute | solution.py:1129
  163.8 9.5 %collective-permute-done.8.far_ref = bf16[2,4,72,2304]{3,2,1,0:T(8,128)(2,1)} collective-permute-done((bf16[2,4,72,2304]{3,2,1,0:T(8,128)(2,1)S(1)}, bf16[2,4,72,2304]{3,2,1,0:T(8,128)(2,1)}, u32[]{:S(2)}, u32[]{:S(2)}) %collective-permute-start.8) | collective-permute-done | bytes 2654240 | tf_op jit(solution)/shard_map/ppermute | solution.py:1137
  175.0 18.8 %entry.1 = (bf16[1024,1152]{1,0:T(8,128)(2,1)}, bf16[1024,128]{1,0:T(8,128)(2,1)}, bf16[3,16,72,1024]{3,2,1,0:T(8,128)(2,1)}) custom-call(bf16[1024,1152]{1,0:T(8,128)(2,1)} %bitcast.134, f32[8,1152]{1,0:T(8,128)} %pad.4.mod_ref, bf16[1152,4608]{1,0:T(8,128)(2,1)} %all-gather.4.cloned.1.call-done.weight_ref, bf16[128,3456]{1,0:T(8,128)(2,1)} %copy-done.40, ...), custom_call_target="tpu_custom_call" | custom-call | flops 9059696640 | bytes 24772608 | tf_op jit(solution)/shard_map/entry/pallas_call | solution.py:598
  193.9 29.5 %heads_forward.1 = (bf16[16,72,1024]{2,1,0:T(8,128)(2,1)S(1)}, f32[16,1,1024]{2,1,0:T(1,128)S(1)}) custom-call(bf16[3,16,72,1024]{3,2,1,0:T(8,128)(2,1)} %get-tuple-element.65.qkv_ref), custom_call_target="tpu_custom_call" | custom-call | flops 17179869184 | bytes 11796480 | tf_op jit(solution)/shard_map/heads_forward/pallas_call | solution.py:422
  223.5 12.6 %before_feed.1 = (bf16[1024,1280]{1,0:T(8,128)(2,1)}, bf16[1024,1280]{1,0:T(8,128)(2,1)}, f32[1024,1152]{1,0:T(8,128)}, bf16[3,16,1024]{2,1,0:T(8,128)(2,1)S(1)}) custom-call(bf16[1152,1024]{1,0:T(8,128)(2,1)S(1)} %bitcast.138, bf16[1024,1152]{1,0:T(8,128)(2,1)S(1)} %bitcast.137, bf16[1024,1152]{1,0:T(8,128)(2,1)} %bitcast.141, f32[8,1152]{1,0:T(8,128)S(1)} %copy-done.26, ...), custom_call_target="tpu_custom_call" | custom-call | flops 6039797760 | bytes 18874368 | tf_op jit(solution)/shard_map/before_feed/pallas_call | solution.py:680
  242.0 7.6 %assemble.1 = bf16[2,4,2,2,72,2304]{5,4,3,2,1,0:T(8,128)(2,1)S(1)} custom-call(s32[4]{0:T(128)S(1)} %pad_add_fusion.place_ref, bf16[2,4,72,2304]{3,2,1,0:T(8,128)(2,1)S(1)} %pad_maximum_fusion.near_ref, bf16[2,4,72,2304]{3,2,1,0:T(8,128)(2,1)} %collective-permute-done.8.far_ref, bf16[2,4,72,2304]{3,2,1,0:T(8,128)(2,1)} %collective-permute-done.9.next_near_ref, ...), custom_call_target="tpu_custom_call" | custom-call | bytes 21233664 | tf_op jit(solution)/shard_map/assemble/pallas_call | solution.py:560
  249.7 3.9 copy-done
  254.1 35.8 %feed.2 = (f32[1024,1280]{1,0:T(8,128)}, f32[1024,1280]{1,0:T(8,128)}, f32[16,2304]{1,0:T(8,128)}, f32[16,2304]{1,0:T(8,128)}) custom-call(bf16[1024,1280]{1,0:T(8,128)(2,1)} %get-tuple-element.71.second_ref, bf16[1024,1280]{1,0:T(8,128)(2,1)} %get-tuple-element.72.dfinal_ref, bf16[3,16,1024]{2,1,0:T(8,128)(2,1)} %copy-done.31, ...), custom_call_target="tpu_custom_call" | custom-call | flops 24159191040 | bytes 21037056 | tf_op jit(solution)/shard_map/feed/pallas_call | solution.py:796
  289.9 38.7 %feed.3 = (f32[1024,1280]{1,0:T(8,128)}, f32[1024,1280]{1,0:T(8,128)}, f32[16,2304]{1,0:T(8,128)}, f32[16,2304]{1,0:T(8,128)}) custom-call(bf16[1024,1280]{1,0:T(8,128)(2,1)} %get-tuple-element.71.second_ref, bf16[1024,1280]{1,0:T(8,128)(2,1)} %get-tuple-element.72.dfinal_ref, ...), custom_call_target="tpu_custom_call", output_to_operand_aliasing={{0}: (8, {}), {1}: (9, {})} | custom-call | flops 24159191040 | bytes 21037056 | tf_op jit(solution)/shard_map/feed/pallas_call | solution.py:796
  328.6 20.7 %after_feed.1 = (bf16[1024,1152]{1,0:T(8,128)(2,1)}, f32[1024,1152]{1,0:T(8,128)}, bf16[1152,1024]{1,0:T(8,128)(2,1)}, f32[8,1152]{1,0:T(8,128)}, f32[16,1152]{1...) custom-call(f32[1024,1280]{1,0:T(8,128)} %get-tuple-element.78.final_ref, ...), custom_call_target="tpu_custom_call" | custom-call | flops 7549747200 | bytes 37748736 | tf_op jit(solution)/shard_map/after_feed/pallas_call | solution.py:935
  349.3 47.2 %heads_back.1.dqkv_ref = bf16[3,16,72,1024]{3,2,1,0:T(8,128)(2,1)} custom-call(bf16[3,16,72,1024]{3,2,1,0:T(8,128)(2,1)} %get-tuple-element.65.qkv_ref, bf16[16,72,1024]{2,1,0:T(8,128)(2,1)} %bitcast.154, bf16[16,72,1024]{2,1,0:T(8,128)(2,1)} %copy-done.3, f32[16,1,1024]{2,1,0:T(1,128)} %copy-done.42), custom_call_target="tpu_custom_call" | custom-call | flops 42949672960 | bytes 18874368 | tf_op jit(solution)/shard_map/heads_back/pallas_call | solution.py:482
  396.5 23.2 %leave.1 = (bf16[1024,1152]{1,0:T(8,128)(2,1)}, f32[8,1152]{1,0:T(8,128)}, f32[16,3456]{1,0:T(8,128)}, f32[16,1152]{1,0:T(8,128)}) custom-call(bf16[3,16,72,1024]{3,2,1,0:T(8,128)(2,1)} %heads_back.1.dqkv_ref, bf16[1024,1152]{1,0:T(8,128)(2,1)} %bitcast.136, f32[1024,1152]{1,0:T(8,128)} %get-tuple-element.84.dresidual_ref, ...), custom_call_target="tpu_custom_call" | custom-call | flops 10569646080 | bytes 31850496 | tf_op jit(solution)/shard_map/leave/pallas_call | solution.py:1066
  419.8 2.5 dynamic-slice_bitcast_fusion
  427.9 5.5 %all-to-all-start.3 = ((bf16[16,16,1656]{2,1,0:T(8,128)(2,1)}), bf16[16,16,1656]{2,1,0:T(8,128)(2,1)S(1)}, u32[]{:S(2)}, u32[]{:S(2)}) async-start(bf16[16,16,1656]{2,1,0:T(8,128)(2,1)} %get-tuple-element.100), calls=%async_computation.3 | async-start | bytes 1703936 | tf_op jit(solution)/shard_map/all_to_all | solution.py:1404
  435.8 18.9 %collective-permute-done.15 = bf16[3456]{0:T(1024)(128)(2,1)S(1)} collective-permute-done((bf16[3456]{0:T(1024)(128)(2,1)S(1)}, bf16[3456]{0:T(1024)(128)(2,1)S(1)}, u32[]{:S(2)}, u32[]{:S(2)}) %collective-permute-start.15) | collective-permute-done | bytes 6944 | tf_op jit(solution)/shard_map/ppermute | solution.py:1381
  460.8 22.8 %collective-permute-done.13 = bf16[4,16,1656]{2,1,0:T(8,128)(2,1)S(1)} collective-permute-done((bf16[4,16,1656]{2,1,0:T(8,128)(2,1)S(1)}, bf16[4,16,1656]{2,1,0:T(8,128)(2,1)S(1)}, u32[]{:S(2)}, u32[]{:S(2)}) %collective-permute-start.13) | collective-permute-done | bytes 212000 | tf_op jit(solution)/shard_map/ppermute | solution.py:1381
  485.6 4.8 all-to-all-start.4
  491.7 2.9 fusion
  494.6 5.5 %convolution_add_fusion = f32[2,1152]{1,0:T(2,128)S(1)} fusion(bf16[1152,3456]{1,0:T(8,128)(2,1)} %all-gather.8.cloned.1.call-done, bf16[1,3456]{1,0:T(2,128)(2,1)S(1)} %stack.130, bf16[1,3456]{1,0:T(2,128)(2,1)S(1)} %stack.129, pred[2]{0:T(512)(128)(4,1)S(1)} %iota_compare_fusion.1, bf16[]{:T(256)} %bitcast.54, f32[1152]{0:T(1024)S(1)} %reduce.5), kind=kOutput, calls=%fused_computation.6 | convolution fusion | flops 15971328 | bytes 7990276 | tf_op jit(solution)/shard_map/so,io->si/dot_general | solution.py:1377
  501.9 2.5 maximum_convert_fusion
  (246 shorter events, 85.7 us)
Async XLA Ops:
  7.2 167.8 %all-gather.4.cloned.1.call-start = ((), (), s32[]{:S(2)}) async-start(), calls=%async_computation.5 | async-start | bytes 11280384 | tf_op jit(solution)/shard_map/all_gather | solution.py:1448
  8.3 10.8 %collective-permute-start.2 = (bf16[72,2304]{1,0:T(8,128)(2,1)S(1)}, bf16[72,2304]{1,0:T(8,128)(2,1)S(1)}, u32[]{:S(2)}, u32[]{:S(2)}) collective-permute-start(bf16[72,2304]{1,0:T(8,128)(2,1)S(1)} %pad_maximum_fusion.7), channel_id=1, source_target_pairs={{0,1},{1,0},{2,3},{3,2},{4,5},{5,4},{6,7},{7,6},{8,9},{9,8},{10,11... | collective-permute-start | bytes 995336 | tf_op jit(solution)/shard_map/ppermute | solution.py:1381
  22.0 231.5 %all-gather.6.cloned.1.call-start = ((), (), s32[]{:S(2)}) async-start(), calls=%async_computation.6 | async-start | bytes 11280384 | tf_op jit(solution)/shard_map/all_gather | solution.py:1448
  24.5 9.1 %collective-permute-start.11 = (bf16[72,2304]{1,0:T(8,128)(2,1)S(1)}, bf16[72,2304]{1,0:T(8,128)(2,1)S(1)}, u32[]{:S(2)}, u32[]{:S(2)}) collective-permute-start(bf16[72,2304]{1,0:T(8,128)(2,1)S(1)} %concatenate.26), channel_id=1, source_target_pairs={{0,1},{1,0},{2,3},{3,2},{4,5},{5,4},{6,7},{7,6},{8,9},{9,8},{10,11... | collective-permute-start | bytes 995336 | tf_op jit(solution)/shard_map/ppermute | solution.py:1381
  37.3 54.6 %collective-permute-start.4 = (bf16[72,2304]{1,0:T(8,128)(2,1)S(1)}, bf16[72,2304]{1,0:T(8,128)(2,1)}, u32[]{:S(2)}, u32[]{:S(2)}) collective-permute-start(bf16[72,2304]{1,0:T(8,128)(2,1)S(1)} %concatenate.25), channel_id=1, source_target_pairs={{0,8},{1,9},{2,10},{3,11},{4,12},{5,13},{6,14},{7,15},{8,16},{9,17... | collective-permute-start | bytes 995336 | tf_op jit(solution)/shard_map/ppermute | solution.py:1124
  38.9 54.7 %collective-permute-start.5 = (bf16[72,2304]{1,0:T(8,128)(2,1)S(1)}, bf16[72,2304]{1,0:T(8,128)(2,1)}, u32[]{:S(2)}, u32[]{:S(2)}) collective-permute-start(bf16[72,2304]{1,0:T(8,128)(2,1)S(1)} %concatenate.25), channel_id=1, source_target_pairs={{0,16},{1,17},{2,18},{3,19},{4,20},{5,21},{6,22},{7,23},{8,24},{9,... | collective-permute-start | bytes 995336 | tf_op jit(solution)/shard_map/ppermute | solution.py:1124
  41.5 52.1 %collective-permute-start.6 = (bf16[72,2304]{1,0:T(8,128)(2,1)S(1)}, bf16[72,2304]{1,0:T(8,128)(2,1)}, u32[]{:S(2)}, u32[]{:S(2)}) collective-permute-start(bf16[72,2304]{1,0:T(8,128)(2,1)S(1)} %concatenate.25), channel_id=1, source_target_pairs={{0,24},{1,25},{2,26},{3,27},{4,28},{5,29},{6,30},{7,31},{8,0},{9,1... | collective-permute-start | bytes 995336 | tf_op jit(solution)/shard_map/ppermute | solution.py:1124
  43.7 54.3 %collective-permute-start.1 = (bf16[4,16,1656]{2,1,0:T(8,128)(2,1)}, bf16[4,16,1656]{2,1,0:T(8,128)(2,1)}, u32[]{:S(2)}, u32[]{:S(2)}) collective-permute-start(bf16[4,16,1656]{2,1,0:T(8,128)(2,1)} %pad_maximum_fusion.8), channel_id=1, source_target_pairs={{0,1},{1,0},{2,3},{3,2},{4,5},{5,4},{6,7},{7,6},{8,9},{9,8},{10,11... | collective-permute-start | bytes 635912 | tf_op jit(solution)/shard_map/ppermute | solution.py:1381
  46.1 40.6 %all-to-all-start = ((bf16[16,2,80]{2,1,0:T(2,128)(2,1)}), bf16[16,2,80]{2,1,0:T(2,128)(2,1)S(1)}, u32[]{:S(2)}, u32[]{:S(2)}) async-start(bf16[16,2,80]{2,1,0:T(2,128)(2,1)} %copy.50), calls=%async_computation | async-start | bytes 16384 | tf_op jit(solution)/shard_map/all_to_all | solution.py:1404
  50.8 75.8 %collective-permute-start = (bf16[512,1152]{1,0:T(8,128)(2,1)}, bf16[512,1152]{1,0:T(8,128)(2,1)}, u32[]{:S(2)}, u32[]{:S(2)}) collective-permute-start(bf16[512,1152]{1,0:T(8,128)(2,1)} %dynamic-slice_bitcast_fusion.3), channel_id=1, source_target_pairs={{0,1},{1,0},{2,3},{3,2},{4,5},{5,4},{6,7},{7,6},{8,9},{9,8},{10,11... | collective-permute-start | bytes 3538952 | tf_op jit(solution)/shard_map/ppermute | solution.py:1381
  51.4 35.3 %copy-start.49 = (bf16[72,3456]{1,0:T(8,128)(2,1)S(1)}, bf16[72,3456]{1,0:T(8,128)(2,1)}, u32[]{:S(2)}) copy-start(bf16[72,3456]{1,0:T(8,128)(2,1)} %param.23) | copy-start | bytes 1492996
  88.1 28.6 %all-to-all-start.1 = ((f32[32,1,3456]{2,1,0:T(1,128)}), f32[32,1,3456]{2,1,0:T(1,128)}, u32[]{:S(2)}, u32[]{:S(2)}) async-start(f32[32,1,3456]{2,1,0:T(1,128)} %copy.51), calls=%async_computation.1 | async-start | bytes 884736 | tf_op jit(solution)/shard_map/all_to_all | solution.py:1400
  91.9 52.7 %collective-permute-start.3 = (bf16[512,1152]{1,0:T(8,128)(2,1)}, bf16[512,1152]{1,0:T(8,128)(2,1)}, u32[]{:S(2)}, u32[]{:S(2)}) collective-permute-start(bf16[512,1152]{1,0:T(8,128)(2,1)} %dynamic-slice_bitcast_fusion.2), channel_id=1, source_target_pairs={{0,1},{1,0},{2,3},{3,2},{4,5},{5,4},{6,7},{7,6},{8,9},{9,8},{10,11... | collective-permute-start | bytes 3538952 | tf_op jit(solution)/shard_map/ppermute | solution.py:1381
  96.5 43.1 %collective-permute-start.7 = (bf16[4,72,2304]{2,1,0:T(8,128)(2,1)}, bf16[4,72,2304]{2,1,0:T(8,128)(2,1)}, u32[]{:S(2)}, u32[]{:S(2)}) collective-permute-start(bf16[4,72,2304]{2,1,0:T(8,128)(2,1)} %get-tuple-element.125), channel_id=1, source_target_pairs={{0,4},{1,5},{2,3},{3,2},{4,0},{5,1},{6,7},{7,6},{8,12},{9,13},{10,... | collective-permute-start | bytes 3981320 | tf_op jit(solution)/shard_map/ppermute | solution.py:1129
  116.7 32.4 %all-to-all-start.2 = ((bf16[16,16,1656]{2,1,0:T(8,128)(2,1)}), bf16[16,16,1656]{2,1,0:T(8,128)(2,1)S(1)}, u32[]{:S(2)}, u32[]{:S(2)}) async-start(bf16[16,16,1656]{2,1,0:T(8,128)(2,1)} %copy.63), calls=%async_computation.2 | async-start | bytes 1703936 | tf_op jit(solution)/shard_map/all_to_all | solution.py:1404
  120.5 374.1 %all-gather.8.cloned.1.call-start = ((), (), s32[]{:S(2)}) async-start(), calls=%async_computation.7 | async-start | bytes 8460288 | tf_op jit(solution)/shard_map/all_gather | solution.py:1590
  141.2 32.2 %collective-permute-start.8 = (bf16[2,4,72,2304]{3,2,1,0:T(8,128)(2,1)S(1)}, bf16[2,4,72,2304]{3,2,1,0:T(8,128)(2,1)}, u32[]{:S(2)}, u32[]{:S(2)}) collective-permute-start(bf16[2,4,72,2304]{3,2,1,0:T(8,128)(2,1)S(1)} %pad_maximum_fusion.near_ref), channel_id=1, source_target_pairs={{0,1},{1,0},{2,6},{3,7},{4,5},{5,4},{6,2},{7,3},{8,9},{9,8},{10,14... | collective-permute-start | bytes 7962632 | tf_op jit(solution)/shard_map/ppermute | solution.py:1137
  148.8 93.3 %collective-permute-start.9 = (bf16[2,4,72,2304]{3,2,1,0:T(8,128)(2,1)S(1)}, bf16[2,4,72,2304]{3,2,1,0:T(8,128)(2,1)}, u32[]{:S(2)}, u32[]{:S(2)}) collective-permute-start(bf16[2,4,72,2304]{3,2,1,0:T(8,128)(2,1)S(1)} %pad_maximum_fusion.near_ref), channel_id=1, source_target_pairs={{0,2},{1,3},{2,0},{3,1},{4,6},{5,7},{6,4},{7,5},{8,10},{9,11},{10,... | collective-permute-start | bytes 7962632 | tf_op jit(solution)/shard_map/ppermute | solution.py:1145
  173.4 68.7 %collective-permute-start.10 = (bf16[2,4,72,2304]{3,2,1,0:T(8,128)(2,1)}, bf16[2,4,72,2304]{3,2,1,0:T(8,128)(2,1)}, u32[]{:S(2)}, u32[]{:S(2)}) collective-permute-start(bf16[2,4,72,2304]{3,2,1,0:T(8,128)(2,1)} %collective-permute-done.8.far_ref), channel_id=1, source_target_pairs={{0,2},{1,3},{2,0},{3,1},{4,6},{5,7},{6,4},{7,5},{8,10},{9,11},{10,... | collective-permute-start | bytes 7962632 | tf_op jit(solution)/shard_map/ppermute | solution.py:1145
  193.8 29.6 %copy-start.16 = (bf16[128,1152]{1,0:T(8,128)(2,1)S(1)}, bf16[128,1152]{1,0:T(8,128)(2,1)}, u32[]{:S(2)}) copy-start(bf16[128,1152]{1,0:T(8,128)(2,1)} %copy-done.15) | copy-start | bytes 884740
  193.8 29.6 %copy-start.18 = (bf16[128,1152]{1,0:T(8,128)(2,1)S(1)}, bf16[128,1152]{1,0:T(8,128)(2,1)}, u32[]{:S(2)}) copy-start(bf16[128,1152]{1,0:T(8,128)(2,1)} %copy-done.17) | copy-start | bytes 884740
  193.8 29.6 %copy-start.20 = (bf16[128,1152]{1,0:T(8,128)(2,1)S(1)}, bf16[128,1152]{1,0:T(8,128)(2,1)}, u32[]{:S(2)}) copy-start(bf16[128,1152]{1,0:T(8,128)(2,1)} %copy-done.19) | copy-start | bytes 884740
  193.9 29.6 %copy-start.22 = (bf16[128,1152]{1,0:T(8,128)(2,1)S(1)}, bf16[128,1152]{1,0:T(8,128)(2,1)}, u32[]{:S(2)}) copy-start(bf16[128,1152]{1,0:T(8,128)(2,1)} %copy-done.21) | copy-start | bytes 884740
  193.9 29.6 %copy-start.26 = (f32[8,1152]{1,0:T(8,128)S(1)}, f32[8,1152]{1,0:T(8,128)}, u32[]{:S(2)}) copy-start(f32[8,1152]{1,0:T(8,128)} %pad.4.mod_ref) | copy-start | bytes 110596
  193.9 29.6 %copy-start.37 = (f32[1,1152]{1,0:T(1,128)S(1)}, f32[1,1152]{1,0:T(1,128)}, u32[]{:S(2)}) copy-start(f32[1,1152]{1,0:T(1,128)} %broadcast_in_dim.45.bias_ref) | copy-start | bytes 13828
  425.5 29.3 %collective-permute-start.12 = (bf16[512,1152]{1,0:T(8,128)(2,1)}, bf16[512,1152]{1,0:T(8,128)(2,1)}, u32[]{:S(2)}, u32[]{:S(2)}) collective-permute-start(bf16[512,1152]{1,0:T(8,128)(2,1)} %dynamic-slice_bitcast_fusion.1), channel_id=1, source_target_pairs={{0,1},{1,0},{2,3},{3,2},{4,5},{5,4},{6,7},{7,6},{8,9},{9,8},{10,11... | collective-permute-start | bytes 3538952 | tf_op jit(solution)/shard_map/ppermute | solution.py:1381
  427.9 28.7 %all-to-all-start.3 = ((bf16[16,16,1656]{2,1,0:T(8,128)(2,1)}), bf16[16,16,1656]{2,1,0:T(8,128)(2,1)S(1)}, u32[]{:S(2)}, u32[]{:S(2)}) async-start(bf16[16,16,1656]{2,1,0:T(8,128)(2,1)} %get-tuple-element.100), calls=%async_computation.3 | async-start | bytes 1703936 | tf_op jit(solution)/shard_map/all_to_all | solution.py:1404
  433.6 21.1 %collective-permute-start.15 = (bf16[3456]{0:T(1024)(128)(2,1)S(1)}, bf16[3456]{0:T(1024)(128)(2,1)S(1)}, u32[]{:S(2)}, u32[]{:S(2)}) collective-permute-start(bf16[3456]{0:T(1024)(128)(2,1)S(1)} %get-tuple-element.113), channel_id=1, source_target_pairs={{0,1},{1,0},{2,3},{3,2},{4,5},{5,4},{6,7},{7,6},{8,9},{9,8},{10,11... | collective-permute-start | bytes 20744 | tf_op jit(solution)/shard_map/ppermute | solution.py:1381
  435.7 56.0 %collective-permute-start.14 = (bf16[512,1152]{1,0:T(8,128)(2,1)}, bf16[512,1152]{1,0:T(8,128)(2,1)}, u32[]{:S(2)}, u32[]{:S(2)}) collective-permute-start(bf16[512,1152]{1,0:T(8,128)(2,1)} %dynamic-slice_bitcast_fusion), channel_id=1, source_target_pairs={{0,1},{1,0},{2,3},{3,2},{4,5},{5,4},{6,7},{7,6},{8,9},{9,8},{10,11... | collective-permute-start | bytes 3538952 | tf_op jit(solution)/shard_map/ppermute | solution.py:1381
  457.5 26.2 %collective-permute-start.13 = (bf16[4,16,1656]{2,1,0:T(8,128)(2,1)S(1)}, bf16[4,16,1656]{2,1,0:T(8,128)(2,1)S(1)}, u32[]{:S(2)}, u32[]{:S(2)}) collective-permute-start(bf16[4,16,1656]{2,1,0:T(8,128)(2,1)S(1)} %get-tuple-element.102), channel_id=1, source_target_pairs={{0,1},{1,0},{2,3},{3,2},{4,5},{5,4},{6,7},{7,6},{8,9},{9,8},{10,11... | collective-permute-start | bytes 635912 | tf_op jit(solution)/shard_map/ppermute | solution.py:1381
  485.6 18.8 %all-to-all-start.4 = ((f32[32,1,128]{2,1,0:T(1,128)}), f32[32,1,128]{2,1,0:T(1,128)S(1)}, u32[]{:S(2)}, u32[]{:S(2)}) async-start(f32[32,1,128]{2,1,0:T(1,128)} %broadcast_in_dim.52), calls=%async_computation.4 | async-start | bytes 32768 | tf_op jit(solution)/shard_map/all_to_all | solution.py:1400
  500.1 6.4 %collective-permute-start.16 = (f32[2,1152]{1,0:T(2,128)S(1)}, f32[2,1152]{1,0:T(2,128)S(1)}, u32[]{:S(2)}, u32[]{:S(2)}) collective-permute-start(f32[2,1152]{1,0:T(2,128)S(1)} %convolution_add_fusion), channel_id=1, source_target_pairs={{0,1},{1,0},{2,3},{3,2},{4,5},{5,4},{6,7},{7,6},{8,9},{9,8},{10,11... | collective-permute-start | bytes 27656 | tf_op jit(solution)/shard_map/ppermute | solution.py:1381
  (55 other events, 338.0 us)
Sparse Core Ops, SparseCore 0:
  22.1 137.7 all-gather.3
  162.2 87.6 all-gather.5
  252.1 70.3 all-gather.7
